TPU v7x, 256 devices: a whole 4x4x8 slice. The times are simulated.
256 devices in a mesh: gz: 4 (over y), grid: 64 (over z, x, core).
Axes of the slice: x: 4, y: 4, z: 8, core: 2. Of those that a mesh axis runs over, the one named last changes fastest.
Arguments:
- leaf_rhs: bfloat16 [4, 1024, 128, 256], P('gz', 'grid'), may hold values from -6 to 6
- leaf_inverse: bfloat16 [4, 1024, 128, 128], P('gz', 'grid'), may hold values from -0.5 to 0.5
- leaf_update: bfloat16 [4, 1024, 128, 128], P('gz', 'grid'), may hold values from -0.125 to 0.125
- leaf_target: int32 [4, 1024, 1], P('gz', 'grid'), may hold values from 0 to 63; in each aligned block of 16 rows (0 to 15, 16 to 31, ..., all dimensions but the last counted through in order) at most 2 rows name the same one
- anc_rhs: float32 [64, 128, 256], P('grid'), may hold values from -6 to 6
- anc_inverse: float32 [64, 128, 128], P('grid'), may hold values from -0.4 to 1.8, as said below
- anc_coupling: float32 [64, 128, 128], P('grid'), may hold values from -256 to 256, as said below
Outputs:
- leaf_solution: bfloat16 [4, 1024, 128, 256], P('gz', 'grid')
- anc_solution: float32 [64, 128, 256], P('grid')
Inputs may be any that keep to these rules, and one draw needn't show every extreme that they name: `leaf_target`: among the 16 leaves of one device at most 2 update the same ancestor. `anc_inverse`: dense blocks. `anc_coupling`: dense blocks.
All inputs are finite; a program needn't handle non-finite values.
Results may differ from a plain program's by a relative error of at most 0.0085.
Values may be sent and summed in bfloat16 or wider, within the bound.
No kernel may reach another device: no remote copies, remote signals or barrier semaphores. Data moves between devices by JAX's collectives and lax.ppermute only.
A program may use at most 128 MiB of HBM per device.

v0:
```python
import jax
import jax.numpy as jnp
from jax import lax
from jax.sharding import PartitionSpec as P


def chain_forward(previous, blocks):
    precise = lax.Precision.HIGHEST
    inverse_block, coupling_block, reduced_block = blocks
    current = jnp.dot(
        inverse_block,
        reduced_block - jnp.dot(coupling_block, previous, precision=precise),
        precision=precise,
    )
    return (current, current)


def chain_backward(following, blocks):
    precise = lax.Precision.HIGHEST
    inverse_block, coupling_block, solved_block = blocks
    current = jnp.dot(
        inverse_block.T,
        solved_block - jnp.dot(coupling_block.T, following, precision=precise),
        precision=precise,
    )
    return (current, current)


def local(leaf_rhs, leaf_inverse, leaf_update, leaf_target, anc_rhs, anc_inverse, anc_coupling):
    rhs_blocks = leaf_rhs[0]
    inverse_blocks = leaf_inverse[0]
    update_blocks = leaf_update[0]
    targets = leaf_target[0, :, 0]
    leaf_count, block_width, rhs_count = rhs_blocks.shape
    chain_length = lax.axis_size("grid")
    forward = jnp.einsum(
        "kij,kjr->kir", inverse_blocks, rhs_blocks, preferred_element_type=jnp.float32
    ).astype(jnp.bfloat16)
    update = jnp.einsum(
        "kij,kjr->kir", update_blocks, forward, preferred_element_type=jnp.float32
    ).astype(jnp.bfloat16)
    flat_update = update.reshape(leaf_count, block_width * rhs_count)
    owners = lax.broadcasted_iota(jnp.int32, (chain_length, leaf_count), 0)
    selector = (owners == targets[None, :]).astype(jnp.bfloat16)
    rounded_term = jnp.dot(selector, flat_update, preferred_element_type=jnp.float32).astype(
        jnp.bfloat16
    )
    own_total = lax.psum_scatter(
        lax.optimization_barrier(rounded_term).astype(jnp.float32),
        "grid",
        scatter_dimension=0,
        tiled=True,
    )[0]
    layer_total = lax.psum(own_total.reshape(block_width, rhs_count), "gz")
    reduced = anc_rhs[0] - layer_total
    all_reduced, all_inverse, all_coupling = (
        lax.all_gather(reduced[None], "grid", axis=0, tiled=True),
        lax.all_gather(anc_inverse, "grid", axis=0, tiled=True),
        lax.all_gather(anc_coupling, "grid", axis=0, tiled=True),
    )
    zero_block = jnp.zeros((block_width, rhs_count), jnp.float32)
    final_forward, solved = lax.scan(
        chain_forward, zero_block, (all_inverse, all_coupling, all_reduced)
    )
    following_coupling = jnp.concatenate(
        [all_coupling[1:], jnp.zeros_like(all_coupling[:1])], axis=0
    )
    final_backward, all_solution = lax.scan(
        chain_backward, zero_block, (all_inverse, following_coupling, solved), reverse=True
    )
    anc_own = lax.dynamic_index_in_dim(all_solution, lax.axis_index("grid"), 0, keepdims=False)
    rounded_all = all_solution.astype(jnp.bfloat16).reshape(chain_length, block_width * rhs_count)
    chosen = jnp.dot(selector.T, rounded_all, preferred_element_type=jnp.float32)
    chosen_blocks = chosen.reshape(leaf_count, block_width, rhs_count).astype(jnp.bfloat16)
    correction = jnp.einsum(
        "kji,kjr->kir", update_blocks, chosen_blocks, preferred_element_type=jnp.float32
    )
    residue = (forward.astype(jnp.float32) - correction).astype(jnp.bfloat16)
    solution = jnp.einsum(
        "kji,kjr->kir", inverse_blocks, residue, preferred_element_type=jnp.float32
    ).astype(jnp.bfloat16)
    return (solution[None], anc_own[None])


def solution(mesh):
    return jax.shard_map(
        local,
        mesh=mesh,
        in_specs=(
            P("gz", "grid", None, None),
            P("gz", "grid", None, None),
            P("gz", "grid", None, None),
            P("gz", "grid", None),
            P("grid", None, None),
            P("grid", None, None),
            P("grid", None, None),
        ),
        out_specs=(P("gz", "grid", None, None), P("grid", None, None)),
        check_vma=False,
    )
```

profile of v0, /device:TPU:1, one launch (start us, length us, event | category | flops | bytes accessed | tf_op | source)
XLA Modules:
  0.0 978.3 jit_solution(15383518840547594341)
XLA Ops:
  13.1 3.3 convolution_convert_fusion
  16.5 296.4 %all-reduce.6 = f32[64,32768]{1,0:T(8,128)} all-reduce(bf16[64,32768]{1,0:T(8,128)(2,1)} %convolution_convert_fusion), channel_id=3, replica_groups=mesh['gz'=4,'grid'=64] {'grid'}, use_global_device_ids=true, to_apply=%region_0.0.clone | all-reduce | flops 2097152 | bytes 12582912
  313.5 2.2 dynamic-slice_reduce_fusion
  317.7 43.3 %all-reduce.5.cloned.1.call-done = f32[128,256]{1,0:T(8,128)} async-done(((f32[128,256]{1,0:T(8,128)}), f32[128,256]{1,0:T(8,128)}) %all-reduce.5.cloned.1.call-update) | async-done | bytes 131088 | tf_op jit(solution)/shard_map/psum | solution.py:54
  362.5 36.5 %all-gather.7.cloned.1.call-done = f32[64,128,128]{2,1,0:T(8,128)} async-done(((f32[1,128,128]{2,1,0:T(8,128)}), f32[64,128,128]{2,1,0:T(8,128)}) %all-gather.7.cloned.1.call-update) | async-done | bytes 4194320 | tf_op jit(solution)/shard_map/all_gather | solution.py:59
  399.1 2.2 slice-done
  401.2 2.3 concatenate.3
  403.5 74.6 %all-gather.5.cloned.1.call-done = f32[64,128,128]{2,1,0:T(8,128)} async-done(((f32[1,128,128]{2,1,0:T(8,128)}), f32[64,128,128]{2,1,0:T(8,128)}) %all-gather.5.cloned.1.call-update) | async-done | bytes 4194320 | tf_op jit(solution)/shard_map/all_gather | solution.py:58
  478.1 84.5 %all-gather.9.cloned.1.call-done = f32[8192,256]{1,0:T(8,128)} async-done(((f32[128,256]{1,0:T(8,128)}), f32[8192,256]{1,0:T(8,128)}) %all-gather.9.cloned.1.call-update) | async-done | bytes 8388624 | tf_op jit(solution)/shard_map/all_gather | solution.py:57
  562.7 4.3 broadcast.5.clone
  566.9 190.4 %while.28 = (s32[]{:T(128)}, f32[128,256]{1,0:T(8,128)S(1)}, f32[64,128,256]{2,1,0:T(8,128)}, f32[64,128,128]{2,1,0:T(8,128)}, f32[64,128,256]{2,1,0:T(8,128)}, /*index=5*/f32[64,128,128]{2,1,0:T(8,128)}, s32[]{:T(128)}) while((s32[]{:T(128)}, f32[128,256]{1,0:T(8,128)S(1)}, f32[64,128,256]{2,1,0:T(8,128)}, f32[64,128,128]{2,1,0:T(8,128)}, ...), condition=%wide.region_3.4_spmd, body=%wide.region_2.3_spmd.sunk | while | flops 100696064 | bytes 919629 | solution.py:62
  757.3 4.2 broadcast.5
  761.6 196.4 %while.29 = (s32[]{:T(128)}, f32[128,256]{1,0:T(8,128)S(1)}, f32[64,128,256]{2,1,0:T(8,128)}, f32[64,128,128]{2,1,0:T(8,128)}, f32[64,128,256]{2,1,0:T(8,128)}, ...) while((s32[]{:T(128)}, f32[128,256]{1,0:T(8,128)S(1)}, f32[64,128,256]{2,1,0:T(8,128)}, ...), condition=%wide.region_5.6_spmd, body=%wide.region_4.5_spmd.sunk | while | flops 100696064 | bytes 919649 | solution.py:68
  765.9 1.8 bitcast_dynamic-update-slice_fusion.5
  769.0 1.8 bitcast_dynamic-update-slice_fusion.5
  827.3 1.8 bitcast_dynamic-update-slice_fusion.5
  830.4 1.8 bitcast_dynamic-update-slice_fusion.5
  833.5 1.8 bitcast_dynamic-update-slice_fusion.5
  867.3 1.8 bitcast_dynamic-update-slice_fusion.5
  913.3 1.8 bitcast_dynamic-update-slice_fusion.5
  916.4 1.8 bitcast_dynamic-update-slice_fusion.5
  958.1 4.0 convert_element_type.40
  963.6 3.3 fusion.18
  966.9 2.4 fusion.21
  (277 shorter events, 383.2 us)
Async XLA Ops:
  8.0 1.2 copy-start
  8.0 5.1 copy-start.3
  8.0 352.9 %all-reduce.5.cloned.1.call-start = ((), (), s32[]{:S(2)}) async-start(), calls=%async_computation.1 | async-start | bytes 262144 | tf_op jit(solution)/shard_map/psum | solution.py:54
  16.5 296.4 %copy-start.4 = (u32[256]{0:T(256)S(1)}, u32[256]{0:T(256)}, u32[]{:S(2)}) copy-start(u32[256]{0:T(256)} %constant.75) | copy-start | bytes 3076
  16.5 344.5 %copy-start.2 = (f32[1,128,256]{2,1,0:T(8,128)S(1)}, f32[1,128,256]{2,1,0:T(8,128)}, u32[]{:S(2)}) copy-start(f32[1,128,256]{2,1,0:T(8,128)} %param.15) | copy-start | bytes 393220
  316.4 82.6 %all-gather.7.cloned.1.call-start = ((), (), s32[]{:S(2)}) async-start(), calls=%async_computation.2 | async-start | bytes 4259840 | tf_op jit(solution)/shard_map/all_gather | solution.py:59
  317.0 161.1 %all-gather.5.cloned.1.call-start = ((), (), s32[]{:S(2)}) async-start(), calls=%async_computation | async-start | bytes 4259840 | tf_op jit(solution)/shard_map/all_gather | solution.py:58
  317.6 245.1 %all-gather.9.cloned.1.call-start = ((), (), s32[]{:S(2)}) async-start(), calls=%async_computation.3 | async-start | bytes 8519680 | tf_op jit(solution)/shard_map/all_gather | solution.py:57
  399.1 2.2 slice-start
  963.6 7.1 copy-start.1
Sparse Core Ops, SparseCore 0:
  316.6 44.3 all-reduce.4
Sparse Core Ops, SparseCore 1:
  319.7 79.3 all-gather.6
  401.7 76.4 all-gather.4
  481.7 80.9 all-gather.8
where the time goes:
time: 987 us; the launch traced here: 978 us
  matrix products  398 us (40%)
  blocking collectives  296 us (30%)
  waiting for transfers between devices  240 us (24%)
  local copies, waits for them, and re-layouts  21.5 us (2%)
  between operations  15.7 us (2%)
    unnamed x1, blocking collectives  296 us
    dot_general x64, matrix products, chain_backward(): jnp.dot(inverse_block.T, solved_block - jnp.dot(coupling_block.T, followi...  116 us
    dot_general x64, matrix products, chain_forward(): jnp.dot(inverse_block, reduced_block - jnp.dot(coupling_block, previous,...  113 us
    all_gather x1, waiting for transfers between devices, local(): lax.all_gather(reduced[None], 'grid', axis=0, tiled=True)  84.5 us
    dot_general x64, matrix products, chain_backward(): jnp.dot(coupling_block.T, following, precision=precise)  80 us
    dot_general x64, matrix products, chain_forward(): jnp.dot(coupling_block, previous, precision=precise)  77 us
    all_gather x1, waiting for transfers between devices, local(): lax.all_gather(anc_inverse, 'grid', axis=0, tiled=True)  74.6 us
    psum x1, waiting for transfers between devices, local(): layer_total = lax.psum(own_total.reshape(block_width, rhs_count), 'gz')  43.3 us
  transfers between devices with their start and end apart: 4, of which 4 were waited for; matrix products, arithmetic and copies ran while one was open for 0% of the time, Pallas kernels for 0%

commit v1 on v0

v1 whole, which is shorter than its diff:
```python
import functools

import jax
import jax.numpy as jnp
from jax import lax
from jax.experimental import pallas as pl
from jax.experimental.pallas import tpu as pltpu
from jax.sharding import Mesh
from jax.sharding import PartitionSpec as P

F32 = jnp.float32
BF16 = jnp.bfloat16
PLANE_AXES = ("y", "x", "c")
STEP_SCALE = 2.0**-8
CHAIN_BLOCK = 4


def dot_nn(a, b):
    return lax.dot_general(
        a, b, (((1,), (0,)), ((), ())), precision=lax.Precision.HIGHEST, preferred_element_type=F32
    )


def dot_nt(a, b):
    return lax.dot_general(
        a, b, (((1,), (1,)), ((), ())), precision=lax.Precision.HIGHEST, preferred_element_type=F32
    )


def leaf_forward_kernel(peers, y_ref, rhs_ref, inv_ref, upd_ref, tgt_ref, anc_ref, fwd_ref, send_ref):
    step = pl.program_id(0)
    last = pl.num_programs(0) - 1
    rhs_count, width = fwd_ref.shape[1:]
    cols = rhs_count // peers

    @pl.when(step < last)
    def _():
        parts = []
        for k in range(2):
            forward = lax.dot_general(
                rhs_ref[k], inv_ref[k], (((0,), (1,)), ((), ())), preferred_element_type=F32
            ).astype(BF16)
            fwd_ref[k] = forward
            update = lax.dot_general(
                forward, upd_ref[k], (((1,), (1,)), ((), ())), preferred_element_type=F32
            )
            parts.append(update.reshape(peers, cols, width))
        send_ref[...] = jnp.concatenate(parts, axis=1).astype(BF16)

    @pl.when(step == last)
    def _():
        rows = anc_ref[...].T
        high = rows.astype(BF16).astype(F32)
        low = rows - high
        layer = y_ref[0]
        mine = jnp.where(layer == 0, high, jnp.where(layer == 1, low, jnp.zeros_like(low)))
        leaf = lax.broadcasted_iota(jnp.int32, (peers, cols, width), 2) // cols
        names = jnp.zeros((peers, cols, width), F32)
        for k in range(tgt_ref.shape[0]):
            names = jnp.where(leaf == k, tgt_ref[k].astype(F32), names)
        send_ref[...] = jnp.concatenate([mine.reshape(peers, cols, width), names], axis=1).astype(BF16)


def transfer_kernel(c_ref, blocks_ref, after_ref, m_ref, out_ref):
    width = m_ref.shape[1]
    count = m_ref.shape[0]
    ms = []
    for j in range(count):
        inverse = blocks_ref[2 * width * j : 2 * width * j + width, :]
        coupling = blocks_ref[2 * width * j + width : 2 * width * (j + 1), :]
        m = dot_nn(inverse, coupling)
        m_ref[j] = m
        ms.append(m * STEP_SCALE)
    core = c_ref[0]
    blocks = count // CHAIN_BLOCK
    chains = [[-ms[b * CHAIN_BLOCK]] for b in range(blocks)]
    for k in range(1, CHAIN_BLOCK):
        for b in range(blocks):
            chains[b].append(-dot_nn(ms[b * CHAIN_BLOCK + k], chains[b][-1]))
    back = [jnp.zeros((width, width), F32) for _ in range(blocks)]
    for k in reversed(range(CHAIN_BLOCK)):
        shrink = STEP_SCALE ** (2 * (CHAIN_BLOCK - 1 - k))
        for b in range(blocks):
            back[b] = dot_nn(ms[b * CHAIN_BLOCK + k].T, chains[b][k] * shrink - back[b])
    for b in range(blocks):
        carry = chains[b][-1] * (STEP_SCALE**-CHAIN_BLOCK)
        out_ref[width * b : width * (b + 1), :] = jnp.where(core == 0, carry, back[b])


def densify_kernel(plane_size, v_ref, after_ref, d_ref, anc_ref, code_ref, acc_ref):
    sources, rows, width = v_ref.shape
    body = rows - 16
    cols = 8
    lane = lax.broadcasted_iota(jnp.int32, (sources, body), 1)
    tail = v_ref[:, body:rows, :].astype(F32)
    codes = tail[:, cols, :].astype(jnp.int32) * cols + lane % cols
    code_ref[...] = codes.astype(F32).T
    row = lax.broadcasted_iota(jnp.int32, (acc_ref.shape[0], body), 0)
    for s in range(0, sources, 2):
        pick = jnp.concatenate(
            [(row == codes[s + i : s + i + 1, :]).astype(F32).astype(BF16) for i in range(2)], axis=1
        )
        values = v_ref[s : s + 2, 0:body, :].reshape(2 * body, width)
        term = jnp.dot(pick, values, preferred_element_type=F32)
        if s == 0:
            acc_ref[...] = term
        else:
            acc_ref[...] += term
    d_ref[...] = acc_ref[...].astype(BF16).reshape(d_ref.shape)
    per = sources // plane_size
    for j in range(plane_size):
        total = tail[j, 0:cols, :]
        for y in range(1, per):
            total = total + tail[y * plane_size + j, 0:cols, :]
        anc_ref[cols * j : cols * (j + 1), :] = total


def block_solve_kernel(e_ref, anc_ref, blocks_ref, m_ref, b_ref, out_ref):
    count, width = m_ref.shape[0:2]
    cols = anc_ref.shape[0] // count
    total = e_ref[0].astype(F32)
    for z in range(1, e_ref.shape[0]):
        total = total + e_ref[z].astype(F32)
    reduced = anc_ref[...] - total
    bs = []
    for j in range(count):
        inverse = blocks_ref[2 * width * j : 2 * width * j + width, :]
        b = dot_nt(reduced[cols * j : cols * (j + 1)], inverse)
        b_ref[cols * j : cols * (j + 1), :] = b
        bs.append(b)
    blocks = count // CHAIN_BLOCK
    solved = [[bs[b * CHAIN_BLOCK]] for b in range(blocks)]
    for k in range(1, CHAIN_BLOCK):
        for b in range(blocks):
            j = b * CHAIN_BLOCK + k
            solved[b].append(bs[j] - dot_nt(solved[b][-1], m_ref[j]))
    back = [jnp.zeros((cols, width), F32) for _ in range(blocks)]
    for k in reversed(range(CHAIN_BLOCK)):
        for b in range(blocks):
            back[b] = dot_nn(solved[b][k] - back[b], m_ref[b * CHAIN_BLOCK + k])
    ends = jnp.concatenate([solved[b][-1] for b in range(blocks)] + back, axis=0)
    for z in range(out_ref.shape[0]):
        out_ref[z] = ends


def carry_kernel(z_ref, ends_ref, pt_ref, b_ref, blocks_ref, m_ref, x_ref, fine_ref, s_ref, u_ref):
    planes = ends_ref.shape[0]
    count, width = m_ref.shape[0:2]
    cols = b_ref.shape[0] // count
    per = count // CHAIN_BLOCK
    blocks = planes * per
    state = jnp.zeros((cols, width), F32)
    grow = STEP_SCALE ** (-2 * CHAIN_BLOCK)
    back_ends = []
    for j in range(blocks):
        z, b = j // per, j % per
        s_ref[j] = state
        back = ends_ref[z, cols * (per + b) : cols * (per + b + 1), :]
        if j > 0:
            back = back + grow * dot_nt(state, pt_ref[2 * z + 1, width * b : width * (b + 1), :])
        back_ends.append(back)
        if j < blocks - 1:
            leaving = ends_ref[z, cols * b : cols * (b + 1), :]
            if j > 0:
                leaving = leaving + dot_nt(state, pt_ref[2 * z, width * b : width * (b + 1), :])
            state = leaving
    follow = jnp.zeros((cols, width), F32)
    for j in reversed(range(blocks)):
        z, b = j // per, j % per
        u_ref[j] = follow
        if j > 0:
            back = back_ends[j]
            if j < blocks - 1:
                back = back + dot_nn(follow, pt_ref[2 * z, width * b : width * (b + 1), :])
            follow = back
    first = z_ref[0] * per
    solved = [[] for _ in range(per)]
    running = [s_ref[first + b] for b in range(per)]
    for k in range(CHAIN_BLOCK):
        for b in range(per):
            j = b * CHAIN_BLOCK + k
            running[b] = b_ref[cols * j : cols * (j + 1), :] - dot_nt(running[b], m_ref[j])
            solved[b].append(running[b])
    running = [u_ref[first + b] for b in range(per)]
    for k in reversed(range(CHAIN_BLOCK)):
        for b in range(per):
            j = b * CHAIN_BLOCK + k
            right = solved[b][k] - running[b]
            if k > 0:
                running[b] = dot_nn(right, m_ref[j])
            answer = dot_nn(right, blocks_ref[2 * width * j : 2 * width * j + width, :])
            high = answer.astype(BF16).astype(F32)
            fine_ref[j] = jnp.concatenate([high, answer - high], axis=0).astype(BF16)
            s_ref[j] = high
    coarse = s_ref[0:count].reshape(count * cols, width).astype(BF16)
    for z in range(x_ref.shape[0]):
        x_ref[z] = coarse


def choose_kernel(plane_size, x_ref, code_ref, fine_ref, send_ref):
    rows = x_ref.shape[0]
    body = code_ref.shape[0]
    lane = lax.broadcasted_iota(jnp.int32, (body, rows), 1)
    codes = code_ref[...].astype(jnp.int32)
    values = x_ref[...]
    for d in range(send_ref.shape[0]):
        pick = (lane == codes[:, d : d + 1]).astype(F32).astype(BF16)
        send_ref[d, 0:body, :] = jnp.dot(pick, values, preferred_element_type=F32).astype(BF16)
        send_ref[d, body : body + 16, :] = fine_ref[d % plane_size]


def leaf_backward_kernel(w_ref, fwd_ref, inv_ref, upd_ref, out_ref, anc_ref):
    step = pl.program_id(0)
    last = pl.num_programs(0) - 1
    peers, rows, width = w_ref.shape
    cols = rows // 2

    @pl.when(step < last)
    def _():
        came = w_ref[...].astype(F32)
        for k in range(2):
            chosen = came[:, k * cols : (k + 1) * cols, :].reshape(peers * cols, width).astype(BF16)
            correction = jnp.dot(chosen, upd_ref[k], preferred_element_type=F32)
            residue = (fwd_ref[k].astype(F32) - correction).astype(BF16)
            out_ref[k] = lax.dot_general(
                inv_ref[k], residue, (((0,), (1,)), ((), ())), preferred_element_type=F32
            ).astype(BF16)

    @pl.when(step == last)
    def _():
        came = w_ref[...].astype(F32)
        total = came[:, 0:cols, :] + came[:, cols:rows, :]
        anc_ref[...] = total.reshape(peers * cols, width).T


def whole(shape):
    return pl.BlockSpec(shape, lambda *_: (0,) * len(shape))


SMEM = pl.BlockSpec(memory_space=pltpu.SMEM)


def call(kernel, operands, outs, scratch=(), flops=0, after=()):
    moved = sum(a.size * a.dtype.itemsize for a in list(operands) + list(outs))
    return pl.pallas_call(
        kernel,
        out_shape=outs,
        in_specs=[
            SMEM if a.dtype == jnp.int32 else pl.BlockSpec(memory_space=pltpu.VMEM) for a in operands
        ]
        + [pl.BlockSpec(memory_space=pl.ANY) for _ in after],
        out_specs=[pl.BlockSpec(memory_space=pltpu.VMEM) for _ in outs],
        scratch_shapes=list(scratch),
        compiler_params=pltpu.CompilerParams(vmem_limit_bytes=40 * 2**20),
        cost_estimate=pl.CostEstimate(flops=flops, bytes_accessed=moved, transcendentals=0),
    )(*operands, *after)


def local(leaf_rhs, leaf_inverse, leaf_update, leaf_target, anc_rhs, anc_inverse, anc_coupling):
    rhs, inv, upd = leaf_rhs[0], leaf_inverse[0], leaf_update[0]
    leaves, width, rhs_count = rhs.shape
    peers = lax.axis_size(PLANE_AXES)
    planes = lax.axis_size("z")
    plane_size = lax.axis_size(("x", "c"))
    chain = planes * plane_size
    cols = rhs_count // peers
    sds = jax.ShapeDtypeStruct
    y_index, z_index, c_index = (
        lax.axis_index(a).astype(jnp.int32).reshape(1) for a in ("y", "z", "c")
    )

    blocks = lax.all_gather(
        jnp.concatenate([anc_inverse[0], anc_coupling[0]], axis=0), ("x", "c"), axis=0, tiled=True
    )

    targets = leaf_target.astype(jnp.int32).reshape(leaves)
    steps = leaves // 2 + 1
    leaf = lambda i: (jnp.minimum(i, steps - 2), 0, 0)
    forward, send = pl.pallas_call(
        functools.partial(leaf_forward_kernel, peers),
        grid=(steps,),
        out_shape=[
            sds((leaves, rhs_count, width), BF16),
            sds((peers, cols * leaves + 2 * cols, width), BF16),
        ],
        in_specs=[
            SMEM,
            pl.BlockSpec((2, width, rhs_count), leaf),
            pl.BlockSpec((2, width, width), leaf),
            pl.BlockSpec((2, width, width), leaf),
            SMEM,
            whole((width, rhs_count)),
        ],
        out_specs=[
            pl.BlockSpec((2, rhs_count, width), leaf),
            pl.BlockSpec((peers, 2 * cols, width), lambda i: (0, i, 0)),
        ],
        compiler_params=pltpu.CompilerParams(
            dimension_semantics=("arbitrary",), vmem_limit_bytes=40 * 2**20
        ),
    )(y_index, rhs, inv, upd, targets, anc_rhs[0])

    came = lax.all_to_all(send, PLANE_AXES, 0, 0, tiled=True)

    m_blocks, transfer = call(
        transfer_kernel,
        (c_index, blocks),
        [sds((plane_size, width, width), F32), sds((plane_size // CHAIN_BLOCK * width, width), F32)],
        after=(came,),
    )
    transfers = lax.all_gather(transfer, ("z", "c"), axis=0, tiled=True)
    transfers = transfers.reshape((2 * planes,) + transfer.shape)

    dense, anc_rows, codes = call(
        functools.partial(densify_kernel, plane_size),
        (came,),
        [
            sds((planes, plane_size * cols, width), BF16),
            sds((plane_size * cols, width), F32),
            sds((leaves * cols, peers), F32),
        ],
        scratch=[pltpu.VMEM((chain * cols, width), F32)],
        after=(transfer,),
    )
    sums = lax.all_to_all(dense, "z", 0, 0, tiled=True)
    b_rows, ends = call(
        block_solve_kernel,
        (sums, anc_rows, blocks, m_blocks),
        [
            sds((plane_size * cols, width), F32),
            sds((planes, 2 * (plane_size // CHAIN_BLOCK) * cols, width), F32),
        ],
    )
    all_ends = lax.all_to_all(ends, "z", 0, 0, tiled=True)
    per_chain = chain // CHAIN_BLOCK
    x_rows, fine = call(
        carry_kernel,
        (z_index, all_ends, transfers, b_rows, blocks, m_blocks),
        [sds((planes, plane_size * cols, width), BF16), sds((plane_size, 2 * cols, width), BF16)],
        scratch=[
            pltpu.VMEM((max(per_chain, plane_size), cols, width), F32),
            pltpu.VMEM((per_chain, cols, width), F32),
        ],
    )
    all_x = lax.all_to_all(x_rows, "z", 0, 0, tiled=True).reshape(chain * cols, width)
    (answer,) = call(
        functools.partial(choose_kernel, plane_size),
        (all_x, codes, fine),
        [sds(send.shape, BF16)],
    )
    answers = lax.all_to_all(answer, PLANE_AXES, 0, 0, tiled=True)

    leaf_solution, anc_solution = pl.pallas_call(
        leaf_backward_kernel,
        grid=(steps,),
        out_shape=[sds((leaves, width, rhs_count), BF16), sds((width, rhs_count), F32)],
        in_specs=[
            pl.BlockSpec((peers, 2 * cols, width), lambda i: (0, i, 0)),
            pl.BlockSpec((2, rhs_count, width), leaf),
            pl.BlockSpec((2, width, width), leaf),
            pl.BlockSpec((2, width, width), leaf),
        ],
        out_specs=[pl.BlockSpec((2, width, rhs_count), leaf), whole((width, rhs_count))],
        compiler_params=pltpu.CompilerParams(
            dimension_semantics=("arbitrary",), vmem_limit_bytes=40 * 2**20
        ),
    )(answers, forward, inv, upd)
    return (leaf_solution[None], anc_solution[None])


def build(mesh, sizes):
    inner = Mesh(mesh.devices.reshape(sizes), ("y", "z", "x", "c"))
    leaf4 = P("y", ("z", "x", "c"), None, None)
    owner = P(("z", "x", "c"), None, None)
    return jax.shard_map(
        local,
        mesh=inner,
        in_specs=(leaf4, leaf4, leaf4, P("y", ("z", "x", "c"), None), owner, owner, owner),
        out_specs=(leaf4, owner),
        check_vma=False,
    )


def solution(mesh):
    return build(mesh, (4, 8, 4, 2))
```

time: 987 us -> 157 us (0.16)
  matrix products: 398 us -> 0 us
  blocking collectives: 296 us -> 54.8 us
  waiting for transfers between devices: 240 us -> 37.5 us
  Pallas kernels: 0 us -> 27.5 us
  local copies, waits for them, and re-layouts: 21.5 us -> 8.67 us
  starting transfers between devices: 0.16 us -> 12 us
    dot_general x261 -> x0, matrix products: 398 us -> none  [the longest x64 116 us: chain_backward(): jnp.dot(inverse_block.T, solved_block - jnp.dot(coupling_block.T, followi...]
    unnamed x1 -> x0, blocking collectives: 296 us -> none
    all_gather x3 -> x2, waiting for transfers between devices: 196 us -> 8.78 us  [the longest x1 8.78 us: local(): transfers = lax.all_gather(transfer, ('z', 'c'), axis=0, tiled=True)]
    all_to_all x0 -> x3, blocking collectives: none -> 54.8 us  [the longest x1 27 us: local(): answers = lax.all_to_all(answer, PLANE_AXES, 0, 0, tiled=True)]
    psum x1 -> x0, waiting for transfers between devices: 43.3 us -> none  [local(): layer_total = lax.psum(own_total.reshape(block_width, rhs_count), 'gz')]
    all_to_all x0 -> x2, waiting for transfers between devices: none -> 28.7 us  [the longest x1 20.4 us: local(): came = lax.all_to_all(send, PLANE_AXES, 0, 0, tiled=True)]
    pallas_call x0 -> x7, Pallas kernels: none -> 27.5 us  [the longest x5 17.1 us: call(): pl.pallas_call(kernel, out_shape=outs, in_specs=[SMEM if a.dtype == jnp.i...]
    all_to_all x0 -> x2, starting transfers between devices: none -> 12 us  [the longest x1 8.59 us: local(): came = lax.all_to_all(send, PLANE_AXES, 0, 0, tiled=True)]
  transfers between devices with their start and end apart: 4 -> 4, of which waited for: 4 -> 3; matrix products, arithmetic and copies ran while one was open for 0% -> 0% of each run, Pallas kernels for 0% -> 6%
where the time goes in v1:
time: 157 us; the launch traced here: 156 us
  blocking collectives  54.8 us (35%)
  waiting for transfers between devices  37.5 us (24%)
  Pallas kernels  27.5 us (18%)
  between operations  14.1 us (9%)
  starting transfers between devices  12 us (8%)
  local copies, waits for them, and re-layouts  8.67 us (6%)
    all_to_all x1, blocking collectives, local(): answers = lax.all_to_all(answer, PLANE_AXES, 0, 0, tiled=True)  27 us
    all_to_all x1, waiting for transfers between devices, local(): came = lax.all_to_all(send, PLANE_AXES, 0, 0, tiled=True)  20.4 us
    pallas_call x5, Pallas kernels, call(): pl.pallas_call(kernel, out_shape=outs, in_specs=[SMEM if a.dtype == jnp.i...  17.1 us
    all_to_all x1, blocking collectives, local(): sums = lax.all_to_all(dense, 'z', 0, 0, tiled=True)  15.7 us
    all_to_all x1, blocking collectives, local(): lax.all_to_all(x_rows, 'z', 0, 0, tiled=True).reshape(chain * cols, width)  12.2 us
    all_gather x1, waiting for transfers between devices, local(): transfers = lax.all_gather(transfer, ('z', 'c'), axis=0, tiled=True)  8.78 us
    unnamed x24, local copies, waits for them, and re-layouts  8.67 us
    all_to_all x1, starting transfers between devices, local(): came = lax.all_to_all(send, PLANE_AXES, 0, 0, tiled=True)  8.59 us
  transfers between devices with their start and end apart: 4, of which 3 were waited for; matrix products, arithmetic and copies ran while one was open for 0% of the time, Pallas kernels for 6%

profile of v1, /device:TPU:1, one launch (start us, length us, event | category | flops | bytes accessed | tf_op | source)
XLA Modules:
  0.0 156.2 jit_solution(2492686333657470462)
XLA Ops:
  7.2 1.5 pad_maximum_fusion
  8.8 1.0 copy-done.3
  9.8 1.0 copy-done.5
  10.9 1.2 copy-done.9
  12.1 0.9 copy-done.10
  13.0 0.7 copy-done.11
  13.6 5.5 %shard_map.86 = (bf16[16,256,128]{2,1,0:T(8,128)(2,1)S(1)}, bf16[32,144,128]{2,1,0:T(8,128)(2,1)}) custom-call(s32[1]{0:T(128)} %bitcast.1.y_ref, bf16[16,128,256]{2,1,0:T(8,128)(2,1)S(1)} %bitcast.19, bf16[16,128,128]{2,1,0:T(8,128)(2,1)S(1)} %bitcast.15, bf16[16,128,128]{2,1,0:T(8,128)(2,1)S(1)} %bitcast.17, s32[16]{0:T(128)S(1)} %bitcast.22, ...), custom_call_target="tpu_custom_call" | custom-call | tf_op jit(solution)/shard_map/pallas_call | solution.py:279
  19.1 1.0 copy-done.7
  20.1 8.6 %all-to-all-start = ((bf16[32,144,128]{2,1,0:T(8,128)(2,1)}), bf16[32,144,128]{2,1,0:T(8,128)(2,1)S(1)}, u32[]{:S(2)}, u32[]{:S(2)}) async-start(bf16[32,144,128]{2,1,0:T(8,128)(2,1)} %get-tuple-element.15), calls=%async_computation | async-start | bytes 2359296 | tf_op jit(solution)/shard_map/all_to_all | solution.py:303
  28.8 20.4 %all-to-all-done.after_ref.v_ref = bf16[32,144,128]{2,1,0:T(8,128)(2,1)S(1)} async-done(((bf16[32,144,128]{2,1,0:T(8,128)(2,1)}), bf16[32,144,128]{2,1,0:T(8,128)(2,1)S(1)}, u32[]{:S(2)}, u32[]{:S(2)}) %all-to-all-start) | async-done | bytes 1179680 | tf_op jit(solution)/shard_map/all_to_all | solution.py:303
  49.2 1.2 copy-done
  50.4 2.8 %shard_map.87 = (f32[8,128,128]{2,1,0:T(8,128)S(1)}, f32[256,128]{1,0:T(8,128)}) custom-call(s32[1]{0:T(128)} %bitcast.7.c_ref, f32[2048,128]{1,0:T(8,128)S(1)} %copy-done, bf16[32,144,128]{2,1,0:T(8,128)(2,1)S(1)} %all-to-all-done.after_ref.v_ref), custom_call_target="tpu_custom_call" | custom-call | bytes 1703940 | tf_op jit(solution)/shard_map/pallas_call | solution.py:245
  53.2 1.2 shard_map.88
  54.5 15.7 %all_to_all.25.e_ref = bf16[8,64,128]{2,1,0:T(8,128)(2,1)S(1)} all-to-all(bf16[8,64,128]{2,1,0:T(8,128)(2,1)S(1)} %get-tuple-element.17), channel_id=1, replica_groups=mesh['y'=4,'z'=8,'x'=4,'c'=2] {'z'}, dimensions={0} | all-to-all | bytes 262144 | tf_op jit(solution)/shard_map/all_to_all | solution.py:325
  70.2 3.2 %shard_map.89 = (f32[64,128]{1,0:T(8,128)S(1)}, f32[8,32,128]{2,1,0:T(8,128)}) custom-call(bf16[8,64,128]{2,1,0:T(8,128)(2,1)S(1)} %all_to_all.25.e_ref, f32[64,128]{1,0:T(8,128)S(1)} %get-tuple-element.18.anc_ref, f32[2048,128]{1,0:T(8,128)S(1)} %copy-done.1, f32[8,128,128]{2,1,0:T(8,128)S(1)} %get-tuple-element.19.m_ref), custom_call_target="tpu_custom_call" | custom-call | bytes 1900544 | tf_op jit(solution)/shard_map/pallas_call | solution.py:245
  73.3 3.4 %all-to-all-start.2 = ((f32[8,32,128]{2,1,0:T(8,128)}), f32[8,32,128]{2,1,0:T(8,128)S(1)}, u32[]{:S(2)}, u32[]{:S(2)}) async-start(f32[8,32,128]{2,1,0:T(8,128)} %get-tuple-element.20), calls=%async_computation.2 | async-start | bytes 262144 | tf_op jit(solution)/shard_map/all_to_all | solution.py:334
  76.7 8.3 %all-to-all-done.2.ends_ref = f32[8,32,128]{2,1,0:T(8,128)S(1)} async-done(((f32[8,32,128]{2,1,0:T(8,128)}), f32[8,32,128]{2,1,0:T(8,128)S(1)}, u32[]{:S(2)}, u32[]{:S(2)}) %all-to-all-start.2) | async-done | bytes 131104 | tf_op jit(solution)/shard_map/all_to_all | solution.py:334
  85.0 8.8 %all-gather.5.cloned.1.call-done = f32[4096,128]{1,0:T(8,128)} async-done(((f32[256,128]{1,0:T(8,128)}), f32[4096,128]{1,0:T(8,128)}) %all-gather.5.cloned.1.call-update) | async-done | bytes 2097168 | tf_op jit(solution)/shard_map/all_gather | solution.py:311
  93.8 1.6 %copy-done.2 = f32[4096,128]{1,0:T(8,128)S(1)} copy-done((f32[4096,128]{1,0:T(8,128)S(1)}, f32[4096,128]{1,0:T(8,128)}, u32[]{:S(2)}) %copy-start.2) | copy-done | bytes 2097176
  95.4 8.6 %shard_map.90 = (bf16[8,64,128]{2,1,0:T(8,128)(2,1)S(1)}, bf16[8,16,128]{2,1,0:T(8,128)(2,1)S(1)}) custom-call(s32[1]{0:T(128)} %bitcast.z_ref, f32[8,32,128]{2,1,0:T(8,128)S(1)} %all-to-all-done.2.ends_ref, f32[16,256,128]{2,1,0:T(8,128)S(1)} %bitcast.14, f32[64,128]{1,0:T(8,128)S(1)} %get-tuple-element.21.b_ref, f32[2048,128]{1,0:T(8,128)S(1)} %copy-done.1, ...), custom_call_target="tpu_custom_call" | custom-call | bytes 3997700 | tf_op jit(solution)/shard_map/pallas_call | solution.py:245
  103.9 12.2 %all_to_all.26 = bf16[8,64,128]{2,1,0:T(8,128)(2,1)S(1)} all-to-all(bf16[8,64,128]{2,1,0:T(8,128)(2,1)S(1)} %get-tuple-element.22), channel_id=1, replica_groups=mesh['y'=4,'z'=8,'x'=4,'c'=2] {'z'}, dimensions={0} | all-to-all | bytes 262144 | tf_op jit(solution)/shard_map/all_to_all | solution.py:345
  116.1 1.3 shard_map.91
  117.4 27.0 %all_to_all.27.w_ref = bf16[32,144,128]{2,1,0:T(8,128)(2,1)S(1)} all-to-all(bf16[32,144,128]{2,1,0:T(8,128)(2,1)S(1)} %shard_map.91), channel_id=1, replica_groups=mesh['y'=4,'z'=8,'x'=4,'c'=2] {'y','x','c'}, dimensions={0} | all-to-all | bytes 2359296 | tf_op jit(solution)/shard_map/all_to_all | solution.py:351
  144.4 5.0 %shard_map.92 = (bf16[16,128,256]{2,1,0:T(8,128)(2,1)}, f32[128,256]{1,0:T(8,128)}) custom-call(bf16[32,144,128]{2,1,0:T(8,128)(2,1)S(1)} %all_to_all.27.w_ref, bf16[16,256,128]{2,1,0:T(8,128)(2,1)S(1)} %copy-done.8, bf16[16,128,128]{2,1,0:T(8,128)(2,1)S(1)} %bitcast.16, bf16[16,128,128]{2,1,0:T(8,128)(2,1)S(1)} %bitcast.18), custom_call_target="tpu_custom_call" | custom-call | tf_op jit(solution)/shard_map/pallas_call | solution.py:353
  (21 shorter events, 0.2 us)
Async XLA Ops:
  7.2 42.0 %all-gather.3.cloned.1.call-start = ((), (), s32[]{:S(2)}) async-start(), calls=%async_computation.5 | async-start | bytes 1179648 | tf_op jit(solution)/shard_map/all_gather | solution.py:272
  8.8 1.0 copy-start.3
  9.8 1.0 copy-start.5
  10.9 1.2 copy-start.9
  12.1 0.9 copy-start.10
  13.0 0.7 copy-start.11
  19.1 1.0 copy-start.7
  20.1 29.1 %all-to-all-start = ((bf16[32,144,128]{2,1,0:T(8,128)(2,1)}), bf16[32,144,128]{2,1,0:T(8,128)(2,1)S(1)}, u32[]{:S(2)}, u32[]{:S(2)}) async-start(bf16[32,144,128]{2,1,0:T(8,128)(2,1)} %get-tuple-element.15), calls=%async_computation | async-start | bytes 2359296 | tf_op jit(solution)/shard_map/all_to_all | solution.py:303
  28.7 65.1 %all-gather.5.cloned.1.call-start = ((), (), s32[]{:S(2)}) async-start(), calls=%async_computation.6 | async-start | bytes 2228224 | tf_op jit(solution)/shard_map/all_gather | solution.py:311
  49.2 1.2 copy-start
  53.2 17.0 %copy-start.1 = (f32[2048,128]{1,0:T(8,128)S(1)}, f32[2048,128]{1,0:T(8,128)}, u32[]{:S(2)}) copy-start(f32[2048,128]{1,0:T(8,128)} %all-gather.3.cloned.1.call-done.blocks_ref) | copy-start | bytes 3145732
  73.3 11.7 %all-to-all-start.2 = ((f32[8,32,128]{2,1,0:T(8,128)}), f32[8,32,128]{2,1,0:T(8,128)S(1)}, u32[]{:S(2)}, u32[]{:S(2)}) async-start(f32[8,32,128]{2,1,0:T(8,128)} %get-tuple-element.20), calls=%async_computation.2 | async-start | bytes 262144 | tf_op jit(solution)/shard_map/all_to_all | solution.py:334
  93.8 1.6 %copy-start.2 = (f32[4096,128]{1,0:T(8,128)S(1)}, f32[4096,128]{1,0:T(8,128)}, u32[]{:S(2)}) copy-start(f32[4096,128]{1,0:T(8,128)} %all-gather.5.cloned.1.call-done) | copy-start | bytes 6291460
  117.4 27.0 %copy-start.4 = (bf16[1,16,128,128]{3,2,1,0:T(8,128)(2,1)S(1)}, bf16[1,16,128,128]{3,2,1,0:T(8,128)(2,1)}, u32[]{:S(2)}) copy-start(bf16[1,16,128,128]{3,2,1,0:T(8,128)(2,1)} %param.8) | copy-start | bytes 1572868
  117.4 27.0 %copy-start.6 = (bf16[1,16,128,128]{3,2,1,0:T(8,128)(2,1)S(1)}, bf16[1,16,128,128]{3,2,1,0:T(8,128)(2,1)}, u32[]{:S(2)}) copy-start(bf16[1,16,128,128]{3,2,1,0:T(8,128)(2,1)} %param.9) | copy-start | bytes 1572868
  117.4 27.0 %copy-start.8 = (bf16[16,256,128]{2,1,0:T(8,128)(2,1)S(1)}, bf16[16,256,128]{2,1,0:T(8,128)(2,1)}, u32[]{:S(2)}) copy-start(bf16[16,256,128]{2,1,0:T(8,128)(2,1)} %copy-done.7) | copy-start | bytes 3145732
Sparse Core Ops, SparseCore 0:
  10.4 33.3 all-gather.2
  53.3 40.3 all-gather.4

commit v2 on v0

v2 whole, which is shorter than its diff:
```python
import functools

import jax
import jax.numpy as jnp
from jax import lax
from jax.experimental import pallas as pl
from jax.experimental.pallas import tpu as pltpu
from jax.sharding import Mesh
from jax.sharding import PartitionSpec as P

F32 = jnp.float32
BF16 = jnp.bfloat16
PLANE_AXES = ("y", "x")
STEP_SCALE = 2.0**-8
CHAIN_BLOCK = 4
COLS = 8
LEAF_STEP = 4


def dot_nn(a, b):
    return lax.dot_general(
        a, b, (((1,), (0,)), ((), ())), precision=lax.Precision.HIGHEST, preferred_element_type=F32
    )


def split(value):
    high = value.astype(BF16)
    return high, (value - high.astype(F32)).astype(BF16)


def rows_by(rows, parts, contract):
    count = rows.shape[0]
    high, low = split(rows)
    dims = (((1,), (contract,)), ((), ()))
    both = jnp.concatenate([high.astype(F32), low.astype(F32)], axis=0).astype(BF16)
    first = lax.dot_general(both, parts[0], dims, preferred_element_type=F32)
    total = first[:count] + first[count:]
    if len(parts) > 1:
        total = total + lax.dot_general(high, parts[1], dims, preferred_element_type=F32)
    return total


def rows_nn(rows, *parts):
    return rows_by(rows, parts, 0)


def rows_nt(rows, *parts):
    return rows_by(rows, parts, 1)


def leaf_forward_kernel(y_ref, tgt_ref, rhs_ref, inv_ref, upd_ref, anc_ref, fwd_ref, send_ref):
    step = pl.program_id(0)
    rhs_count, width = fwd_ref.shape[1:]
    peers = send_ref.shape[0]
    tiles = send_ref.shape[1]
    for pair in range(LEAF_STEP // 2):
        parts = []
        for k in range(2):
            leaf = 2 * pair + k
            forward = lax.dot_general(
                rhs_ref[leaf], inv_ref[leaf], (((0,), (1,)), ((), ())), preferred_element_type=F32
            ).astype(BF16)
            fwd_ref[leaf] = forward
            update = lax.dot_general(
                forward, upd_ref[leaf], (((1,), (1,)), ((), ())), preferred_element_type=F32
            )
            parts.append(update.reshape(peers, 2 * COLS, width))
        for half in range(2):
            rows = jnp.concatenate([p[:, half * COLS : (half + 1) * COLS, :] for p in parts], axis=1)
            send_ref[:, 2 * (step * (LEAF_STEP // 2) + pair) + half] = rows.astype(BF16)

    @pl.when(step == 0)
    def _():
        rows = anc_ref[...].T.reshape(peers, 2 * COLS, width)
        high = rows.astype(BF16).astype(F32)
        layer = y_ref[0]
        mine = jnp.where(layer == 0, high, jnp.where(layer == 2, rows - high, jnp.zeros_like(rows)))
        over = jnp.where(layer == 1, high, jnp.where(layer == 3, rows - high, jnp.zeros_like(rows)))
        mine = mine[:, 0:COLS] + over[:, COLS : 2 * COLS]
        leaf = lax.broadcasted_iota(jnp.int32, (COLS, width), 1) // COLS
        names = jnp.zeros((COLS, width), F32)
        for k in range(tgt_ref.shape[0]):
            names = jnp.where(leaf == k, tgt_ref[k].astype(F32), names)
        names = jnp.broadcast_to(names[None], (peers, COLS, width))
        send_ref[:, tiles - 1] = jnp.concatenate([mine, names], axis=1).astype(BF16)


def own_pair_kernel(inv_ref, cpl_ref, out_ref):
    inverse = inv_ref[0]
    out_ref[0], out_ref[1] = split(dot_nn(inverse, cpl_ref[0]))
    out_ref[2] = inverse.astype(BF16)


def transfer_kernel(x_count, x_ref, c_ref, *refs):
    pairs = refs[: 2 * x_count]
    m_ref, carry_ref, plane_ref = refs[-3:]
    count, _, width = m_ref.shape[0:3]
    x, core = x_ref[0], c_ref[0]
    for d in range(x_count):
        for other in range(2):
            place = 2 * lax.rem(x + d, x_count) + jnp.where(other == 0, core, 1 - core)
            m_ref[place] = pairs[other * x_count + d][...]
    blocks = count // CHAIN_BLOCK

    def scaled(j):
        return (m_ref[j, 0].astype(F32) + m_ref[j, 1].astype(F32)) * STEP_SCALE

    chains = [-scaled(b * CHAIN_BLOCK) for b in range(blocks)]
    for k in range(1, CHAIN_BLOCK):
        for b in range(blocks):
            chains[b] = -dot_nn(scaled(b * CHAIN_BLOCK + k), chains[b])
    total = chains[0]
    for b in range(1, blocks):
        total = dot_nn(chains[b], total)
    for b in range(blocks):
        carry_ref[b, 0], carry_ref[b, 1] = split(chains[b] * (STEP_SCALE**-CHAIN_BLOCK))
    high, low = split(total)
    plane_ref[...] = jnp.where(core == 0, high.astype(F32), low.astype(F32)).astype(BF16)


def densify_kernel(plane_size, z_ref, c_ref, v_ref, keep_ref, give_ref, code_ref, acc_ref):
    sources, tiles, rows, width = v_ref.shape
    planes = keep_ref.shape[0]
    x_count = plane_size // 2
    body = (tiles - 1) // 2 * rows
    lane = lax.broadcasted_iota(jnp.int32, (sources, body), 1)
    last = v_ref[:, tiles - 1].astype(F32)
    codes = last[:, COLS, :].astype(jnp.int32) * COLS + lane % COLS
    code_ref[...] = codes.astype(F32).T
    row = lax.broadcasted_iota(jnp.int32, (acc_ref.shape[1], body), 0)

    def values(s):
        came = v_ref[s, 0 : tiles - 1].reshape((tiles - 1) // 2, 2, rows, width)
        return jnp.concatenate([came[:, half].reshape(body, width) for half in range(2)], axis=1)

    total = None
    for s in range(0, sources, 2):
        pick = jnp.concatenate(
            [(row == codes[s + i : s + i + 1, :]).astype(F32).astype(BF16) for i in range(2)], axis=1
        )
        both = jnp.concatenate([values(s), values(s + 1)], axis=0)
        term = jnp.dot(pick, both, preferred_element_type=F32)
        total = term if total is None else total + term
    for half in range(2):
        acc_ref[half] = -total[:, width * half : width * (half + 1)]
    z, core = z_ref[0], c_ref[0]
    own = pl.multiple_of(z * plane_size * COLS, plane_size * COLS)
    for x in range(x_count):
        for half in range(2):
            mine = last[half * x_count + x, 0:COLS]
            for y in range(half + 2, sources // x_count, 2):
                mine = mine + last[y * x_count + x, 0:COLS]
            place = pl.ds(pl.multiple_of(own + (2 * x + core) * COLS, COLS), COLS)
            acc_ref[half, place, :] += mine
    per = plane_size * COLS
    for z in range(planes):
        keep_ref[z] = acc_ref[core, per * z : per * (z + 1), :]
        give_ref[z] = acc_ref[1 - core, per * z : per * (z + 1), :].astype(BF16)


def block_solve_kernel(e_ref, m_ref, carry_ref, plane_ref, b_ref, mid_ref, out_ref):
    count, _, width = m_ref.shape[0:3]
    reduced = e_ref[0].astype(F32)
    for s in range(1, e_ref.shape[0]):
        reduced = reduced + e_ref[s].astype(F32)
    bs = []
    for j in range(count):
        b = rows_nt(reduced[COLS * j : COLS * (j + 1)], m_ref[j, 2])
        b_ref[COLS * j : COLS * (j + 1), :] = b
        bs.append(b)
    ends = [bs[0], bs[CHAIN_BLOCK]]
    for k in range(1, CHAIN_BLOCK):
        for b in range(2):
            j = b * CHAIN_BLOCK + k
            ends[b] = bs[j] - rows_nt(ends[b], m_ref[j, 0], m_ref[j, 1])
    mid_ref[...] = ends[0]
    leaving = ends[1] + rows_nt(ends[0], carry_ref[1, 0], carry_ref[1, 1])
    high, low = split(leaving)
    ends = jnp.concatenate([high.astype(F32), low.astype(F32)], axis=0).astype(BF16)
    for z in range(out_ref.shape[0]):
        out_ref[z, 0 : 2 * COLS] = ends
        out_ref[z, 2 * COLS : 2 * COLS + width] = plane_ref[...]


def carry_forward_kernel(
    z_ref, c_ref, ends_ref, other_ref, b_ref, mid_ref, m_ref, carry_ref, s_ref, back_ref, flow_ref, phi_ref
):
    planes = ends_ref.shape[0]
    width = m_ref.shape[2]
    core = c_ref[0]
    for z in range(planes):
        phi_ref[z, core] = ends_ref[z, 2 * COLS : 2 * COLS + width]
        phi_ref[z, 1 - core] = other_ref[z, 2 * COLS : 2 * COLS + width]
    grow = STEP_SCALE ** (-2 * CHAIN_BLOCK)
    own = z_ref[0]
    state = jnp.zeros((COLS, width), F32)
    flow = state
    for z in range(planes - 1):
        parts = ends_ref[z, 0 : 2 * COLS].astype(F32)
        leaving = parts[0:COLS] + parts[COLS : 2 * COLS]
        if z > 0:
            leaving = leaving + grow * rows_nt(state, phi_ref[z, 0], phi_ref[z, 1])
        state = leaving
        flow = jnp.where(own == z + 1, state, flow)
    running = [flow, mid_ref[...] + rows_nt(flow, carry_ref[0, 0], carry_ref[0, 1])]
    solved = [[], []]
    for k in range(CHAIN_BLOCK):
        for b in range(2):
            j = b * CHAIN_BLOCK + k
            running[b] = b_ref[COLS * j : COLS * (j + 1), :] - rows_nt(running[b], m_ref[j, 0], m_ref[j, 1])
            s_ref[COLS * j : COLS * (j + 1), :] = running[b]
            solved[b].append(running[b])
    back = [None, None]
    for k in reversed(range(CHAIN_BLOCK)):
        for b in range(2):
            j = b * CHAIN_BLOCK + k
            right = solved[b][k] if back[b] is None else solved[b][k] - back[b]
            back[b] = rows_nn(right, m_ref[j, 0], m_ref[j, 1])
    flow_ref[...] = back[1]
    leaving = back[0] + rows_nn(back[1], carry_ref[0, 0], carry_ref[0, 1])
    for z in range(back_ref.shape[0]):
        back_ref[z] = leaving


def carry_backward_kernel(z_ref, ends_ref, phi_ref, s_ref, flow_ref, m_ref, carry_ref, x_ref):
    planes = ends_ref.shape[0]
    count, _, width = m_ref.shape[0:3]
    grow = STEP_SCALE ** (-2 * CHAIN_BLOCK)
    own = z_ref[0]
    state = jnp.zeros((COLS, width), F32)
    flow = state
    for z in reversed(range(1, planes)):
        leaving = ends_ref[z]
        if z < planes - 1:
            leaving = leaving + grow * rows_nn(state, phi_ref[z, 0], phi_ref[z, 1])
        state = leaving
        flow = jnp.where(own == z - 1, state, flow)
    running = [flow_ref[...] + rows_nn(flow, carry_ref[1, 0], carry_ref[1, 1]), flow]
    answers = [None] * count
    for k in reversed(range(CHAIN_BLOCK)):
        for b in range(2):
            j = b * CHAIN_BLOCK + k
            right = s_ref[COLS * j : COLS * (j + 1), :] - running[b]
            if k > 0:
                running[b] = rows_nn(right, m_ref[j, 0], m_ref[j, 1])
            answers[j] = rows_nn(right, m_ref[j, 2])
    coarse = jnp.concatenate(answers, axis=0).astype(BF16)
    for z in range(x_ref.shape[0]):
        x_ref[z] = coarse


def choose_kernel(plane_size, z_ref, c_ref, x_ref, other_ref, code_ref, send_ref):
    peers, tiles, rows, width = send_ref.shape
    planes = x_ref.shape[0]
    body = code_ref.shape[0]
    core = c_ref[0]
    lane = lax.broadcasted_iota(jnp.int32, (body, planes * plane_size * COLS), 1)
    codes = code_ref[...].astype(jnp.int32)
    x_count = plane_size // 2
    mine, theirs = x_ref[...].astype(F32), other_ref[...].astype(F32)
    halves = [jnp.where(core == half, mine, theirs).reshape(lane.shape[1], width) for half in range(2)]
    values = jnp.concatenate(halves, axis=1).astype(BF16)
    mine, theirs = x_ref[z_ref[0]].astype(F32), other_ref[z_ref[0]].astype(F32)
    own = [jnp.where(core == half, mine, theirs) for half in range(2)]
    for d in range(peers):
        pick = (lane == codes[:, d : d + 1]).astype(F32).astype(BF16)
        chosen = jnp.dot(pick, values, preferred_element_type=F32).astype(BF16)
        for half in range(2):
            part = chosen[:, width * half : width * (half + 1)].reshape(body // rows, rows, width)
            for pair in range(body // rows):
                send_ref[d, 2 * pair + half] = part[pair]
        j = 2 * (d % x_count)
        ends = [
            jnp.where(
                core == 0, own[half][COLS * j : COLS * (j + 1)], own[half][COLS * (j + 1) : COLS * (j + 2)]
            )
            for half in range(2)
        ]
        send_ref[d, tiles - 1] = jnp.concatenate(ends, axis=0).astype(BF16)


def leaf_backward_kernel(w_ref, tail_ref, fwd_ref, inv_ref, upd_ref, out_ref, anc_ref):
    step = pl.program_id(0)
    peers, _, rows, width = w_ref.shape
    rhs_count = fwd_ref.shape[1]
    for pair in range(LEAF_STEP // 2):
        came = [w_ref[:, 2 * pair + half].astype(F32) for half in range(2)]
        for k in range(2):
            leaf = 2 * pair + k
            both = jnp.concatenate([c[:, k * COLS : (k + 1) * COLS, :] for c in came], axis=1)
            chosen = both.reshape(rhs_count, width).astype(BF16)
            correction = jnp.dot(chosen, upd_ref[leaf], preferred_element_type=F32)
            residue = (fwd_ref[leaf].astype(F32) - correction).astype(BF16)
            out_ref[leaf] = lax.dot_general(
                inv_ref[leaf], residue, (((0,), (1,)), ((), ())), preferred_element_type=F32
            ).astype(BF16)

    @pl.when(step == 0)
    def _():
        anc_ref[...] = tail_ref[:, 0].astype(F32).reshape(rhs_count, width).T


SMEM = pl.BlockSpec(memory_space=pltpu.SMEM)


def call(kernel, operands, outs, scratch=(), flops=0, after=()):
    moved = sum(a.size * a.dtype.itemsize for a in list(operands) + list(outs))
    if after:
        inner, count = kernel, len(operands)
        kernel = lambda *refs: inner(*refs[:count], *refs[count + len(after) :])
    return pl.pallas_call(
        kernel,
        out_shape=outs,
        in_specs=[
            SMEM if a.dtype == jnp.int32 else pl.BlockSpec(memory_space=pltpu.VMEM) for a in operands
        ]
        + [pl.BlockSpec(memory_space=pl.ANY) for _ in after],
        out_specs=[pl.BlockSpec(memory_space=pltpu.VMEM) for _ in outs],
        scratch_shapes=list(scratch),
        compiler_params=pltpu.CompilerParams(vmem_limit_bytes=16 * 2**20),
        cost_estimate=pl.CostEstimate(flops=flops, bytes_accessed=moved, transcendentals=0),
    )(*operands, *after)


def shift(value, axis, by):
    size = lax.axis_size(axis)
    return lax.ppermute(value, axis, [((i + by) % size, i) for i in range(size)])


def local(leaf_rhs, leaf_inverse, leaf_update, leaf_target, anc_rhs, anc_inverse, anc_coupling):
    rhs, inv, upd = leaf_rhs[0], leaf_inverse[0], leaf_update[0]
    leaves, width, rhs_count = rhs.shape
    peers = lax.axis_size(PLANE_AXES)
    planes = lax.axis_size("z")
    x_count = lax.axis_size("x")
    plane_size = 2 * x_count
    chain = planes * plane_size
    pairs = leaves // 2
    sds = jax.ShapeDtypeStruct
    y_index, z_index, x_index, c_index = (
        lax.axis_index(a).astype(jnp.int32).reshape(1) for a in ("y", "z", "x", "c")
    )

    (own_pair,) = call(own_pair_kernel, (anc_inverse, anc_coupling), [sds((3, width, width), BF16)])
    along = [own_pair] + [shift(own_pair, "x", d) for d in range(1, x_count)]

    steps = leaves // LEAF_STEP
    leaf = lambda i: (i, 0, 0)
    forward, send = pl.pallas_call(
        leaf_forward_kernel,
        grid=(steps,),
        out_shape=[
            sds((leaves, rhs_count, width), BF16),
            sds((peers, 2 * pairs + 1, 2 * COLS, width), BF16),
        ],
        in_specs=[
            SMEM,
            SMEM,
            pl.BlockSpec((LEAF_STEP, width, rhs_count), leaf),
            pl.BlockSpec((LEAF_STEP, width, width), leaf),
            pl.BlockSpec((LEAF_STEP, width, width), leaf),
            pl.BlockSpec((width, rhs_count), lambda i: (0, 0)),
        ],
        out_specs=[
            pl.BlockSpec((LEAF_STEP, rhs_count, width), leaf),
            pl.BlockSpec((peers, 2 * pairs + 1, 2 * COLS, width), lambda i: (0, 0, 0, 0)),
        ],
        compiler_params=pltpu.CompilerParams(
            dimension_semantics=("arbitrary",), vmem_limit_bytes=60 * 2**20
        ),
    )(y_index, leaf_target.astype(jnp.int32).reshape(leaves), rhs, inv, upd, anc_rhs[0])

    send, *along = lax.optimization_barrier((send, *along))
    came = lax.all_to_all(send, PLANE_AXES, 0, 0, tiled=True)

    across = [shift(pair, "c", 1) for pair in along]
    m_blocks, carries, plane_carry = call(
        functools.partial(transfer_kernel, x_count),
        (x_index, c_index, *along, *across),
        [
            sds((plane_size, 3, width, width), BF16),
            sds((2, 2, width, width), BF16),
            sds((width, width), BF16),
        ],
    )

    keep, give, codes = call(
        functools.partial(densify_kernel, plane_size),
        (z_index, c_index, came),
        [
            sds((planes, plane_size * COLS, width), F32),
            sds((planes, plane_size * COLS, width), BF16),
            sds((leaves * COLS, peers), F32),
        ],
        scratch=[pltpu.VMEM((2, chain * COLS, width), F32)],
        after=(plane_carry,),
    )
    dense = (keep + shift(give, "c", 1).astype(F32)).astype(BF16)
    sums = lax.all_to_all(dense, "z", 0, 0, tiled=True)
    b_rows, middle, ends = call(
        block_solve_kernel,
        (sums, m_blocks, carries, plane_carry),
        [
            sds((plane_size * COLS, width), F32),
            sds((COLS, width), F32),
            sds((planes, 2 * COLS + width, width), BF16),
        ],
    )
    all_ends = lax.all_to_all(ends, "z", 0, 0, tiled=True)
    other_ends = shift(all_ends, "c", 1)
    s_rows, back, flow, phis = call(
        carry_forward_kernel,
        (z_index, c_index, all_ends, other_ends, b_rows, middle, m_blocks, carries),
        [
            sds((plane_size * COLS, width), F32),
            sds((planes, COLS, width), F32),
            sds((COLS, width), F32),
            sds((planes, 2, width, width), BF16),
        ],
    )
    all_back = lax.all_to_all(back, "z", 0, 0, tiled=True)
    (x_rows,) = call(
        carry_backward_kernel,
        (z_index, all_back, phis, s_rows, flow, m_blocks, carries),
        [sds((planes, plane_size * COLS, width), BF16)],
    )
    all_x = lax.all_to_all(x_rows, "z", 0, 0, tiled=True)
    other_x = shift(all_x, "c", 1)
    (answer,) = call(
        functools.partial(choose_kernel, plane_size),
        (z_index, c_index, all_x, other_x, codes),
        [sds((peers, 2 * pairs + 1, 2 * COLS, width), BF16)],
    )
    answers = lax.all_to_all(answer, PLANE_AXES, 0, 0, tiled=True)

    leaf_solution, anc_solution = pl.pallas_call(
        leaf_backward_kernel,
        grid=(steps,),
        out_shape=[sds((leaves, width, rhs_count), BF16), sds((width, rhs_count), F32)],
        in_specs=[
            pl.BlockSpec((peers, LEAF_STEP, 2 * COLS, width), lambda i: (0, i, 0, 0)),
            pl.BlockSpec((peers, 1, 2 * COLS, width), lambda i: (0, 2 * pairs, 0, 0)),
            pl.BlockSpec((LEAF_STEP, rhs_count, width), leaf),
            pl.BlockSpec((LEAF_STEP, width, width), leaf),
            pl.BlockSpec((LEAF_STEP, width, width), leaf),
        ],
        out_specs=[
            pl.BlockSpec((LEAF_STEP, width, rhs_count), leaf),
            pl.BlockSpec((width, rhs_count), lambda i: (0, 0)),
        ],
        compiler_params=pltpu.CompilerParams(
            dimension_semantics=("arbitrary",), vmem_limit_bytes=40 * 2**20
        ),
    )(answers, answers, forward, inv, upd)
    return (leaf_solution[None], anc_solution[None])


def build(mesh, sizes):
    inner = Mesh(mesh.devices.reshape(sizes), ("y", "z", "x", "c"))
    leaf4 = P("y", ("z", "x", "c"), None, None)
    owner = P(("z", "x", "c"), None, None)
    return jax.shard_map(
        local,
        mesh=inner,
        in_specs=(leaf4, leaf4, leaf4, P("y", ("z", "x", "c"), None), owner, owner, owner),
        out_specs=(leaf4, owner),
        check_vma=False,
    )


def solution(mesh):
    return build(mesh, (4, 8, 4, 2))
```

time: 987 us -> 123 us (0.12)
  matrix products: 398 us -> 0 us
  blocking collectives: 296 us -> 67 us
  waiting for transfers between devices: 240 us -> 15.3 us
  starting transfers between devices: 0.16 us -> 23 us
  local copies, waits for them, and re-layouts: 21.5 us -> 1.69 us
  between operations: 15.7 us -> 0.77 us
  Pallas kernels: 0 us -> 14.9 us
    dot_general x261 -> x0, matrix products: 398 us -> none  [the longest x64 116 us: chain_backward(): jnp.dot(inverse_block.T, solved_block - jnp.dot(coupling_block.T, followi...]
    unnamed x1 -> x0, blocking collectives: 296 us -> none
    all_gather x3 -> x0, waiting for transfers between devices: 196 us -> none  [the longest x1 84.5 us: local(): lax.all_gather(reduced[None], 'grid', axis=0, tiled=True)]
    all_to_all x0 -> x5, blocking collectives: none -> 67 us  [the longest x1 19.8 us: local(): answers = lax.all_to_all(answer, PLANE_AXES, 0, 0, tiled=True)]
    psum x1 -> x0, waiting for transfers between devices: 43.3 us -> none  [local(): layer_total = lax.psum(own_total.reshape(block_width, rhs_count), 'gz')]
    ppermute x0 -> x10, starting transfers between devices: none -> 18.7 us  [shift(): lax.ppermute(value, axis, [((i + by) % size, i) for i in range(size)])]
    pallas_call x0 -> x9, Pallas kernels: none -> 14.9 us  [the longest x7 6.75 us: call(): pl.pallas_call(kernel, out_shape=outs, in_specs=[SMEM if a.dtype == jnp.i...]
    all_to_all x0 -> x1, waiting for transfers between devices: none -> 10.9 us  [local(): came = lax.all_to_all(send, PLANE_AXES, 0, 0, tiled=True)]
  transfers between devices with their start and end apart: 4 -> 11, of which waited for: 4 -> 8; matrix products, arithmetic and copies ran while one was open for 0% -> 0% of each run, Pallas kernels for 0% -> 5%
where the time goes in v2:
time: 123 us
  blocking collectives  67 us (54%)
  starting transfers between devices  23 us (19%)
  waiting for transfers between devices  15.3 us (12%)
  Pallas kernels  14.9 us (12%)
  local copies, waits for them, and re-layouts  1.69 us (1%)
    all_to_all x1, blocking collectives, local(): answers = lax.all_to_all(answer, PLANE_AXES, 0, 0, tiled=True)  19.8 us
    ppermute x10, starting transfers between devices, shift(): lax.ppermute(value, axis, [((i + by) % size, i) for i in range(size)])  18.7 us
    all_to_all x1, blocking collectives, local(): sums = lax.all_to_all(dense, 'z', 0, 0, tiled=True)  15.9 us
    all_to_all x1, blocking collectives, local(): all_ends = lax.all_to_all(ends, 'z', 0, 0, tiled=True)  11.7 us
    all_to_all x1, waiting for transfers between devices, local(): came = lax.all_to_all(send, PLANE_AXES, 0, 0, tiled=True)  10.9 us
    all_to_all x1, blocking collectives, local(): all_x = lax.all_to_all(x_rows, 'z', 0, 0, tiled=True)  10.4 us
    all_to_all x1, blocking collectives, local(): all_back = lax.all_to_all(back, 'z', 0, 0, tiled=True)  9.26 us
    pallas_call x7, Pallas kernels, call(): pl.pallas_call(kernel, out_shape=outs, in_specs=[SMEM if a.dtype == jnp.i...  6.75 us
  transfers between devices with their start and end apart: 11, of which 8 were waited for; matrix products, arithmetic and copies ran while one was open for 0% of the time, Pallas kernels for 5%

profile of v2, /device:TPU:1, one launch (start us, length us, event | category | flops | bytes accessed | tf_op | source)
XLA Modules:
  0.0 122.6 jit_solution(6285216943092125522)
XLA Ops:
  0.6 0.8 copy-done.3
  1.5 0.8 copy-done.4
  2.5 2.1 %collective-permute-start.2 = (bf16[3,128,128]{2,1,0:T(8,128)(2,1)S(1)}, bf16[3,128,128]{2,1,0:T(8,128)(2,1)S(1)}, u32[]{:S(2)}, u32[]{:S(2)}) collective-permute-start(bf16[3,128,128]{2,1,0:T(8,128)(2,1)S(1)} %shard_map.87.refs_0_), channel_id=1, source_target_pairs={{6,0},{0,2},{2,4},{4,6},{7,1},{1,3},{3,5},{5,7},{14,8},{8,10},{10,... | collective-permute-start | bytes 294920 | tf_op jit(solution)/shard_map/ppermute | solution.py:327
  4.6 2.5 %collective-permute-start.1 = (bf16[3,128,128]{2,1,0:T(8,128)(2,1)S(1)}, bf16[3,128,128]{2,1,0:T(8,128)(2,1)S(1)}, u32[]{:S(2)}, u32[]{:S(2)}) collective-permute-start(bf16[3,128,128]{2,1,0:T(8,128)(2,1)S(1)} %shard_map.87.refs_0_), channel_id=1, source_target_pairs={{4,0},{6,2},{0,4},{2,6},{5,1},{7,3},{1,5},{3,7},{12,8},{14,10},{8,... | collective-permute-start | bytes 294920 | tf_op jit(solution)/shard_map/ppermute | solution.py:327
  7.1 1.2 collective-permute-start
  8.2 5.0 %shard_map.86 = (bf16[16,256,128]{2,1,0:T(8,128)(2,1)}, bf16[16,17,16,128]{3,2,1,0:T(8,128)(2,1)}) custom-call(s32[1]{0:T(128)} %bitcast.2.y_ref, s32[16]{0:T(128)} %bitcast.17, bf16[16,128,256]{2,1,0:T(8,128)(2,1)} %bitcast.15, bf16[16,128,128]{2,1,0:T(8,128)(2,1)} %bitcast.11, bf16[16,128,128]{2,1,0:T(8,128)(2,1)} %bitcast.13, f32[128,256]{1,0:T(8,128)} %bitcast.16), custom_call_target="tpu_custom_call" | custom-call | tf_op jit(solution)/shard_map/pallas_call | solution.py:349
  13.3 4.3 %all-to-all-start = ((bf16[16,17,16,128]{3,2,1,0:T(8,128)(2,1)}), bf16[16,17,16,128]{3,2,1,0:T(8,128)(2,1)S(1)}, u32[]{:S(2)}, u32[]{:S(2)}) async-start(bf16[16,17,16,128]{3,2,1,0:T(8,128)(2,1)} %get-tuple-element.25), calls=%async_computation | async-start | bytes 2228224 | tf_op jit(solution)/shard_map/all_to_all | solution.py:374
  17.6 2.1 %collective-permute-start.3 = (bf16[3,128,128]{2,1,0:T(8,128)(2,1)S(1)}, bf16[3,128,128]{2,1,0:T(8,128)(2,1)S(1)}, u32[]{:S(2)}, u32[]{:S(2)}) collective-permute-start(bf16[3,128,128]{2,1,0:T(8,128)(2,1)S(1)} %shard_map.87.refs_0_), channel_id=1, source_target_pairs={{1,0},{0,1},{3,2},{2,3},{5,4},{4,5},{7,6},{6,7},{9,8},{8,9},{11,10... | collective-permute-start | bytes 294920 | tf_op jit(solution)/shard_map/ppermute | solution.py:327
  21.5 1.0 shard_map.88
  22.6 10.9 %all-to-all-done.refs_2_ = bf16[16,17,16,128]{3,2,1,0:T(8,128)(2,1)S(1)} async-done(((bf16[16,17,16,128]{3,2,1,0:T(8,128)(2,1)}), bf16[16,17,16,128]{3,2,1,0:T(8,128)(2,1)S(1)}, u32[]{:S(2)}, u32[]{:S(2)}) %all-to-all-start) | async-done | bytes 1114144 | tf_op jit(solution)/shard_map/all_to_all | solution.py:374
  34.2 3.4 %collective-permute-start.7 = (bf16[8,64,128]{2,1,0:T(8,128)(2,1)S(1)}, bf16[8,64,128]{2,1,0:T(8,128)(2,1)S(1)}, u32[]{:S(2)}, u32[]{:S(2)}) collective-permute-start(bf16[8,64,128]{2,1,0:T(8,128)(2,1)S(1)} %get-tuple-element.32), channel_id=1, source_target_pairs={{1,0},{0,1},{3,2},{2,3},{5,4},{4,5},{7,6},{6,7},{9,8},{8,9},{11,10... | collective-permute-start | bytes 393224 | tf_op jit(solution)/shard_map/ppermute | solution.py:327
  37.6 1.0 collective-permute-done.7
  38.6 15.9 %all_to_all.30.e_ref = bf16[8,64,128]{2,1,0:T(8,128)(2,1)S(1)} all-to-all(bf16[8,64,128]{2,1,0:T(8,128)(2,1)S(1)} %add_convert_fusion), channel_id=1, replica_groups=mesh['y'=4,'z'=8,'x'=4,'c'=2] {'z'}, dimensions={0} | all-to-all | bytes 262144 | tf_op jit(solution)/shard_map/all_to_all | solution.py:399
  55.1 11.7 %all_to_all.31.ends_ref = bf16[8,144,128]{2,1,0:T(8,128)(2,1)S(1)} all-to-all(bf16[8,144,128]{2,1,0:T(8,128)(2,1)S(1)} %get-tuple-element.35), channel_id=1, replica_groups=mesh['y'=4,'z'=8,'x'=4,'c'=2] {'z'}, dimensions={0} | all-to-all | bytes 589824 | tf_op jit(solution)/shard_map/all_to_all | solution.py:409
  66.8 4.2 %collective-permute-start.8 = (bf16[8,144,128]{2,1,0:T(8,128)(2,1)S(1)}, bf16[8,144,128]{2,1,0:T(8,128)(2,1)S(1)}, u32[]{:S(2)}, u32[]{:S(2)}) collective-permute-start(bf16[8,144,128]{2,1,0:T(8,128)(2,1)S(1)} %all_to_all.31.ends_ref), channel_id=1, source_target_pairs={{1,0},{0,1},{3,2},{2,3},{5,4},{4,5},{7,6},{6,7},{9,8},{8,9},{11,10... | collective-permute-start | bytes 884744 | tf_op jit(solution)/shard_map/ppermute | solution.py:327
  71.0 1.2 collective-permute-done.8.other_ref
  72.3 2.0 %shard_map.91 = (f32[64,128]{1,0:T(8,128)S(1)}, f32[8,8,128]{2,1,0:T(8,128)S(1)}, f32[8,128]{1,0:T(8,128)S(1)}, bf16[8,2,128,128]{3,2,1,0:T(8,128)(2,1)S(1)}) custom-call(s32[1]{0:T(128)} %bitcast.refs_0_.z_ref, s32[1]{0:T(128)} %bitcast.1.c_ref.refs_1_, bf16[8,144,128]{2,1,0:T(8,128)(2,1)S(1)} %all_to_all.31.ends_ref, ...), custom_call_target="tpu_custom_call" | custom-call | bytes 2138120 | tf_op jit(solution)/shard_map/pallas_call | solution.py:311
  74.3 9.3 %all_to_all.32.ends_ref = f32[8,8,128]{2,1,0:T(8,128)S(1)} all-to-all(f32[8,8,128]{2,1,0:T(8,128)S(1)} %get-tuple-element.38), channel_id=1, replica_groups=mesh['y'=4,'z'=8,'x'=4,'c'=2] {'z'}, dimensions={0} | all-to-all | bytes 65536 | tf_op jit(solution)/shard_map/all_to_all | solution.py:421
  83.5 1.4 %shard_map.92 = bf16[8,64,128]{2,1,0:T(8,128)(2,1)S(1)} custom-call(s32[1]{0:T(128)} %bitcast.refs_0_.z_ref, f32[8,8,128]{2,1,0:T(8,128)S(1)} %all_to_all.32.ends_ref, bf16[8,2,128,128]{3,2,1,0:T(8,128)(2,1)S(1)} %get-tuple-element.39.phi_ref, f32[64,128]{1,0:T(8,128)S(1)} %get-tuple-element.40.s_ref, f32[8,128]{1,0:T(8,128)S(1)} %get-tuple-element.41.flow_ref, ...), custom_call_target="tpu_custom_call" | custom-call | bytes 1642500 | tf_op jit(solution)/shard_map/pallas_call | solution.py:311
  84.9 10.4 %all_to_all.33.x_ref = bf16[8,64,128]{2,1,0:T(8,128)(2,1)S(1)} all-to-all(bf16[8,64,128]{2,1,0:T(8,128)(2,1)S(1)} %shard_map.92), channel_id=1, replica_groups=mesh['y'=4,'z'=8,'x'=4,'c'=2] {'z'}, dimensions={0} | all-to-all | bytes 262144 | tf_op jit(solution)/shard_map/all_to_all | solution.py:427
  95.2 2.6 %collective-permute-start.9 = (bf16[8,64,128]{2,1,0:T(8,128)(2,1)S(1)}, bf16[8,64,128]{2,1,0:T(8,128)(2,1)S(1)}, u32[]{:S(2)}, u32[]{:S(2)}) collective-permute-start(bf16[8,64,128]{2,1,0:T(8,128)(2,1)S(1)} %all_to_all.33.x_ref), channel_id=1, source_target_pairs={{1,0},{0,1},{3,2},{2,3},{5,4},{4,5},{7,6},{6,7},{9,8},{8,9},{11,10... | collective-permute-start | bytes 393224 | tf_op jit(solution)/shard_map/ppermute | solution.py:327
  97.9 1.0 collective-permute-done.9.other_ref
  99.7 19.8 %all_to_all.34.w_ref.tail_ref = bf16[16,17,16,128]{3,2,1,0:T(8,128)(2,1)S(1)} all-to-all(bf16[16,17,16,128]{3,2,1,0:T(8,128)(2,1)S(1)} %shard_map.93), channel_id=1, replica_groups=mesh['y'=4,'z'=8,'x'=4,'c'=2] {'y','x'}, dimensions={0} | all-to-all | bytes 2228224 | tf_op jit(solution)/shard_map/all_to_all | solution.py:434
  119.5 3.1 %shard_map.94 = (bf16[16,128,256]{2,1,0:T(8,128)(2,1)}, f32[128,256]{1,0:T(8,128)}) custom-call(bf16[16,17,16,128]{3,2,1,0:T(8,128)(2,1)S(1)} %all_to_all.34.w_ref.tail_ref, bf16[16,17,16,128]{3,2,1,0:T(8,128)(2,1)S(1)} %all_to_all.34.w_ref.tail_ref, bf16[16,256,128]{2,1,0:T(8,128)(2,1)S(1)} %copy-done.2, bf16[16,128,128]{2,1,0:T(8,128)(2,1)S(1)} %bitcast.12, ...), custom_call_target="tpu_custom_call" | custom-call | tf_op jit(solution)/shard_map/pallas_call | solution.py:436
  (23 shorter events, 4.2 us)
Async XLA Ops:
  0.6 0.8 copy-start.3
  1.5 0.8 copy-start.4
  2.5 10.7 %collective-permute-start.2 = (bf16[3,128,128]{2,1,0:T(8,128)(2,1)S(1)}, bf16[3,128,128]{2,1,0:T(8,128)(2,1)S(1)}, u32[]{:S(2)}, u32[]{:S(2)}) collective-permute-start(bf16[3,128,128]{2,1,0:T(8,128)(2,1)S(1)} %shard_map.87.refs_0_), channel_id=1, source_target_pairs={{6,0},{0,2},{2,4},{4,6},{7,1},{1,3},{3,5},{5,7},{14,8},{8,10},{10,... | collective-permute-start | bytes 294920 | tf_op jit(solution)/shard_map/ppermute | solution.py:327
  4.6 8.6 %collective-permute-start.1 = (bf16[3,128,128]{2,1,0:T(8,128)(2,1)S(1)}, bf16[3,128,128]{2,1,0:T(8,128)(2,1)S(1)}, u32[]{:S(2)}, u32[]{:S(2)}) collective-permute-start(bf16[3,128,128]{2,1,0:T(8,128)(2,1)S(1)} %shard_map.87.refs_0_), channel_id=1, source_target_pairs={{4,0},{6,2},{0,4},{2,6},{5,1},{7,3},{1,5},{3,7},{12,8},{14,10},{8,... | collective-permute-start | bytes 294920 | tf_op jit(solution)/shard_map/ppermute | solution.py:327
  7.1 6.2 %collective-permute-start = (bf16[3,128,128]{2,1,0:T(8,128)(2,1)S(1)}, bf16[3,128,128]{2,1,0:T(8,128)(2,1)S(1)}, u32[]{:S(2)}, u32[]{:S(2)}) collective-permute-start(bf16[3,128,128]{2,1,0:T(8,128)(2,1)S(1)} %shard_map.87.refs_0_), channel_id=1, source_target_pairs={{2,0},{4,2},{6,4},{0,6},{3,1},{5,3},{7,5},{1,7},{10,8},{12,10},{14... | collective-permute-start | bytes 294920 | tf_op jit(solution)/shard_map/ppermute | solution.py:327
  13.3 20.1 %all-to-all-start = ((bf16[16,17,16,128]{3,2,1,0:T(8,128)(2,1)}), bf16[16,17,16,128]{3,2,1,0:T(8,128)(2,1)S(1)}, u32[]{:S(2)}, u32[]{:S(2)}) async-start(bf16[16,17,16,128]{3,2,1,0:T(8,128)(2,1)} %get-tuple-element.25), calls=%async_computation | async-start | bytes 2228224 | tf_op jit(solution)/shard_map/all_to_all | solution.py:374
  17.6 3.0 %collective-permute-start.3 = (bf16[3,128,128]{2,1,0:T(8,128)(2,1)S(1)}, bf16[3,128,128]{2,1,0:T(8,128)(2,1)S(1)}, u32[]{:S(2)}, u32[]{:S(2)}) collective-permute-start(bf16[3,128,128]{2,1,0:T(8,128)(2,1)S(1)} %shard_map.87.refs_0_), channel_id=1, source_target_pairs={{1,0},{0,1},{3,2},{2,3},{5,4},{4,5},{7,6},{6,7},{9,8},{8,9},{11,10... | collective-permute-start | bytes 294920 | tf_op jit(solution)/shard_map/ppermute | solution.py:327
  19.7 1.3 %collective-permute-start.4 = (bf16[3,128,128]{2,1,0:T(8,128)(2,1)S(1)}, bf16[3,128,128]{2,1,0:T(8,128)(2,1)S(1)}, u32[]{:S(2)}, u32[]{:S(2)}) collective-permute-start(bf16[3,128,128]{2,1,0:T(8,128)(2,1)S(1)} %collective-permute-done.refs_1_), channel_id=1, source_target_pairs={{1,0},{0,1},{3,2},{2,3},{5,4},{4,5},{7,6},{6,7},{9,8},{8,9},{11,10... | collective-permute-start | bytes 294920 | tf_op jit(solution)/shard_map/ppermute | solution.py:327
  19.8 1.4 %collective-permute-start.5 = (bf16[3,128,128]{2,1,0:T(8,128)(2,1)S(1)}, bf16[3,128,128]{2,1,0:T(8,128)(2,1)S(1)}, u32[]{:S(2)}, u32[]{:S(2)}) collective-permute-start(bf16[3,128,128]{2,1,0:T(8,128)(2,1)S(1)} %collective-permute-done.1.refs_2_), channel_id=1, source_target_pairs={{1,0},{0,1},{3,2},{2,3},{5,4},{4,5},{7,6},{6,7},{9,8},{8,9},{11,10... | collective-permute-start | bytes 294920 | tf_op jit(solution)/shard_map/ppermute | solution.py:327
  20.2 1.3 %collective-permute-start.6 = (bf16[3,128,128]{2,1,0:T(8,128)(2,1)S(1)}, bf16[3,128,128]{2,1,0:T(8,128)(2,1)S(1)}, u32[]{:S(2)}, u32[]{:S(2)}) collective-permute-start(bf16[3,128,128]{2,1,0:T(8,128)(2,1)S(1)} %collective-permute-done.2.refs_3_), channel_id=1, source_target_pairs={{1,0},{0,1},{3,2},{2,3},{5,4},{4,5},{7,6},{6,7},{9,8},{8,9},{11,10... | collective-permute-start | bytes 294920 | tf_op jit(solution)/shard_map/ppermute | solution.py:327
  34.2 4.4 %collective-permute-start.7 = (bf16[8,64,128]{2,1,0:T(8,128)(2,1)S(1)}, bf16[8,64,128]{2,1,0:T(8,128)(2,1)S(1)}, u32[]{:S(2)}, u32[]{:S(2)}) collective-permute-start(bf16[8,64,128]{2,1,0:T(8,128)(2,1)S(1)} %get-tuple-element.32), channel_id=1, source_target_pairs={{1,0},{0,1},{3,2},{2,3},{5,4},{4,5},{7,6},{6,7},{9,8},{8,9},{11,10... | collective-permute-start | bytes 393224 | tf_op jit(solution)/shard_map/ppermute | solution.py:327
  66.8 5.4 %collective-permute-start.8 = (bf16[8,144,128]{2,1,0:T(8,128)(2,1)S(1)}, bf16[8,144,128]{2,1,0:T(8,128)(2,1)S(1)}, u32[]{:S(2)}, u32[]{:S(2)}) collective-permute-start(bf16[8,144,128]{2,1,0:T(8,128)(2,1)S(1)} %all_to_all.31.ends_ref), channel_id=1, source_target_pairs={{1,0},{0,1},{3,2},{2,3},{5,4},{4,5},{7,6},{6,7},{9,8},{8,9},{11,10... | collective-permute-start | bytes 884744 | tf_op jit(solution)/shard_map/ppermute | solution.py:327
  95.2 3.6 %collective-permute-start.9 = (bf16[8,64,128]{2,1,0:T(8,128)(2,1)S(1)}, bf16[8,64,128]{2,1,0:T(8,128)(2,1)S(1)}, u32[]{:S(2)}, u32[]{:S(2)}) collective-permute-start(bf16[8,64,128]{2,1,0:T(8,128)(2,1)S(1)} %all_to_all.33.x_ref), channel_id=1, source_target_pairs={{1,0},{0,1},{3,2},{2,3},{5,4},{4,5},{7,6},{6,7},{9,8},{8,9},{11,10... | collective-permute-start | bytes 393224 | tf_op jit(solution)/shard_map/ppermute | solution.py:327
  99.6 19.8 %copy-start = (bf16[1,16,128,128]{3,2,1,0:T(8,128)(2,1)S(1)}, bf16[1,16,128,128]{3,2,1,0:T(8,128)(2,1)}, u32[]{:S(2)}) copy-start(bf16[1,16,128,128]{3,2,1,0:T(8,128)(2,1)} %param.8) | copy-start | bytes 1572868
  99.7 19.8 %copy-start.1 = (bf16[1,16,128,128]{3,2,1,0:T(8,128)(2,1)S(1)}, bf16[1,16,128,128]{3,2,1,0:T(8,128)(2,1)}, u32[]{:S(2)}) copy-start(bf16[1,16,128,128]{3,2,1,0:T(8,128)(2,1)} %param.9) | copy-start | bytes 1572868
  99.7 19.8 %copy-start.2 = (bf16[16,256,128]{2,1,0:T(8,128)(2,1)S(1)}, bf16[16,256,128]{2,1,0:T(8,128)(2,1)}, u32[]{:S(2)}) copy-start(bf16[16,256,128]{2,1,0:T(8,128)(2,1)} %get-tuple-element.43.fwd_ref) | copy-start | bytes 3145732

commit v3 on v2

--- a/solution.py
+++ b/solution.py
@@ -12,7 +12,6 @@
 BF16 = jnp.bfloat16
 PLANE_AXES = ("y", "x")
 STEP_SCALE = 2.0**-8
-CHAIN_BLOCK = 4
 COLS = 8
 LEAF_STEP = 4
 
@@ -93,29 +92,40 @@
 
 def transfer_kernel(x_count, x_ref, c_ref, *refs):
     pairs = refs[: 2 * x_count]
-    m_ref, carry_ref, plane_ref = refs[-3:]
+    m_ref, pack_ref, top_ref = refs[-3:]
     count, _, width = m_ref.shape[0:3]
     x, core = x_ref[0], c_ref[0]
     for d in range(x_count):
         for other in range(2):
             place = 2 * lax.rem(x + d, x_count) + jnp.where(other == 0, core, 1 - core)
             m_ref[place] = pairs[other * x_count + d][...]
-    blocks = count // CHAIN_BLOCK
-
-    def scaled(j):
-        return (m_ref[j, 0].astype(F32) + m_ref[j, 1].astype(F32)) * STEP_SCALE
-
-    chains = [-scaled(b * CHAIN_BLOCK) for b in range(blocks)]
-    for k in range(1, CHAIN_BLOCK):
-        for b in range(blocks):
-            chains[b] = -dot_nn(scaled(b * CHAIN_BLOCK + k), chains[b])
-    total = chains[0]
-    for b in range(1, blocks):
-        total = dot_nn(chains[b], total)
-    for b in range(blocks):
-        carry_ref[b, 0], carry_ref[b, 1] = split(chains[b] * (STEP_SCALE**-CHAIN_BLOCK))
-    high, low = split(total)
-    plane_ref[...] = jnp.where(core == 0, high.astype(F32), low.astype(F32)).astype(BF16)
+    half = count // 2
+    runs = []
+    for k in range(count):
+        m = (m_ref[k, 0].astype(F32) + m_ref[k, 1].astype(F32)) * STEP_SCALE
+        runs.append(-m if k % half == 0 else -dot_nn(m, runs[-1]))
+    first = jnp.concatenate(
+        [runs[k] * STEP_SCALE ** (count - 1 - k) for k in range(half)], axis=0
+    )
+    second = jnp.concatenate(
+        [runs[k] * STEP_SCALE ** (count - 1 - k) for k in range(half, count)], axis=0
+    )
+    second = dot_nn(second, runs[half - 1])
+    stack = jnp.concatenate([first, second], axis=0)
+    top = jnp.maximum(jnp.max(jnp.abs(stack)), 1e-30)
+    high, low = split((stack / top).T)
+    gram = lax.dot_general(high, high, (((1,), (1,)), ((), ())), preferred_element_type=F32)
+    cross = lax.dot_general(high, low, (((1,), (1,)), ((), ())), preferred_element_type=F32)
+    pack_ref[0], pack_ref[1] = split(stack[width * (count - 1) :])
+    pack_ref[2] = (gram + (cross + cross.T)).astype(BF16)
+    top_ref[...] = jnp.full(top_ref.shape, top, F32)
+
+
+def order_kernel(z_ref, *refs):
+    out_ref = refs[-1]
+    count = out_ref.shape[0]
+    for d in range(count):
+        out_ref[lax.rem(z_ref[0] // 2 + d, count)] = refs[d][...]
 
 
 def densify_kernel(plane_size, z_ref, c_ref, v_ref, keep_ref, give_ref, code_ref, acc_ref):
@@ -158,92 +168,69 @@
         give_ref[z] = acc_ref[1 - core, per * z : per * (z + 1), :].astype(BF16)
 
 
-def block_solve_kernel(e_ref, m_ref, carry_ref, plane_ref, b_ref, mid_ref, out_ref):
-    count, _, width = m_ref.shape[0:3]
+def block_solve_kernel(e_ref, m_ref, top_ref, b_ref, out_ref):
+    count = m_ref.shape[0]
     reduced = e_ref[0].astype(F32)
     for s in range(1, e_ref.shape[0]):
         reduced = reduced + e_ref[s].astype(F32)
-    bs = []
+    solved = []
     for j in range(count):
         b = rows_nt(reduced[COLS * j : COLS * (j + 1)], m_ref[j, 2])
         b_ref[COLS * j : COLS * (j + 1), :] = b
-        bs.append(b)
-    ends = [bs[0], bs[CHAIN_BLOCK]]
-    for k in range(1, CHAIN_BLOCK):
-        for b in range(2):
-            j = b * CHAIN_BLOCK + k
-            ends[b] = bs[j] - rows_nt(ends[b], m_ref[j, 0], m_ref[j, 1])
-    mid_ref[...] = ends[0]
-    leaving = ends[1] + rows_nt(ends[0], carry_ref[1, 0], carry_ref[1, 1])
-    high, low = split(leaving)
-    ends = jnp.concatenate([high.astype(F32), low.astype(F32)], axis=0).astype(BF16)
+        if j > 0:
+            b = b - rows_nt(solved[-1], m_ref[j, 0], m_ref[j, 1])
+        solved.append(b)
+    back = rows_nn(solved[-1], m_ref[count - 1, 0], m_ref[count - 1, 1])
+    for j in reversed(range(count - 1)):
+        back = rows_nn(solved[j] - back, m_ref[j, 0], m_ref[j, 1])
+    ends = jnp.concatenate([solved[-1], back, top_ref[...]], axis=0)
     for z in range(out_ref.shape[0]):
-        out_ref[z, 0 : 2 * COLS] = ends
-        out_ref[z, 2 * COLS : 2 * COLS + width] = plane_ref[...]
-
-
-def carry_forward_kernel(
-    z_ref, c_ref, ends_ref, other_ref, b_ref, mid_ref, m_ref, carry_ref, s_ref, back_ref, flow_ref, phi_ref
-):
+        out_ref[z] = ends
+
+
+def carry_kernel(z_ref, c_ref, ends_ref, mine_ref, other_ref, b_ref, m_ref, x_ref, pack_ref):
     planes = ends_ref.shape[0]
-    width = m_ref.shape[2]
+    count, _, width = m_ref.shape[0:3]
     core = c_ref[0]
-    for z in range(planes):
-        phi_ref[z, core] = ends_ref[z, 2 * COLS : 2 * COLS + width]
-        phi_ref[z, 1 - core] = other_ref[z, 2 * COLS : 2 * COLS + width]
-    grow = STEP_SCALE ** (-2 * CHAIN_BLOCK)
+    for i in range(planes // 2):
+        pack_ref[2 * i + core] = mine_ref[i]
+        pack_ref[2 * i + 1 - core] = other_ref[i]
+    grow = STEP_SCALE**-count
+    half_grow = STEP_SCALE ** (-count // 2)
     own = z_ref[0]
     state = jnp.zeros((COLS, width), F32)
-    flow = state
-    for z in range(planes - 1):
-        parts = ends_ref[z, 0 : 2 * COLS].astype(F32)
-        leaving = parts[0:COLS] + parts[COLS : 2 * COLS]
+    inflow = state
+    backs = []
+    for z in range(planes):
+        leaving, back, top = (ends_ref[z, COLS * i : COLS * (i + 1)] for i in range(3))
         if z > 0:
-            leaving = leaving + grow * rows_nt(state, phi_ref[z, 0], phi_ref[z, 1])
+            answer = rows_nn(state, pack_ref[z, 2])
+            for _ in range(2):
+                answer = (answer * half_grow) * top * half_grow
+            back = back - answer
+            leaving = leaving + grow * rows_nt(state, pack_ref[z, 0], pack_ref[z, 1])
+        backs.append(back)
         state = leaving
-        flow = jnp.where(own == z + 1, state, flow)
-    running = [flow, mid_ref[...] + rows_nt(flow, carry_ref[0, 0], carry_ref[0, 1])]
-    solved = [[], []]
-    for k in range(CHAIN_BLOCK):
-        for b in range(2):
-            j = b * CHAIN_BLOCK + k
-            running[b] = b_ref[COLS * j : COLS * (j + 1), :] - rows_nt(running[b], m_ref[j, 0], m_ref[j, 1])
-            s_ref[COLS * j : COLS * (j + 1), :] = running[b]
-            solved[b].append(running[b])
-    back = [None, None]
-    for k in reversed(range(CHAIN_BLOCK)):
-        for b in range(2):
-            j = b * CHAIN_BLOCK + k
-            right = solved[b][k] if back[b] is None else solved[b][k] - back[b]
-            back[b] = rows_nn(right, m_ref[j, 0], m_ref[j, 1])
-    flow_ref[...] = back[1]
-    leaving = back[0] + rows_nn(back[1], carry_ref[0, 0], carry_ref[0, 1])
-    for z in range(back_ref.shape[0]):
-        back_ref[z] = leaving
-
-
-def carry_backward_kernel(z_ref, ends_ref, phi_ref, s_ref, flow_ref, m_ref, carry_ref, x_ref):
-    planes = ends_ref.shape[0]
-    count, _, width = m_ref.shape[0:3]
-    grow = STEP_SCALE ** (-2 * CHAIN_BLOCK)
-    own = z_ref[0]
+        if z < planes - 1:
+            inflow = jnp.where(own == z + 1, state, inflow)
     state = jnp.zeros((COLS, width), F32)
-    flow = state
+    running = state
     for z in reversed(range(1, planes)):
-        leaving = ends_ref[z]
+        leaving = backs[z]
         if z < planes - 1:
-            leaving = leaving + grow * rows_nn(state, phi_ref[z, 0], phi_ref[z, 1])
+            leaving = leaving + grow * rows_nn(state, pack_ref[z, 0], pack_ref[z, 1])
         state = leaving
-        flow = jnp.where(own == z - 1, state, flow)
-    running = [flow_ref[...] + rows_nn(flow, carry_ref[1, 0], carry_ref[1, 1]), flow]
+        running = jnp.where(own == z - 1, state, running)
+    solved = []
+    for j in range(count):
+        inflow = b_ref[COLS * j : COLS * (j + 1), :] - rows_nt(inflow, m_ref[j, 0], m_ref[j, 1])
+        solved.append(inflow)
     answers = [None] * count
-    for k in reversed(range(CHAIN_BLOCK)):
-        for b in range(2):
-            j = b * CHAIN_BLOCK + k
-            right = s_ref[COLS * j : COLS * (j + 1), :] - running[b]
-            if k > 0:
-                running[b] = rows_nn(right, m_ref[j, 0], m_ref[j, 1])
-            answers[j] = rows_nn(right, m_ref[j, 2])
+    for j in reversed(range(count)):
+        right = solved[j] - running
+        if j > 0:
+            running = rows_nn(right, m_ref[j, 0], m_ref[j, 1])
+        answers[j] = rows_nn(right, m_ref[j, 2])
     coarse = jnp.concatenate(answers, axis=0).astype(BF16)
     for z in range(x_ref.shape[0]):
         x_ref[z] = coarse
@@ -303,7 +290,7 @@
 SMEM = pl.BlockSpec(memory_space=pltpu.SMEM)
 
 
-def call(kernel, operands, outs, scratch=(), flops=0, after=()):
+def call(kernel, operands, outs, scratch=(), flops=0, after=(), vmem=16):
     moved = sum(a.size * a.dtype.itemsize for a in list(operands) + list(outs))
     if after:
         inner, count = kernel, len(operands)
@@ -317,7 +304,7 @@
         + [pl.BlockSpec(memory_space=pl.ANY) for _ in after],
         out_specs=[pl.BlockSpec(memory_space=pltpu.VMEM) for _ in outs],
         scratch_shapes=list(scratch),
-        compiler_params=pltpu.CompilerParams(vmem_limit_bytes=16 * 2**20),
+        compiler_params=pltpu.CompilerParams(vmem_limit_bytes=vmem * 2**20),
         cost_estimate=pl.CostEstimate(flops=flops, bytes_accessed=moved, transcendentals=0),
     )(*operands, *after)
 
@@ -325,6 +312,19 @@
 def shift(value, axis, by):
     size = lax.axis_size(axis)
     return lax.ppermute(value, axis, [((i + by) % size, i) for i in range(size)])
+
+
+def every_other(value, by):
+    half = lax.axis_size("z") // 2
+    return lax.ppermute(
+        value,
+        ("z", "c"),
+        [
+            (2 * (2 * ((z // 2 + by) % half) + c) + z % 2, 2 * z + c)
+            for z in range(2 * half)
+            for c in range(2)
+        ],
+    )
 
 
 def local(leaf_rhs, leaf_inverse, leaf_update, leaf_target, anc_rhs, anc_inverse, anc_coupling):
@@ -341,7 +341,7 @@
         lax.axis_index(a).astype(jnp.int32).reshape(1) for a in ("y", "z", "x", "c")
     )
 
-    (own_pair,) = call(own_pair_kernel, (anc_inverse, anc_coupling), [sds((3, width, width), BF16)])
+    (own_pair,) = call(own_pair_kernel, (anc_inverse, anc_coupling), [sds((3, width, width), BF16)], vmem=60)
     along = [own_pair] + [shift(own_pair, "x", d) for d in range(1, x_count)]
 
     steps = leaves // LEAF_STEP
@@ -371,18 +371,20 @@
     )(y_index, leaf_target.astype(jnp.int32).reshape(leaves), rhs, inv, upd, anc_rhs[0])
 
     send, *along = lax.optimization_barrier((send, *along))
-    came = lax.all_to_all(send, PLANE_AXES, 0, 0, tiled=True)
+    came = lax.all_to_all(send.reshape(peers, -1, width), PLANE_AXES, 0, 0, tiled=True).reshape(send.shape)
 
     across = [shift(pair, "c", 1) for pair in along]
-    m_blocks, carries, plane_carry = call(
+    m_blocks, pack, top = call(
         functools.partial(transfer_kernel, x_count),
         (x_index, c_index, *along, *across),
         [
             sds((plane_size, 3, width, width), BF16),
-            sds((2, 2, width, width), BF16),
-            sds((width, width), BF16),
-        ],
-    )
+            sds((3, width, width), BF16),
+            sds((COLS, width), F32),
+        ],
+    )
+    packs = [every_other(pack, d) for d in range(planes // 2)]
+    came, *packs = lax.optimization_barrier((came, *packs))
 
     keep, give, codes = call(
         functools.partial(densify_kernel, plane_size),
@@ -393,36 +395,22 @@
             sds((leaves * COLS, peers), F32),
         ],
         scratch=[pltpu.VMEM((2, chain * COLS, width), F32)],
-        after=(plane_carry,),
     )
     dense = (keep + shift(give, "c", 1).astype(F32)).astype(BF16)
     sums = lax.all_to_all(dense, "z", 0, 0, tiled=True)
-    b_rows, middle, ends = call(
+    (own_packs,) = call(order_kernel, (z_index, *packs), [sds((planes // 2, 3, width, width), BF16)])
+    other_packs = shift(own_packs, "c", 1)
+    b_rows, ends = call(
         block_solve_kernel,
-        (sums, m_blocks, carries, plane_carry),
-        [
-            sds((plane_size * COLS, width), F32),
-            sds((COLS, width), F32),
-            sds((planes, 2 * COLS + width, width), BF16),
-        ],
+        (sums, m_blocks, top),
+        [sds((plane_size * COLS, width), F32), sds((planes, 3 * COLS, width), F32)],
     )
     all_ends = lax.all_to_all(ends, "z", 0, 0, tiled=True)
-    other_ends = shift(all_ends, "c", 1)
-    s_rows, back, flow, phis = call(
-        carry_forward_kernel,
-        (z_index, c_index, all_ends, other_ends, b_rows, middle, m_blocks, carries),
-        [
-            sds((plane_size * COLS, width), F32),
-            sds((planes, COLS, width), F32),
-            sds((COLS, width), F32),
-            sds((planes, 2, width, width), BF16),
-        ],
-    )
-    all_back = lax.all_to_all(back, "z", 0, 0, tiled=True)
     (x_rows,) = call(
-        carry_backward_kernel,
-        (z_index, all_back, phis, s_rows, flow, m_blocks, carries),
+        carry_kernel,
+        (z_index, c_index, all_ends, own_packs, other_packs, b_rows, m_blocks),
         [sds((planes, plane_size * COLS, width), BF16)],
+        scratch=[pltpu.VMEM((planes, 3, width, width), BF16)],
     )
     all_x = lax.all_to_all(x_rows, "z", 0, 0, tiled=True)
     other_x = shift(all_x, "c", 1)
@@ -431,7 +419,8 @@
         (z_index, c_index, all_x, other_x, codes),
         [sds((peers, 2 * pairs + 1, 2 * COLS, width), BF16)],
     )
-    answers = lax.all_to_all(answer, PLANE_AXES, 0, 0, tiled=True)
+    answers = lax.all_to_all(answer.reshape(peers, -1, width), PLANE_AXES, 0, 0, tiled=True)
+    answers = answers.reshape(answer.shape)
 
     leaf_solution, anc_solution = pl.pallas_call(
         leaf_backward_kernel,

time: 123 us -> 119 us (0.967)
  blocking collectives: 67 us -> 34.3 us
  starting transfers between devices: 23 us -> 39.7 us
  waiting for transfers between devices: 15.3 us -> 22.9 us
  Pallas kernels: 14.9 us -> 19.8 us
  local copies, waits for them, and re-layouts: 1.69 us -> 0.03 us
    all_to_all x4 -> x1, blocking collectives: 56.6 us -> 23.9 us  [local(): lax.all_to_all(answer.reshape(peers, -1, width), PLANE_AXES, 0, 0, tiled=...]
    ppermute x0 -> x4, starting transfers between devices: none -> 13.3 us  [every_other(): lax.ppermute(value, ('z', 'c'), [(2 * (2 * ((z // 2 + by) % half) + c) +...]
    all_to_all x1 -> x3, starting transfers between devices: 4.34 us -> 12.9 us  [the longest x1 4.71 us: local(): sums = lax.all_to_all(dense, 'z', 0, 0, tiled=True)]
    ppermute x10, starting transfers between devices: 18.7 us -> 13.5 us  [shift(): lax.ppermute(value, axis, [((i + by) % size, i) for i in range(size)])]
    ppermute x0 -> x4, waiting for transfers between devices: none -> 4.97 us  [every_other(): lax.ppermute(value, ('z', 'c'), [(2 * (2 * ((z // 2 + by) % half) + c) +...]
    pallas_call x7, Pallas kernels: 6.75 us -> 11.7 us  [call(): pl.pallas_call(kernel, out_shape=outs, in_specs=[SMEM if a.dtype == jnp.i...]
    all_to_all x1 -> x3, waiting for transfers between devices: 10.9 us -> 14.4 us  [the longest x1 7.3 us: local(): all_ends = lax.all_to_all(ends, 'z', 0, 0, tiled=True)]
    unnamed x10 -> x8, local copies, waits for them, and re-layouts: 1.69 us -> 0.03 us
  transfers between devices with their start and end apart: 11 -> 17, of which waited for: 8 -> 11; matrix products, arithmetic and copies ran while one was open for 0% -> 0% of each run, Pallas kernels for 5% -> 8%
where the time goes in v3:
time: 119 us; the launch traced here: 118 us
  starting transfers between devices  39.7 us (33%)
  blocking collectives  34.3 us (29%)
  waiting for transfers between devices  22.9 us (19%)
  Pallas kernels  19.8 us (17%)
    all_to_all x1, blocking collectives, local(): lax.all_to_all(answer.reshape(peers, -1, width), PLANE_AXES, 0, 0, tiled=...  23.9 us
    ppermute x10, starting transfers between devices, shift(): lax.ppermute(value, axis, [((i + by) % size, i) for i in range(size)])  13.5 us
    ppermute x4, starting transfers between devices, every_other(): lax.ppermute(value, ('z', 'c'), [(2 * (2 * ((z // 2 + by) % half) + c) +...  13.3 us
    pallas_call x7, Pallas kernels, call(): pl.pallas_call(kernel, out_shape=outs, in_specs=[SMEM if a.dtype == jnp.i...  11.7 us
    all_to_all x1, blocking collectives, local(): all_x = lax.all_to_all(x_rows, 'z', 0, 0, tiled=True)  10.4 us
    all_to_all x1, waiting for transfers between devices, local(): all_ends = lax.all_to_all(ends, 'z', 0, 0, tiled=True)  7.3 us
    all_to_all x1, waiting for transfers between devices, local(): sums = lax.all_to_all(dense, 'z', 0, 0, tiled=True)  7.13 us
    pallas_call x1, Pallas kernels, local(): pl.pallas_call(leaf_forward_kernel, grid=(steps,), out_shape=[sds((leaves...  5 us
  transfers between devices with their start and end apart: 17, of which 11 were waited for; matrix products, arithmetic and copies ran while one was open for 0% of the time, Pallas kernels for 8%

profile of v3, /device:TPU:1, one launch (start us, length us, event | category | flops | bytes accessed | tf_op | source)
XLA Modules:
  0.0 118.2 jit_solution(17912776554716388884)
XLA Ops:
  0.6 1.7 %shard_map.87.refs_0_ = bf16[3,128,128]{2,1,0:T(8,128)(2,1)} custom-call(f32[1,128,128]{2,1,0:T(8,128)} %inv_ref.1, f32[1,128,128]{2,1,0:T(8,128)} %cpl_ref.1), custom_call_target="tpu_custom_call" | custom-call | bytes 229376 | tf_op jit(solution)/shard_map/pallas_call | solution.py:298
  2.3 2.0 %collective-permute-start.2 = (bf16[3,128,128]{2,1,0:T(8,128)(2,1)}, bf16[3,128,128]{2,1,0:T(8,128)(2,1)S(1)}, u32[]{:S(2)}, u32[]{:S(2)}) collective-permute-start(bf16[3,128,128]{2,1,0:T(8,128)(2,1)} %shard_map.87.refs_0_), channel_id=1, source_target_pairs={{6,0},{0,2},{2,4},{4,6},{7,1},{1,3},{3,5},{5,7},{14,8},{8,10},{10,... | collective-permute-start | bytes 294920 | tf_op jit(solution)/shard_map/ppermute | solution.py:314
  4.4 2.5 %collective-permute-start.1 = (bf16[3,128,128]{2,1,0:T(8,128)(2,1)}, bf16[3,128,128]{2,1,0:T(8,128)(2,1)S(1)}, u32[]{:S(2)}, u32[]{:S(2)}) collective-permute-start(bf16[3,128,128]{2,1,0:T(8,128)(2,1)} %shard_map.87.refs_0_), channel_id=1, source_target_pairs={{4,0},{6,2},{0,4},{2,6},{5,1},{7,3},{1,5},{3,7},{12,8},{14,10},{8,... | collective-permute-start | bytes 294920 | tf_op jit(solution)/shard_map/ppermute | solution.py:314
  8.0 5.0 %shard_map.86 = (bf16[16,256,128]{2,1,0:T(8,128)(2,1)}, bf16[16,17,16,128]{3,2,1,0:T(8,128)(2,1)}) custom-call(s32[1]{0:T(128)} %bitcast.2.y_ref, s32[16]{0:T(128)} %bitcast.26, bf16[16,128,256]{2,1,0:T(8,128)(2,1)} %bitcast.24, bf16[16,128,128]{2,1,0:T(8,128)(2,1)} %bitcast.19, bf16[16,128,128]{2,1,0:T(8,128)(2,1)} %bitcast.21, f32[128,256]{1,0:T(8,128)} %bitcast.25), custom_call_target="tpu_custom_call" | custom-call | tf_op jit(solution)/shard_map/pallas_call | solution.py:349
  13.0 4.6 %all-to-all-start = ((bf16[16,272,128]{2,1,0:T(8,128)(2,1)}), bf16[16,272,128]{2,1,0:T(8,128)(2,1)S(1)}, u32[]{:S(2)}, u32[]{:S(2)}) async-start(bf16[16,272,128]{2,1,0:T(8,128)(2,1)} %bitcast.23), calls=%async_computation | async-start | bytes 2228224 | tf_op jit(solution)/shard_map/all_to_all | solution.py:374
  17.7 2.1 %collective-permute-start.3 = (bf16[3,128,128]{2,1,0:T(8,128)(2,1)S(1)}, bf16[3,128,128]{2,1,0:T(8,128)(2,1)S(1)}, u32[]{:S(2)}, u32[]{:S(2)}) collective-permute-start(bf16[3,128,128]{2,1,0:T(8,128)(2,1)S(1)} %copy-done.3), channel_id=1, source_target_pairs={{1,0},{0,1},{3,2},{2,3},{5,4},{4,5},{7,6},{6,7},{9,8},{8,9},{11,10... | collective-permute-start | bytes 294920 | tf_op jit(solution)/shard_map/ppermute | solution.py:314
  21.6 2.1 %shard_map.88 = (bf16[8,3,128,128]{3,2,1,0:T(8,128)(2,1)S(1)}, bf16[3,128,128]{2,1,0:T(8,128)(2,1)S(1)}, f32[8,128]{1,0:T(8,128)S(1)}) custom-call(s32[1]{0:T(128)} %bitcast.10.x_ref, s32[1]{0:T(128)} %bitcast.1.c_ref, bf16[3,128,128]{2,1,0:T(8,128)(2,1)S(1)} %copy-done.3, bf16[3,128,128]{2,1,0:T(8,128)(2,1)S(1)} %collective-permute-done.refs_1_, ...), custom_call_target="tpu_custom_call" | custom-call | bytes 1675272 | tf_op jit(solution)/shard_map/pallas_call | solution.py:298
  23.7 4.5 %collective-permute-start.10 = (bf16[3,128,128]{2,1,0:T(8,128)(2,1)S(1)}, bf16[3,128,128]{2,1,0:T(8,128)(2,1)S(1)}, u32[]{:S(2)}, u32[]{:S(2)}) collective-permute-start(bf16[3,128,128]{2,1,0:T(8,128)(2,1)S(1)} %get-tuple-element.30), channel_id=1, source_target_pairs={{48,0},{56,1},{49,8},{57,9},{0,16},{8,17},{1,24},{9,25},{16,32},{2... | collective-permute-start | bytes 294920 | tf_op jit(solution)/shard_map/ppermute | solution.py:319
  28.2 3.1 %collective-permute-start.9 = (bf16[3,128,128]{2,1,0:T(8,128)(2,1)S(1)}, bf16[3,128,128]{2,1,0:T(8,128)(2,1)S(1)}, u32[]{:S(2)}, u32[]{:S(2)}) collective-permute-start(bf16[3,128,128]{2,1,0:T(8,128)(2,1)S(1)} %get-tuple-element.30), channel_id=1, source_target_pairs={{32,0},{40,1},{33,8},{41,9},{48,16},{56,17},{49,24},{57,25},{0,32}... | collective-permute-start | bytes 294920 | tf_op jit(solution)/shard_map/ppermute | solution.py:319
  31.3 2.9 %collective-permute-start.8 = (bf16[3,128,128]{2,1,0:T(8,128)(2,1)S(1)}, bf16[3,128,128]{2,1,0:T(8,128)(2,1)S(1)}, u32[]{:S(2)}, u32[]{:S(2)}) collective-permute-start(bf16[3,128,128]{2,1,0:T(8,128)(2,1)S(1)} %get-tuple-element.30), channel_id=1, source_target_pairs={{16,0},{24,1},{17,8},{25,9},{32,16},{40,17},{33,24},{41,25},{48,32... | collective-permute-start | bytes 294920 | tf_op jit(solution)/shard_map/ppermute | solution.py:319
  34.1 2.9 %collective-permute-start.7 = (bf16[3,128,128]{2,1,0:T(8,128)(2,1)S(1)}, bf16[3,128,128]{2,1,0:T(8,128)(2,1)S(1)}, u32[]{:S(2)}, u32[]{:S(2)}) collective-permute-start(bf16[3,128,128]{2,1,0:T(8,128)(2,1)S(1)} %get-tuple-element.30), channel_id=1, source_target_pairs={{0,0},{8,1},{1,8},{9,9},{16,16},{24,17},{17,24},{25,25},{32,32},{4... | collective-permute-start | bytes 294920 | tf_op jit(solution)/shard_map/ppermute | solution.py:319
  37.0 1.7 %collective-permute-done.9.refs_2_ = bf16[3,128,128]{2,1,0:T(8,128)(2,1)S(1)} collective-permute-done((bf16[3,128,128]{2,1,0:T(8,128)(2,1)S(1)}, bf16[3,128,128]{2,1,0:T(8,128)(2,1)S(1)}, u32[]{:S(2)}, u32[]{:S(2)}) %collective-permute-start.9) | collective-permute-done | bytes 98336 | tf_op jit(solution)/shard_map/ppermute | solution.py:319
  39.0 3.0 %collective-permute-done.7.refs_0_ = bf16[3,128,128]{2,1,0:T(8,128)(2,1)S(1)} collective-permute-done((bf16[3,128,128]{2,1,0:T(8,128)(2,1)S(1)}, bf16[3,128,128]{2,1,0:T(8,128)(2,1)S(1)}, u32[]{:S(2)}, u32[]{:S(2)}) %collective-permute-start.7) | collective-permute-done | bytes 98336 | tf_op jit(solution)/shard_map/ppermute | solution.py:319
  42.9 1.3 %collective-permute-done.11 = bf16[8,64,128]{2,1,0:T(8,128)(2,1)S(1)} collective-permute-done((bf16[8,64,128]{2,1,0:T(8,128)(2,1)S(1)}, bf16[8,64,128]{2,1,0:T(8,128)(2,1)S(1)}, u32[]{:S(2)}, u32[]{:S(2)}) %collective-permute-start.11) | collective-permute-done | bytes 131104 | tf_op jit(solution)/shard_map/ppermute | solution.py:314
  44.9 4.7 %all-to-all-start.1 = ((bf16[8,64,128]{2,1,0:T(8,128)(2,1)}), bf16[8,64,128]{2,1,0:T(8,128)(2,1)S(1)}, u32[]{:S(2)}, u32[]{:S(2)}) async-start(bf16[8,64,128]{2,1,0:T(8,128)(2,1)} %add_convert_fusion), calls=%async_computation.1 | async-start | bytes 262144 | tf_op jit(solution)/shard_map/all_to_all | solution.py:400
  50.4 7.1 %all-to-all-done.1.e_ref = bf16[8,64,128]{2,1,0:T(8,128)(2,1)S(1)} async-done(((bf16[8,64,128]{2,1,0:T(8,128)(2,1)}), bf16[8,64,128]{2,1,0:T(8,128)(2,1)S(1)}, u32[]{:S(2)}, u32[]{:S(2)}) %all-to-all-start.1) | async-done | bytes 131104 | tf_op jit(solution)/shard_map/all_to_all | solution.py:400
  57.5 2.6 %shard_map.90 = (f32[64,128]{1,0:T(8,128)S(1)}, f32[8,24,128]{2,1,0:T(8,128)}) custom-call(bf16[8,64,128]{2,1,0:T(8,128)(2,1)S(1)} %all-to-all-done.1.e_ref, bf16[8,3,128,128]{3,2,1,0:T(8,128)(2,1)S(1)} %get-tuple-element.34.m_ref, f32[8,128]{1,0:T(8,128)S(1)} %get-tuple-element.35.top_ref), custom_call_target="tpu_custom_call" | custom-call | bytes 1052672 | tf_op jit(solution)/shard_map/pallas_call | solution.py:298
  60.1 3.5 %all-to-all-start.2 = ((f32[8,24,128]{2,1,0:T(8,128)}), f32[8,24,128]{2,1,0:T(8,128)S(1)}, u32[]{:S(2)}, u32[]{:S(2)}) async-start(f32[8,24,128]{2,1,0:T(8,128)} %get-tuple-element.36), calls=%async_computation.2 | async-start | bytes 196608 | tf_op jit(solution)/shard_map/all_to_all | solution.py:408
  63.7 7.3 %all-to-all-done.2.ends_ref = f32[8,24,128]{2,1,0:T(8,128)S(1)} async-done(((f32[8,24,128]{2,1,0:T(8,128)}), f32[8,24,128]{2,1,0:T(8,128)S(1)}, u32[]{:S(2)}, u32[]{:S(2)}) %all-to-all-start.2) | async-done | bytes 98336 | tf_op jit(solution)/shard_map/all_to_all | solution.py:408
  71.0 3.7 %shard_map.92 = bf16[8,64,128]{2,1,0:T(8,128)(2,1)S(1)} custom-call(s32[1]{0:T(128)} %bitcast.z_ref, s32[1]{0:T(128)} %bitcast.1.c_ref, f32[8,24,128]{2,1,0:T(8,128)S(1)} %all-to-all-done.2.ends_ref, bf16[4,3,128,128]{3,2,1,0:T(8,128)(2,1)S(1)} %shard_map.91.mine_ref, bf16[4,3,128,128]{3,2,1,0:T(8,128)(2,1)S(1)} %collective-permute-done.12.other_ref, ...), custom_call_target="tpu_custom_call" | custom-call | bytes 1835016 | tf_op jit(solution)/shard_map/pallas_call | solution.py:298
  74.7 10.4 %all_to_all.25.x_ref = bf16[8,64,128]{2,1,0:T(8,128)(2,1)S(1)} all-to-all(bf16[8,64,128]{2,1,0:T(8,128)(2,1)S(1)} %shard_map.92), channel_id=1, replica_groups=mesh['y'=4,'z'=8,'x'=4,'c'=2] {'z'}, dimensions={0} | all-to-all | bytes 262144 | tf_op jit(solution)/shard_map/all_to_all | solution.py:415
  85.1 4.3 %collective-permute-start.13 = (bf16[8,64,128]{2,1,0:T(8,128)(2,1)S(1)}, bf16[8,64,128]{2,1,0:T(8,128)(2,1)S(1)}, u32[]{:S(2)}, u32[]{:S(2)}) collective-permute-start(bf16[8,64,128]{2,1,0:T(8,128)(2,1)S(1)} %all_to_all.25.x_ref), channel_id=1, source_target_pairs={{1,0},{0,1},{3,2},{2,3},{5,4},{4,5},{7,6},{6,7},{9,8},{8,9},{11,10... | collective-permute-start | bytes 393224 | tf_op jit(solution)/shard_map/ppermute | solution.py:314
  91.2 23.9 %all_to_all.26 = bf16[16,272,128]{2,1,0:T(8,128)(2,1)S(1)} all-to-all(bf16[16,272,128]{2,1,0:T(8,128)(2,1)S(1)} %bitcast.18), channel_id=1, replica_groups=mesh['y'=4,'z'=8,'x'=4,'c'=2] {'y','x'}, dimensions={0} | all-to-all | bytes 2228224 | tf_op jit(solution)/shard_map/all_to_all | solution.py:422
  115.2 3.1 %shard_map.94 = (bf16[16,128,256]{2,1,0:T(8,128)(2,1)}, f32[128,256]{1,0:T(8,128)}) custom-call(bf16[16,17,16,128]{3,2,1,0:T(8,128)(2,1)S(1)} %bitcast.15, bf16[16,17,16,128]{3,2,1,0:T(8,128)(2,1)S(1)} %bitcast.16, bf16[16,256,128]{2,1,0:T(8,128)(2,1)S(1)} %copy-done.2, bf16[16,128,128]{2,1,0:T(8,128)(2,1)S(1)} %bitcast.20, bf16[16,128,128]{2,1,0:T(8,128)(2,1)S(1)} %bitcast.22), custom_call_target="tpu_custom_call" | custom-call | tf_op jit(solution)/shard_map/pallas_call | solution.py:425
  (30 shorter events, 7.3 us)
Async XLA Ops:
  2.3 10.6 %collective-permute-start.2 = (bf16[3,128,128]{2,1,0:T(8,128)(2,1)}, bf16[3,128,128]{2,1,0:T(8,128)(2,1)S(1)}, u32[]{:S(2)}, u32[]{:S(2)}) collective-permute-start(bf16[3,128,128]{2,1,0:T(8,128)(2,1)} %shard_map.87.refs_0_), channel_id=1, source_target_pairs={{6,0},{0,2},{2,4},{4,6},{7,1},{1,3},{3,5},{5,7},{14,8},{8,10},{10,... | collective-permute-start | bytes 294920 | tf_op jit(solution)/shard_map/ppermute | solution.py:314
  4.4 8.6 %collective-permute-start.1 = (bf16[3,128,128]{2,1,0:T(8,128)(2,1)}, bf16[3,128,128]{2,1,0:T(8,128)(2,1)S(1)}, u32[]{:S(2)}, u32[]{:S(2)}) collective-permute-start(bf16[3,128,128]{2,1,0:T(8,128)(2,1)} %shard_map.87.refs_0_), channel_id=1, source_target_pairs={{4,0},{6,2},{0,4},{2,6},{5,1},{7,3},{1,5},{3,7},{12,8},{14,10},{8,... | collective-permute-start | bytes 294920 | tf_op jit(solution)/shard_map/ppermute | solution.py:314
  6.8 6.2 %collective-permute-start = (bf16[3,128,128]{2,1,0:T(8,128)(2,1)}, bf16[3,128,128]{2,1,0:T(8,128)(2,1)S(1)}, u32[]{:S(2)}, u32[]{:S(2)}) collective-permute-start(bf16[3,128,128]{2,1,0:T(8,128)(2,1)} %shard_map.87.refs_0_), channel_id=1, source_target_pairs={{2,0},{4,2},{6,4},{0,6},{3,1},{5,3},{7,5},{1,7},{10,8},{12,10},{14... | collective-permute-start | bytes 294920 | tf_op jit(solution)/shard_map/ppermute | solution.py:314
  13.0 4.6 %copy-start.3 = (bf16[3,128,128]{2,1,0:T(8,128)(2,1)S(1)}, bf16[3,128,128]{2,1,0:T(8,128)(2,1)}, u32[]{:S(2)}) copy-start(bf16[3,128,128]{2,1,0:T(8,128)(2,1)} %shard_map.87.refs_0_) | copy-start | bytes 294916
  13.0 29.0 %all-to-all-start = ((bf16[16,272,128]{2,1,0:T(8,128)(2,1)}), bf16[16,272,128]{2,1,0:T(8,128)(2,1)S(1)}, u32[]{:S(2)}, u32[]{:S(2)}) async-start(bf16[16,272,128]{2,1,0:T(8,128)(2,1)} %bitcast.23), calls=%async_computation | async-start | bytes 2228224 | tf_op jit(solution)/shard_map/all_to_all | solution.py:374
  17.7 3.1 %collective-permute-start.3 = (bf16[3,128,128]{2,1,0:T(8,128)(2,1)S(1)}, bf16[3,128,128]{2,1,0:T(8,128)(2,1)S(1)}, u32[]{:S(2)}, u32[]{:S(2)}) collective-permute-start(bf16[3,128,128]{2,1,0:T(8,128)(2,1)S(1)} %copy-done.3), channel_id=1, source_target_pairs={{1,0},{0,1},{3,2},{2,3},{5,4},{4,5},{7,6},{6,7},{9,8},{8,9},{11,10... | collective-permute-start | bytes 294920 | tf_op jit(solution)/shard_map/ppermute | solution.py:314
  19.8 1.3 %collective-permute-start.4 = (bf16[3,128,128]{2,1,0:T(8,128)(2,1)S(1)}, bf16[3,128,128]{2,1,0:T(8,128)(2,1)S(1)}, u32[]{:S(2)}, u32[]{:S(2)}) collective-permute-start(bf16[3,128,128]{2,1,0:T(8,128)(2,1)S(1)} %collective-permute-done.refs_1_), channel_id=1, source_target_pairs={{1,0},{0,1},{3,2},{2,3},{5,4},{4,5},{7,6},{6,7},{9,8},{8,9},{11,10... | collective-permute-start | bytes 294920 | tf_op jit(solution)/shard_map/ppermute | solution.py:314
  19.9 1.4 %collective-permute-start.5 = (bf16[3,128,128]{2,1,0:T(8,128)(2,1)S(1)}, bf16[3,128,128]{2,1,0:T(8,128)(2,1)S(1)}, u32[]{:S(2)}, u32[]{:S(2)}) collective-permute-start(bf16[3,128,128]{2,1,0:T(8,128)(2,1)S(1)} %collective-permute-done.1.refs_2_), channel_id=1, source_target_pairs={{1,0},{0,1},{3,2},{2,3},{5,4},{4,5},{7,6},{6,7},{9,8},{8,9},{11,10... | collective-permute-start | bytes 294920 | tf_op jit(solution)/shard_map/ppermute | solution.py:314
  20.3 1.3 %collective-permute-start.6 = (bf16[3,128,128]{2,1,0:T(8,128)(2,1)S(1)}, bf16[3,128,128]{2,1,0:T(8,128)(2,1)S(1)}, u32[]{:S(2)}, u32[]{:S(2)}) collective-permute-start(bf16[3,128,128]{2,1,0:T(8,128)(2,1)S(1)} %collective-permute-done.2.refs_3_), channel_id=1, source_target_pairs={{1,0},{0,1},{3,2},{2,3},{5,4},{4,5},{7,6},{6,7},{9,8},{8,9},{11,10... | collective-permute-start | bytes 294920 | tf_op jit(solution)/shard_map/ppermute | solution.py:314
  23.7 13.3 %collective-permute-start.10 = (bf16[3,128,128]{2,1,0:T(8,128)(2,1)S(1)}, bf16[3,128,128]{2,1,0:T(8,128)(2,1)S(1)}, u32[]{:S(2)}, u32[]{:S(2)}) collective-permute-start(bf16[3,128,128]{2,1,0:T(8,128)(2,1)S(1)} %get-tuple-element.30), channel_id=1, source_target_pairs={{48,0},{56,1},{49,8},{57,9},{0,16},{8,17},{1,24},{9,25},{16,32},{2... | collective-permute-start | bytes 294920 | tf_op jit(solution)/shard_map/ppermute | solution.py:319
  28.2 10.6 %collective-permute-start.9 = (bf16[3,128,128]{2,1,0:T(8,128)(2,1)S(1)}, bf16[3,128,128]{2,1,0:T(8,128)(2,1)S(1)}, u32[]{:S(2)}, u32[]{:S(2)}) collective-permute-start(bf16[3,128,128]{2,1,0:T(8,128)(2,1)S(1)} %get-tuple-element.30), channel_id=1, source_target_pairs={{32,0},{40,1},{33,8},{41,9},{48,16},{56,17},{49,24},{57,25},{0,32}... | collective-permute-start | bytes 294920 | tf_op jit(solution)/shard_map/ppermute | solution.py:319
  31.3 7.7 %collective-permute-start.8 = (bf16[3,128,128]{2,1,0:T(8,128)(2,1)S(1)}, bf16[3,128,128]{2,1,0:T(8,128)(2,1)S(1)}, u32[]{:S(2)}, u32[]{:S(2)}) collective-permute-start(bf16[3,128,128]{2,1,0:T(8,128)(2,1)S(1)} %get-tuple-element.30), channel_id=1, source_target_pairs={{16,0},{24,1},{17,8},{25,9},{32,16},{40,17},{33,24},{41,25},{48,32... | collective-permute-start | bytes 294920 | tf_op jit(solution)/shard_map/ppermute | solution.py:319
  34.1 7.9 %collective-permute-start.7 = (bf16[3,128,128]{2,1,0:T(8,128)(2,1)S(1)}, bf16[3,128,128]{2,1,0:T(8,128)(2,1)S(1)}, u32[]{:S(2)}, u32[]{:S(2)}) collective-permute-start(bf16[3,128,128]{2,1,0:T(8,128)(2,1)S(1)} %get-tuple-element.30), channel_id=1, source_target_pairs={{0,0},{8,1},{1,8},{9,9},{16,16},{24,17},{17,24},{25,25},{32,32},{4... | collective-permute-start | bytes 294920 | tf_op jit(solution)/shard_map/ppermute | solution.py:319
  42.8 1.4 %collective-permute-start.11 = (bf16[8,64,128]{2,1,0:T(8,128)(2,1)S(1)}, bf16[8,64,128]{2,1,0:T(8,128)(2,1)S(1)}, u32[]{:S(2)}, u32[]{:S(2)}) collective-permute-start(bf16[8,64,128]{2,1,0:T(8,128)(2,1)S(1)} %get-tuple-element.33), channel_id=1, source_target_pairs={{1,0},{0,1},{3,2},{2,3},{5,4},{4,5},{7,6},{6,7},{9,8},{8,9},{11,10... | collective-permute-start | bytes 393224 | tf_op jit(solution)/shard_map/ppermute | solution.py:314
  44.9 12.6 %all-to-all-start.1 = ((bf16[8,64,128]{2,1,0:T(8,128)(2,1)}), bf16[8,64,128]{2,1,0:T(8,128)(2,1)S(1)}, u32[]{:S(2)}, u32[]{:S(2)}) async-start(bf16[8,64,128]{2,1,0:T(8,128)(2,1)} %add_convert_fusion), calls=%async_computation.1 | async-start | bytes 262144 | tf_op jit(solution)/shard_map/all_to_all | solution.py:400
  49.7 14.0 %collective-permute-start.12 = (bf16[4,3,128,128]{3,2,1,0:T(8,128)(2,1)S(1)}, bf16[4,3,128,128]{3,2,1,0:T(8,128)(2,1)S(1)}, u32[]{:S(2)}, u32[]{:S(2)}) collective-permute-start(bf16[4,3,128,128]{3,2,1,0:T(8,128)(2,1)S(1)} %shard_map.91.mine_ref), channel_id=1, source_target_pairs={{1,0},{0,1},{3,2},{2,3},{5,4},{4,5},{7,6},{6,7},{9,8},{8,9},{11,10... | collective-permute-start | bytes 1179656 | tf_op jit(solution)/shard_map/ppermute | solution.py:314
  60.1 10.9 %all-to-all-start.2 = ((f32[8,24,128]{2,1,0:T(8,128)}), f32[8,24,128]{2,1,0:T(8,128)S(1)}, u32[]{:S(2)}, u32[]{:S(2)}) async-start(f32[8,24,128]{2,1,0:T(8,128)} %get-tuple-element.36), calls=%async_computation.2 | async-start | bytes 196608 | tf_op jit(solution)/shard_map/all_to_all | solution.py:408
  85.1 5.3 %collective-permute-start.13 = (bf16[8,64,128]{2,1,0:T(8,128)(2,1)S(1)}, bf16[8,64,128]{2,1,0:T(8,128)(2,1)S(1)}, u32[]{:S(2)}, u32[]{:S(2)}) collective-permute-start(bf16[8,64,128]{2,1,0:T(8,128)(2,1)S(1)} %all_to_all.25.x_ref), channel_id=1, source_target_pairs={{1,0},{0,1},{3,2},{2,3},{5,4},{4,5},{7,6},{6,7},{9,8},{8,9},{11,10... | collective-permute-start | bytes 393224 | tf_op jit(solution)/shard_map/ppermute | solution.py:314
  91.2 24.0 %copy-start = (bf16[1,16,128,128]{3,2,1,0:T(8,128)(2,1)S(1)}, bf16[1,16,128,128]{3,2,1,0:T(8,128)(2,1)}, u32[]{:S(2)}) copy-start(bf16[1,16,128,128]{3,2,1,0:T(8,128)(2,1)} %param.8) | copy-start | bytes 1572868
  91.2 23.9 %copy-start.1 = (bf16[1,16,128,128]{3,2,1,0:T(8,128)(2,1)S(1)}, bf16[1,16,128,128]{3,2,1,0:T(8,128)(2,1)}, u32[]{:S(2)}) copy-start(bf16[1,16,128,128]{3,2,1,0:T(8,128)(2,1)} %param.9) | copy-start | bytes 1572868
  91.2 23.9 %copy-start.2 = (bf16[16,256,128]{2,1,0:T(8,128)(2,1)S(1)}, bf16[16,256,128]{2,1,0:T(8,128)(2,1)}, u32[]{:S(2)}) copy-start(bf16[16,256,128]{2,1,0:T(8,128)(2,1)} %get-tuple-element.43.fwd_ref) | copy-start | bytes 3145732

commit v4 on v3

--- a/solution.py
+++ b/solution.py
@@ -11,9 +11,10 @@
 F32 = jnp.float32
 BF16 = jnp.bfloat16
 PLANE_AXES = ("y", "x")
+CORE_AXES = ("y", "x", "c")
 STEP_SCALE = 2.0**-8
 COLS = 8
-LEAF_STEP = 4
+LEAF_STEP = 8
 
 
 def dot_nn(a, b):
@@ -48,11 +49,9 @@
 
 
 def leaf_forward_kernel(y_ref, tgt_ref, rhs_ref, inv_ref, upd_ref, anc_ref, fwd_ref, send_ref):
-    step = pl.program_id(0)
     rhs_count, width = fwd_ref.shape[1:]
-    peers = send_ref.shape[0]
-    tiles = send_ref.shape[1]
-    for pair in range(LEAF_STEP // 2):
+    peers, tiles = send_ref.shape[0:2]
+    for pair in range(tiles - 1):
         parts = []
         for k in range(2):
             leaf = 2 * pair + k
@@ -63,25 +62,18 @@
             update = lax.dot_general(
                 forward, upd_ref[leaf], (((1,), (1,)), ((), ())), preferred_element_type=F32
             )
-            parts.append(update.reshape(peers, 2 * COLS, width))
-        for half in range(2):
-            rows = jnp.concatenate([p[:, half * COLS : (half + 1) * COLS, :] for p in parts], axis=1)
-            send_ref[:, 2 * (step * (LEAF_STEP // 2) + pair) + half] = rows.astype(BF16)
-
-    @pl.when(step == 0)
-    def _():
-        rows = anc_ref[...].T.reshape(peers, 2 * COLS, width)
-        high = rows.astype(BF16).astype(F32)
-        layer = y_ref[0]
-        mine = jnp.where(layer == 0, high, jnp.where(layer == 2, rows - high, jnp.zeros_like(rows)))
-        over = jnp.where(layer == 1, high, jnp.where(layer == 3, rows - high, jnp.zeros_like(rows)))
-        mine = mine[:, 0:COLS] + over[:, COLS : 2 * COLS]
-        leaf = lax.broadcasted_iota(jnp.int32, (COLS, width), 1) // COLS
-        names = jnp.zeros((COLS, width), F32)
-        for k in range(tgt_ref.shape[0]):
-            names = jnp.where(leaf == k, tgt_ref[k].astype(F32), names)
-        names = jnp.broadcast_to(names[None], (peers, COLS, width))
-        send_ref[:, tiles - 1] = jnp.concatenate([mine, names], axis=1).astype(BF16)
+            parts.append(update.reshape(peers, COLS, width))
+        send_ref[:, pair] = jnp.concatenate(parts, axis=1).astype(BF16)
+    rows = anc_ref[...].T
+    high = rows.astype(BF16).astype(F32)
+    layer = y_ref[0]
+    mine = jnp.where(layer == 0, high, jnp.where(layer == 1, rows - high, jnp.zeros_like(rows)))
+    leaf = lax.broadcasted_iota(jnp.int32, (COLS, width), 1) // COLS
+    names = jnp.zeros((COLS, width), F32)
+    for k in range(tgt_ref.shape[0]):
+        names = jnp.where(leaf == k, tgt_ref[k].astype(F32), names)
+    names = jnp.broadcast_to(names[None], (peers, COLS, width))
+    send_ref[:, tiles - 1] = jnp.concatenate([mine.reshape(peers, COLS, width), names], axis=1).astype(BF16)
 
 
 def own_pair_kernel(inv_ref, cpl_ref, out_ref):
@@ -92,7 +84,7 @@
 
 def transfer_kernel(x_count, x_ref, c_ref, *refs):
     pairs = refs[: 2 * x_count]
-    m_ref, pack_ref, top_ref = refs[-3:]
+    m_ref, pack_ref, unit_ref, top_ref = refs[-4:]
     count, _, width = m_ref.shape[0:3]
     x, core = x_ref[0], c_ref[0]
     for d in range(x_count):
@@ -102,18 +94,26 @@
     half = count // 2
     runs = []
     for k in range(count):
-        m = (m_ref[k, 0].astype(F32) + m_ref[k, 1].astype(F32)) * STEP_SCALE
-        runs.append(-m if k % half == 0 else -dot_nn(m, runs[-1]))
+        if k % half == 0:
+            run = m_ref[k, 0].astype(F32) + m_ref[k, 1].astype(F32)
+        else:
+            high, low = split(runs[-1])
+            run = jnp.dot(m_ref[k, 0], high, preferred_element_type=F32)
+            run += jnp.dot(m_ref[k, 0], low, preferred_element_type=F32)
+            run += jnp.dot(m_ref[k, 1], high, preferred_element_type=F32)
+        runs.append(run * -STEP_SCALE)
     first = jnp.concatenate(
         [runs[k] * STEP_SCALE ** (count - 1 - k) for k in range(half)], axis=0
     )
     second = jnp.concatenate(
         [runs[k] * STEP_SCALE ** (count - 1 - k) for k in range(half, count)], axis=0
     )
-    second = dot_nn(second, runs[half - 1])
+    second = rows_nn(second, *split(runs[half - 1]))
     stack = jnp.concatenate([first, second], axis=0)
     top = jnp.maximum(jnp.max(jnp.abs(stack)), 1e-30)
-    high, low = split((stack / top).T)
+    unit = stack * (1.0 / top)
+    unit_ref[0], unit_ref[1] = split(unit)
+    high, low = split(unit.T)
     gram = lax.dot_general(high, high, (((1,), (1,)), ((), ())), preferred_element_type=F32)
     cross = lax.dot_general(high, low, (((1,), (1,)), ((), ())), preferred_element_type=F32)
     pack_ref[0], pack_ref[1] = split(stack[width * (count - 1) :])
@@ -128,47 +128,34 @@
         out_ref[lax.rem(z_ref[0] // 2 + d, count)] = refs[d][...]
 
 
-def densify_kernel(plane_size, z_ref, c_ref, v_ref, keep_ref, give_ref, code_ref, acc_ref):
+def densify_kernel(plane_size, z_ref, c_ref, v_ref, dense_ref, code_ref, acc_ref):
     sources, tiles, rows, width = v_ref.shape
-    planes = keep_ref.shape[0]
-    x_count = plane_size // 2
-    body = (tiles - 1) // 2 * rows
+    planes = dense_ref.shape[0]
+    body = (tiles - 1) * rows
     lane = lax.broadcasted_iota(jnp.int32, (sources, body), 1)
     last = v_ref[:, tiles - 1].astype(F32)
     codes = last[:, COLS, :].astype(jnp.int32) * COLS + lane % COLS
-    code_ref[...] = codes.astype(F32).T
-    row = lax.broadcasted_iota(jnp.int32, (acc_ref.shape[1], body), 0)
-
-    def values(s):
-        came = v_ref[s, 0 : tiles - 1].reshape((tiles - 1) // 2, 2, rows, width)
-        return jnp.concatenate([came[:, half].reshape(body, width) for half in range(2)], axis=1)
-
+    by_core = codes.astype(F32).reshape(sources // 2, 2, body)
+    code_ref[...] = jnp.where(c_ref[0] == 0, by_core[:, 0], by_core[:, 1]).T
+    row = lax.broadcasted_iota(jnp.int32, (acc_ref.shape[0], body), 0)
     total = None
     for s in range(0, sources, 2):
         pick = jnp.concatenate(
             [(row == codes[s + i : s + i + 1, :]).astype(F32).astype(BF16) for i in range(2)], axis=1
         )
-        both = jnp.concatenate([values(s), values(s + 1)], axis=0)
+        both = v_ref[s : s + 2, 0 : tiles - 1].reshape(2 * body, width)
         term = jnp.dot(pick, both, preferred_element_type=F32)
         total = term if total is None else total + term
-    for half in range(2):
-        acc_ref[half] = -total[:, width * half : width * (half + 1)]
-    z, core = z_ref[0], c_ref[0]
-    own = pl.multiple_of(z * plane_size * COLS, plane_size * COLS)
-    for x in range(x_count):
-        for half in range(2):
-            mine = last[half * x_count + x, 0:COLS]
-            for y in range(half + 2, sources // x_count, 2):
-                mine = mine + last[y * x_count + x, 0:COLS]
-            place = pl.ds(pl.multiple_of(own + (2 * x + core) * COLS, COLS), COLS)
-            acc_ref[half, place, :] += mine
-    per = plane_size * COLS
-    for z in range(planes):
-        keep_ref[z] = acc_ref[core, per * z : per * (z + 1), :]
-        give_ref[z] = acc_ref[1 - core, per * z : per * (z + 1), :].astype(BF16)
-
-
-def block_solve_kernel(e_ref, m_ref, top_ref, b_ref, out_ref):
+    acc_ref[...] = -total
+    own = pl.multiple_of(z_ref[0] * plane_size * COLS, plane_size * COLS)
+    mine = last[0:plane_size, 0:COLS]
+    for y in range(1, sources // plane_size):
+        mine = mine + last[y * plane_size : (y + 1) * plane_size, 0:COLS]
+    acc_ref[pl.ds(own, plane_size * COLS), :] += mine.reshape(plane_size * COLS, width)
+    dense_ref[...] = acc_ref[...].astype(BF16).reshape(dense_ref.shape)
+
+
+def block_solve_kernel(e_ref, m_ref, unit_ref, top_ref, b_ref, out_ref):
     count = m_ref.shape[0]
     reduced = e_ref[0].astype(F32)
     for s in range(1, e_ref.shape[0]):
@@ -180,9 +167,9 @@
         if j > 0:
             b = b - rows_nt(solved[-1], m_ref[j, 0], m_ref[j, 1])
         solved.append(b)
-    back = rows_nn(solved[-1], m_ref[count - 1, 0], m_ref[count - 1, 1])
-    for j in reversed(range(count - 1)):
-        back = rows_nn(solved[j] - back, m_ref[j, 0], m_ref[j, 1])
+    half_grow = STEP_SCALE ** (-count // 2)
+    back = rows_nn(jnp.concatenate(solved, axis=1), unit_ref[0], unit_ref[1])
+    back = -((back * half_grow) * top_ref[...] * half_grow)
     ends = jnp.concatenate([solved[-1], back, top_ref[...]], axis=0)
     for z in range(out_ref.shape[0]):
         out_ref[z] = ends
@@ -331,6 +318,7 @@
     rhs, inv, upd = leaf_rhs[0], leaf_inverse[0], leaf_update[0]
     leaves, width, rhs_count = rhs.shape
     peers = lax.axis_size(PLANE_AXES)
+    both_peers = 2 * peers
     planes = lax.axis_size("z")
     x_count = lax.axis_size("x")
     plane_size = 2 * x_count
@@ -344,65 +332,51 @@
     (own_pair,) = call(own_pair_kernel, (anc_inverse, anc_coupling), [sds((3, width, width), BF16)], vmem=60)
     along = [own_pair] + [shift(own_pair, "x", d) for d in range(1, x_count)]
 
-    steps = leaves // LEAF_STEP
-    leaf = lambda i: (i, 0, 0)
+    whole = lambda shape: pl.BlockSpec(shape, lambda i: (0,) * len(shape))
+    sent = (both_peers, pairs + 1, 2 * COLS, width)
     forward, send = pl.pallas_call(
         leaf_forward_kernel,
-        grid=(steps,),
-        out_shape=[
-            sds((leaves, rhs_count, width), BF16),
-            sds((peers, 2 * pairs + 1, 2 * COLS, width), BF16),
-        ],
-        in_specs=[
-            SMEM,
-            SMEM,
-            pl.BlockSpec((LEAF_STEP, width, rhs_count), leaf),
-            pl.BlockSpec((LEAF_STEP, width, width), leaf),
-            pl.BlockSpec((LEAF_STEP, width, width), leaf),
-            pl.BlockSpec((width, rhs_count), lambda i: (0, 0)),
-        ],
-        out_specs=[
-            pl.BlockSpec((LEAF_STEP, rhs_count, width), leaf),
-            pl.BlockSpec((peers, 2 * pairs + 1, 2 * COLS, width), lambda i: (0, 0, 0, 0)),
-        ],
+        grid=(1,),
+        out_shape=[sds((leaves, rhs_count, width), BF16), sds(sent, BF16)],
+        in_specs=[SMEM, SMEM] + [whole(a.shape) for a in (rhs, inv, upd, anc_rhs[0])],
+        out_specs=[whole((leaves, rhs_count, width)), whole(sent)],
         compiler_params=pltpu.CompilerParams(
             dimension_semantics=("arbitrary",), vmem_limit_bytes=60 * 2**20
         ),
     )(y_index, leaf_target.astype(jnp.int32).reshape(leaves), rhs, inv, upd, anc_rhs[0])
 
     send, *along = lax.optimization_barrier((send, *along))
-    came = lax.all_to_all(send.reshape(peers, -1, width), PLANE_AXES, 0, 0, tiled=True).reshape(send.shape)
+    came = lax.all_to_all(send.reshape(both_peers, -1, width), CORE_AXES, 0, 0, tiled=True).reshape(sent)
 
     across = [shift(pair, "c", 1) for pair in along]
-    m_blocks, pack, top = call(
+    m_blocks, pack, unit, top = call(
         functools.partial(transfer_kernel, x_count),
         (x_index, c_index, *along, *across),
         [
             sds((plane_size, 3, width, width), BF16),
             sds((3, width, width), BF16),
+            sds((2, plane_size * width, width), BF16),
             sds((COLS, width), F32),
         ],
     )
     packs = [every_other(pack, d) for d in range(planes // 2)]
-    came, *packs = lax.optimization_barrier((came, *packs))
-
-    keep, give, codes = call(
+
+    dense, codes = call(
         functools.partial(densify_kernel, plane_size),
         (z_index, c_index, came),
         [
-            sds((planes, plane_size * COLS, width), F32),
             sds((planes, plane_size * COLS, width), BF16),
             sds((leaves * COLS, peers), F32),
         ],
-        scratch=[pltpu.VMEM((2, chain * COLS, width), F32)],
-    )
-    dense = (keep + shift(give, "c", 1).astype(F32)).astype(BF16)
+        scratch=[pltpu.VMEM((chain * COLS, width), F32)],
+    )
+    dense, *packs = lax.optimization_barrier((dense, *packs))
     sums = lax.all_to_all(dense, "z", 0, 0, tiled=True)
     (own_packs,) = call(order_kernel, (z_index, *packs), [sds((planes // 2, 3, width, width), BF16)])
     other_packs = shift(own_packs, "c", 1)
     b_rows, ends = call(
         block_solve_kernel,
-        (sums, m_blocks, top),
+        (sums, m_blocks, unit, top),
         [sds((plane_size * COLS, width), F32), sds((planes, 3 * COLS, width), F32)],
     )
     all_ends = lax.all_to_all(ends, "z", 0, 0, tiled=True)
@@ -422,9 +396,10 @@
     answers = lax.all_to_all(answer.reshape(peers, -1, width), PLANE_AXES, 0, 0, tiled=True)
     answers = answers.reshape(answer.shape)
 
+    leaf = lambda i: (i, 0, 0)
     leaf_solution, anc_solution = pl.pallas_call(
         leaf_backward_kernel,
-        grid=(steps,),
+        grid=(leaves // LEAF_STEP,),
         out_shape=[sds((leaves, width, rhs_count), BF16), sds((width, rhs_count), F32)],
         in_specs=[
             pl.BlockSpec((peers, LEAF_STEP, 2 * COLS, width), lambda i: (0, i, 0, 0)),

time: 119 us -> 114 us (0.958)
  starting transfers between devices: 39.7 us -> 44.2 us
  waiting for transfers between devices: 22.9 us -> 18.7 us
  blocking collectives: 34.3 us -> 32 us
  Pallas kernels: 19.8 us -> 17.7 us
    all_to_all x1, starting transfers between devices: 4.62 us -> 8.07 us  [local(): lax.all_to_all(send.reshape(both_peers, -1, width), CORE_AXES, 0, 0, tile...]
    ppermute x4, waiting for transfers between devices: 4.97 us -> 2.36 us  [every_other(): lax.ppermute(value, ('z', 'c'), [(2 * (2 * ((z // 2 + by) % half) + c) +...]
    all_to_all x1, blocking collectives: 23.9 us -> 21.6 us  [local(): lax.all_to_all(answer.reshape(peers, -1, width), PLANE_AXES, 0, 0, tiled=...]
    pallas_call x2, Pallas kernels: 8.08 us -> 6.01 us  [the longest x1 3.66 us: local(): pl.pallas_call(leaf_forward_kernel, grid=(1,), out_shape=[sds((leaves, rh...]
    ppermute x10 -> x9, waiting for transfers between devices: 3.53 us -> 2.02 us  [shift(): lax.ppermute(value, axis, [((i + by) % size, i) for i in range(size)])]
    ppermute x10 -> x9, starting transfers between devices: 13.5 us -> 13.9 us  [shift(): lax.ppermute(value, axis, [((i + by) % size, i) for i in range(size)])]
  transfers between devices with their start and end apart: 17 -> 16, of which waited for: 11 -> 9; matrix products, arithmetic and copies ran while one was open for 0% -> 0% of each run, Pallas kernels for 8% -> 8%
where the time goes in v4:
time: 114 us; the launch traced here: 113 us
  starting transfers between devices  44.2 us (39%)
  blocking collectives  32 us (28%)
  waiting for transfers between devices  18.7 us (16%)
  Pallas kernels  17.7 us (16%)
    all_to_all x1, blocking collectives, local(): lax.all_to_all(answer.reshape(peers, -1, width), PLANE_AXES, 0, 0, tiled=...  21.6 us
    ppermute x9, starting transfers between devices, shift(): lax.ppermute(value, axis, [((i + by) % size, i) for i in range(size)])  13.9 us
    ppermute x4, starting transfers between devices, every_other(): lax.ppermute(value, ('z', 'c'), [(2 * (2 * ((z // 2 + by) % half) + c) +...  13.3 us
    pallas_call x7, Pallas kernels, call(): pl.pallas_call(kernel, out_shape=outs, in_specs=[SMEM if a.dtype == jnp.i...  11.7 us
    all_to_all x1, blocking collectives, local(): all_x = lax.all_to_all(x_rows, 'z', 0, 0, tiled=True)  10.3 us
    all_to_all x1, starting transfers between devices, local(): lax.all_to_all(send.reshape(both_peers, -1, width), CORE_AXES, 0, 0, tile...  8.07 us
    all_to_all x1, waiting for transfers between devices, local(): all_ends = lax.all_to_all(ends, 'z', 0, 0, tiled=True)  7.58 us
    all_to_all x1, waiting for transfers between devices, local(): sums = lax.all_to_all(dense, 'z', 0, 0, tiled=True)  5.95 us
  transfers between devices with their start and end apart: 16, of which 9 were waited for; matrix products, arithmetic and copies ran while one was open for 0% of the time, Pallas kernels for 8%

profile of v4, /device:TPU:1, one launch (start us, length us, event | category | flops | bytes accessed | tf_op | source)
XLA Modules:
  0.0 113.3 jit_solution(5551180999825263050)
XLA Ops:
  0.6 1.7 %shard_map.87.refs_0_ = bf16[3,128,128]{2,1,0:T(8,128)(2,1)} custom-call(f32[1,128,128]{2,1,0:T(8,128)} %inv_ref.1, f32[1,128,128]{2,1,0:T(8,128)} %cpl_ref.1), custom_call_target="tpu_custom_call" | custom-call | bytes 229376 | tf_op jit(solution)/shard_map/pallas_call | solution.py:285
  2.3 2.0 %collective-permute-start.2 = (bf16[3,128,128]{2,1,0:T(8,128)(2,1)}, bf16[3,128,128]{2,1,0:T(8,128)(2,1)S(1)}, u32[]{:S(2)}, u32[]{:S(2)}) collective-permute-start(bf16[3,128,128]{2,1,0:T(8,128)(2,1)} %shard_map.87.refs_0_), channel_id=1, source_target_pairs={{6,0},{0,2},{2,4},{4,6},{7,1},{1,3},{3,5},{5,7},{14,8},{8,10},{10,... | collective-permute-start | bytes 294920 | tf_op jit(solution)/shard_map/ppermute | solution.py:301
  4.4 2.4 %collective-permute-start.1 = (bf16[3,128,128]{2,1,0:T(8,128)(2,1)}, bf16[3,128,128]{2,1,0:T(8,128)(2,1)S(1)}, u32[]{:S(2)}, u32[]{:S(2)}) collective-permute-start(bf16[3,128,128]{2,1,0:T(8,128)(2,1)} %shard_map.87.refs_0_), channel_id=1, source_target_pairs={{4,0},{6,2},{0,4},{2,6},{5,1},{7,3},{1,5},{3,7},{12,8},{14,10},{8,... | collective-permute-start | bytes 294920 | tf_op jit(solution)/shard_map/ppermute | solution.py:301
  6.8 1.2 %collective-permute-start = (bf16[3,128,128]{2,1,0:T(8,128)(2,1)}, bf16[3,128,128]{2,1,0:T(8,128)(2,1)S(1)}, u32[]{:S(2)}, u32[]{:S(2)}) collective-permute-start(bf16[3,128,128]{2,1,0:T(8,128)(2,1)} %shard_map.87.refs_0_), channel_id=1, source_target_pairs={{2,0},{4,2},{6,4},{0,6},{3,1},{5,3},{7,5},{1,7},{10,8},{12,10},{14... | collective-permute-start | bytes 294920 | tf_op jit(solution)/shard_map/ppermute | solution.py:301
  8.0 3.7 %shard_map.86 = (bf16[16,256,128]{2,1,0:T(8,128)(2,1)}, bf16[32,9,16,128]{3,2,1,0:T(8,128)(2,1)}) custom-call(s32[1]{0:T(128)} %bitcast.2.y_ref, s32[16]{0:T(128)} %bitcast.26, bf16[16,128,256]{2,1,0:T(8,128)(2,1)} %bitcast.24, bf16[16,128,128]{2,1,0:T(8,128)(2,1)} %bitcast.19, bf16[16,128,128]{2,1,0:T(8,128)(2,1)} %bitcast.21, f32[128,256]{1,0:T(8,128)} %bitcast.25), custom_call_target="tpu_custom_call" | custom-call | tf_op jit(solution)/shard_map/pallas_call | solution.py:337
  11.7 8.1 %all-to-all-start = ((bf16[32,144,128]{2,1,0:T(8,128)(2,1)}), bf16[32,144,128]{2,1,0:T(8,128)(2,1)S(1)}, u32[]{:S(2)}, u32[]{:S(2)}) async-start(bf16[32,144,128]{2,1,0:T(8,128)(2,1)} %bitcast.23), calls=%async_computation | async-start | bytes 2359296 | tf_op jit(solution)/shard_map/all_to_all | solution.py:349
  21.9 1.7 %shard_map.89 = (bf16[8,3,128,128]{3,2,1,0:T(8,128)(2,1)S(1)}, bf16[3,128,128]{2,1,0:T(8,128)(2,1)S(1)}, bf16[2,1024,128]{2,1,0:T(8,128)(2,1)S(1)}, f32[8,128]{1,0:T(8,128)S(1)}) custom-call(s32[1]{0:T(128)} %bitcast.10.x_ref, s32[1]{0:T(128)} %bitcast.1.c_ref, bf16[3,128,128]{2,1,0:T(8,128)(2,1)S(1)} %copy-done.3, ...), custom_call_target="tpu_custom_call" | custom-call | bytes 2199560 | tf_op jit(solution)/shard_map/pallas_call | solution.py:285
  23.6 4.6 %collective-permute-start.10 = (bf16[3,128,128]{2,1,0:T(8,128)(2,1)S(1)}, bf16[3,128,128]{2,1,0:T(8,128)(2,1)S(1)}, u32[]{:S(2)}, u32[]{:S(2)}) collective-permute-start(bf16[3,128,128]{2,1,0:T(8,128)(2,1)S(1)} %get-tuple-element.31), channel_id=1, source_target_pairs={{48,0},{56,1},{49,8},{57,9},{0,16},{8,17},{1,24},{9,25},{16,32},{2... | collective-permute-start | bytes 294920 | tf_op jit(solution)/shard_map/ppermute | solution.py:306
  28.2 3.0 %collective-permute-start.9 = (bf16[3,128,128]{2,1,0:T(8,128)(2,1)S(1)}, bf16[3,128,128]{2,1,0:T(8,128)(2,1)S(1)}, u32[]{:S(2)}, u32[]{:S(2)}) collective-permute-start(bf16[3,128,128]{2,1,0:T(8,128)(2,1)S(1)} %get-tuple-element.31), channel_id=1, source_target_pairs={{32,0},{40,1},{33,8},{41,9},{48,16},{56,17},{49,24},{57,25},{0,32}... | collective-permute-start | bytes 294920 | tf_op jit(solution)/shard_map/ppermute | solution.py:306
  31.2 3.0 %collective-permute-start.8 = (bf16[3,128,128]{2,1,0:T(8,128)(2,1)S(1)}, bf16[3,128,128]{2,1,0:T(8,128)(2,1)S(1)}, u32[]{:S(2)}, u32[]{:S(2)}) collective-permute-start(bf16[3,128,128]{2,1,0:T(8,128)(2,1)S(1)} %get-tuple-element.31), channel_id=1, source_target_pairs={{16,0},{24,1},{17,8},{25,9},{32,16},{40,17},{33,24},{41,25},{48,32... | collective-permute-start | bytes 294920 | tf_op jit(solution)/shard_map/ppermute | solution.py:306
  34.2 2.7 %collective-permute-start.7 = (bf16[3,128,128]{2,1,0:T(8,128)(2,1)S(1)}, bf16[3,128,128]{2,1,0:T(8,128)(2,1)S(1)}, u32[]{:S(2)}, u32[]{:S(2)}) collective-permute-start(bf16[3,128,128]{2,1,0:T(8,128)(2,1)S(1)} %get-tuple-element.31), channel_id=1, source_target_pairs={{0,0},{8,1},{1,8},{9,9},{16,16},{24,17},{17,24},{25,25},{32,32},{4... | collective-permute-start | bytes 294920 | tf_op jit(solution)/shard_map/ppermute | solution.py:306
  37.7 1.9 %shard_map.88 = (bf16[8,64,128]{2,1,0:T(8,128)(2,1)}, f32[128,16]{1,0:T(8,128)S(1)}) custom-call(s32[1]{0:T(128)} %bitcast.z_ref, s32[1]{0:T(128)} %bitcast.1.c_ref, bf16[32,9,16,128]{3,2,1,0:T(8,128)(2,1)S(1)} %bitcast.17), custom_call_target="tpu_custom_call" | custom-call | bytes 1318920 | tf_op jit(solution)/shard_map/pallas_call | solution.py:285
  39.7 2.4 %collective-permute-done.7.refs_0_ = bf16[3,128,128]{2,1,0:T(8,128)(2,1)S(1)} collective-permute-done((bf16[3,128,128]{2,1,0:T(8,128)(2,1)S(1)}, bf16[3,128,128]{2,1,0:T(8,128)(2,1)S(1)}, u32[]{:S(2)}, u32[]{:S(2)}) %collective-permute-start.7) | collective-permute-done | bytes 98336 | tf_op jit(solution)/shard_map/ppermute | solution.py:306
  42.1 5.6 %all-to-all-start.1 = ((bf16[8,64,128]{2,1,0:T(8,128)(2,1)}), bf16[8,64,128]{2,1,0:T(8,128)(2,1)S(1)}, u32[]{:S(2)}, u32[]{:S(2)}) async-start(bf16[8,64,128]{2,1,0:T(8,128)(2,1)} %get-tuple-element.32), calls=%async_computation.1 | async-start | bytes 262144 | tf_op jit(solution)/shard_map/all_to_all | solution.py:374
  47.6 1.9 %collective-permute-start.11 = (bf16[4,3,128,128]{3,2,1,0:T(8,128)(2,1)S(1)}, bf16[4,3,128,128]{3,2,1,0:T(8,128)(2,1)S(1)}, u32[]{:S(2)}, u32[]{:S(2)}) collective-permute-start(bf16[4,3,128,128]{3,2,1,0:T(8,128)(2,1)S(1)} %shard_map.91.mine_ref), channel_id=1, source_target_pairs={{1,0},{0,1},{3,2},{2,3},{5,4},{4,5},{7,6},{6,7},{9,8},{8,9},{11,10... | collective-permute-start | bytes 1179656 | tf_op jit(solution)/shard_map/ppermute | solution.py:301
  49.6 6.0 %all-to-all-done.1.e_ref = bf16[8,64,128]{2,1,0:T(8,128)(2,1)S(1)} async-done(((bf16[8,64,128]{2,1,0:T(8,128)(2,1)}), bf16[8,64,128]{2,1,0:T(8,128)(2,1)S(1)}, u32[]{:S(2)}, u32[]{:S(2)}) %all-to-all-start.1) | async-done | bytes 131104 | tf_op jit(solution)/shard_map/all_to_all | solution.py:374
  55.5 1.8 %shard_map.90 = (f32[64,128]{1,0:T(8,128)S(1)}, f32[8,24,128]{2,1,0:T(8,128)}) custom-call(bf16[8,64,128]{2,1,0:T(8,128)(2,1)S(1)} %all-to-all-done.1.e_ref, bf16[8,3,128,128]{3,2,1,0:T(8,128)(2,1)S(1)} %get-tuple-element.33.m_ref, bf16[2,1024,128]{2,1,0:T(8,128)(2,1)S(1)} %get-tuple-element.34.unit_ref, f32[8,128]{1,0:T(8,128)S(1)} %get-tuple-element.35.top_ref), custom_call_target="tpu_custom_call" | custom-call | bytes 1576960 | tf_op jit(solution)/shard_map/pallas_call | solution.py:285
  57.3 3.4 %all-to-all-start.2 = ((f32[8,24,128]{2,1,0:T(8,128)}), f32[8,24,128]{2,1,0:T(8,128)S(1)}, u32[]{:S(2)}, u32[]{:S(2)}) async-start(f32[8,24,128]{2,1,0:T(8,128)} %get-tuple-element.36), calls=%async_computation.2 | async-start | bytes 196608 | tf_op jit(solution)/shard_map/all_to_all | solution.py:382
  60.7 7.6 %all-to-all-done.2.ends_ref = f32[8,24,128]{2,1,0:T(8,128)S(1)} async-done(((f32[8,24,128]{2,1,0:T(8,128)}), f32[8,24,128]{2,1,0:T(8,128)S(1)}, u32[]{:S(2)}, u32[]{:S(2)}) %all-to-all-start.2) | async-done | bytes 98336 | tf_op jit(solution)/shard_map/all_to_all | solution.py:382
  68.3 3.7 %shard_map.92 = bf16[8,64,128]{2,1,0:T(8,128)(2,1)S(1)} custom-call(s32[1]{0:T(128)} %bitcast.z_ref, s32[1]{0:T(128)} %bitcast.1.c_ref, f32[8,24,128]{2,1,0:T(8,128)S(1)} %all-to-all-done.2.ends_ref, bf16[4,3,128,128]{3,2,1,0:T(8,128)(2,1)S(1)} %shard_map.91.mine_ref, bf16[4,3,128,128]{3,2,1,0:T(8,128)(2,1)S(1)} %collective-permute-done.11.other_ref, ...), custom_call_target="tpu_custom_call" | custom-call | bytes 1835016 | tf_op jit(solution)/shard_map/pallas_call | solution.py:285
  72.0 10.3 %all_to_all.25.x_ref = bf16[8,64,128]{2,1,0:T(8,128)(2,1)S(1)} all-to-all(bf16[8,64,128]{2,1,0:T(8,128)(2,1)S(1)} %shard_map.92), channel_id=1, replica_groups=mesh['y'=4,'z'=8,'x'=4,'c'=2] {'z'}, dimensions={0} | all-to-all | bytes 262144 | tf_op jit(solution)/shard_map/all_to_all | solution.py:389
  82.3 5.2 %collective-permute-start.12 = (bf16[8,64,128]{2,1,0:T(8,128)(2,1)S(1)}, bf16[8,64,128]{2,1,0:T(8,128)(2,1)S(1)}, u32[]{:S(2)}, u32[]{:S(2)}) collective-permute-start(bf16[8,64,128]{2,1,0:T(8,128)(2,1)S(1)} %all_to_all.25.x_ref), channel_id=1, source_target_pairs={{1,0},{0,1},{3,2},{2,3},{5,4},{4,5},{7,6},{6,7},{9,8},{8,9},{11,10... | collective-permute-start | bytes 393224 | tf_op jit(solution)/shard_map/ppermute | solution.py:301
  89.3 21.6 %all_to_all.26 = bf16[16,272,128]{2,1,0:T(8,128)(2,1)S(1)} all-to-all(bf16[16,272,128]{2,1,0:T(8,128)(2,1)S(1)} %bitcast.18), channel_id=1, replica_groups=mesh['y'=4,'z'=8,'x'=4,'c'=2] {'y','x'}, dimensions={0} | all-to-all | bytes 2228224 | tf_op jit(solution)/shard_map/all_to_all | solution.py:396
  111.0 2.4 %shard_map.94 = (bf16[16,128,256]{2,1,0:T(8,128)(2,1)}, f32[128,256]{1,0:T(8,128)}) custom-call(bf16[16,17,16,128]{3,2,1,0:T(8,128)(2,1)S(1)} %bitcast.15, bf16[16,17,16,128]{3,2,1,0:T(8,128)(2,1)S(1)} %bitcast.16, bf16[16,256,128]{2,1,0:T(8,128)(2,1)S(1)} %copy-done.2, bf16[16,128,128]{2,1,0:T(8,128)(2,1)S(1)} %bitcast.20, bf16[16,128,128]{2,1,0:T(8,128)(2,1)S(1)} %bitcast.22), custom_call_target="tpu_custom_call" | custom-call | tf_op jit(solution)/shard_map/pallas_call | solution.py:400
  (27 shorter events, 4.8 us)
Async XLA Ops:
  2.3 9.3 %collective-permute-start.2 = (bf16[3,128,128]{2,1,0:T(8,128)(2,1)}, bf16[3,128,128]{2,1,0:T(8,128)(2,1)S(1)}, u32[]{:S(2)}, u32[]{:S(2)}) collective-permute-start(bf16[3,128,128]{2,1,0:T(8,128)(2,1)} %shard_map.87.refs_0_), channel_id=1, source_target_pairs={{6,0},{0,2},{2,4},{4,6},{7,1},{1,3},{3,5},{5,7},{14,8},{8,10},{10,... | collective-permute-start | bytes 294920 | tf_op jit(solution)/shard_map/ppermute | solution.py:301
  4.4 7.3 %collective-permute-start.1 = (bf16[3,128,128]{2,1,0:T(8,128)(2,1)}, bf16[3,128,128]{2,1,0:T(8,128)(2,1)S(1)}, u32[]{:S(2)}, u32[]{:S(2)}) collective-permute-start(bf16[3,128,128]{2,1,0:T(8,128)(2,1)} %shard_map.87.refs_0_), channel_id=1, source_target_pairs={{4,0},{6,2},{0,4},{2,6},{5,1},{7,3},{1,5},{3,7},{12,8},{14,10},{8,... | collective-permute-start | bytes 294920 | tf_op jit(solution)/shard_map/ppermute | solution.py:301
  6.8 4.8 %collective-permute-start = (bf16[3,128,128]{2,1,0:T(8,128)(2,1)}, bf16[3,128,128]{2,1,0:T(8,128)(2,1)S(1)}, u32[]{:S(2)}, u32[]{:S(2)}) collective-permute-start(bf16[3,128,128]{2,1,0:T(8,128)(2,1)} %shard_map.87.refs_0_), channel_id=1, source_target_pairs={{2,0},{4,2},{6,4},{0,6},{3,1},{5,3},{7,5},{1,7},{10,8},{12,10},{14... | collective-permute-start | bytes 294920 | tf_op jit(solution)/shard_map/ppermute | solution.py:301
  11.7 8.1 %copy-start.3 = (bf16[3,128,128]{2,1,0:T(8,128)(2,1)S(1)}, bf16[3,128,128]{2,1,0:T(8,128)(2,1)}, u32[]{:S(2)}) copy-start(bf16[3,128,128]{2,1,0:T(8,128)(2,1)} %shard_map.87.refs_0_) | copy-start | bytes 294916
  11.7 26.1 %all-to-all-start = ((bf16[32,144,128]{2,1,0:T(8,128)(2,1)}), bf16[32,144,128]{2,1,0:T(8,128)(2,1)S(1)}, u32[]{:S(2)}, u32[]{:S(2)}) async-start(bf16[32,144,128]{2,1,0:T(8,128)(2,1)} %bitcast.23), calls=%async_computation | async-start | bytes 2359296 | tf_op jit(solution)/shard_map/all_to_all | solution.py:349
  19.8 1.4 %collective-permute-start.3 = (bf16[3,128,128]{2,1,0:T(8,128)(2,1)S(1)}, bf16[3,128,128]{2,1,0:T(8,128)(2,1)S(1)}, u32[]{:S(2)}, u32[]{:S(2)}) collective-permute-start(bf16[3,128,128]{2,1,0:T(8,128)(2,1)S(1)} %copy-done.3), channel_id=1, source_target_pairs={{1,0},{0,1},{3,2},{2,3},{5,4},{4,5},{7,6},{6,7},{9,8},{8,9},{11,10... | collective-permute-start | bytes 294920 | tf_op jit(solution)/shard_map/ppermute | solution.py:301
  20.1 1.3 %collective-permute-start.4 = (bf16[3,128,128]{2,1,0:T(8,128)(2,1)S(1)}, bf16[3,128,128]{2,1,0:T(8,128)(2,1)S(1)}, u32[]{:S(2)}, u32[]{:S(2)}) collective-permute-start(bf16[3,128,128]{2,1,0:T(8,128)(2,1)S(1)} %collective-permute-done.refs_1_), channel_id=1, source_target_pairs={{1,0},{0,1},{3,2},{2,3},{5,4},{4,5},{7,6},{6,7},{9,8},{8,9},{11,10... | collective-permute-start | bytes 294920 | tf_op jit(solution)/shard_map/ppermute | solution.py:301
  20.4 1.3 %collective-permute-start.5 = (bf16[3,128,128]{2,1,0:T(8,128)(2,1)S(1)}, bf16[3,128,128]{2,1,0:T(8,128)(2,1)S(1)}, u32[]{:S(2)}, u32[]{:S(2)}) collective-permute-start(bf16[3,128,128]{2,1,0:T(8,128)(2,1)S(1)} %collective-permute-done.1.refs_2_), channel_id=1, source_target_pairs={{1,0},{0,1},{3,2},{2,3},{5,4},{4,5},{7,6},{6,7},{9,8},{8,9},{11,10... | collective-permute-start | bytes 294920 | tf_op jit(solution)/shard_map/ppermute | solution.py:301
  20.6 1.3 %collective-permute-start.6 = (bf16[3,128,128]{2,1,0:T(8,128)(2,1)S(1)}, bf16[3,128,128]{2,1,0:T(8,128)(2,1)S(1)}, u32[]{:S(2)}, u32[]{:S(2)}) collective-permute-start(bf16[3,128,128]{2,1,0:T(8,128)(2,1)S(1)} %collective-permute-done.2.refs_3_), channel_id=1, source_target_pairs={{1,0},{0,1},{3,2},{2,3},{5,4},{4,5},{7,6},{6,7},{9,8},{8,9},{11,10... | collective-permute-start | bytes 294920 | tf_op jit(solution)/shard_map/ppermute | solution.py:301
  23.6 16.1 %collective-permute-start.10 = (bf16[3,128,128]{2,1,0:T(8,128)(2,1)S(1)}, bf16[3,128,128]{2,1,0:T(8,128)(2,1)S(1)}, u32[]{:S(2)}, u32[]{:S(2)}) collective-permute-start(bf16[3,128,128]{2,1,0:T(8,128)(2,1)S(1)} %get-tuple-element.31), channel_id=1, source_target_pairs={{48,0},{56,1},{49,8},{57,9},{0,16},{8,17},{1,24},{9,25},{16,32},{2... | collective-permute-start | bytes 294920 | tf_op jit(solution)/shard_map/ppermute | solution.py:306
  28.2 11.5 %collective-permute-start.9 = (bf16[3,128,128]{2,1,0:T(8,128)(2,1)S(1)}, bf16[3,128,128]{2,1,0:T(8,128)(2,1)S(1)}, u32[]{:S(2)}, u32[]{:S(2)}) collective-permute-start(bf16[3,128,128]{2,1,0:T(8,128)(2,1)S(1)} %get-tuple-element.31), channel_id=1, source_target_pairs={{32,0},{40,1},{33,8},{41,9},{48,16},{56,17},{49,24},{57,25},{0,32}... | collective-permute-start | bytes 294920 | tf_op jit(solution)/shard_map/ppermute | solution.py:306
  31.2 8.5 %collective-permute-start.8 = (bf16[3,128,128]{2,1,0:T(8,128)(2,1)S(1)}, bf16[3,128,128]{2,1,0:T(8,128)(2,1)S(1)}, u32[]{:S(2)}, u32[]{:S(2)}) collective-permute-start(bf16[3,128,128]{2,1,0:T(8,128)(2,1)S(1)} %get-tuple-element.31), channel_id=1, source_target_pairs={{16,0},{24,1},{17,8},{25,9},{32,16},{40,17},{33,24},{41,25},{48,32... | collective-permute-start | bytes 294920 | tf_op jit(solution)/shard_map/ppermute | solution.py:306
  34.2 7.9 %collective-permute-start.7 = (bf16[3,128,128]{2,1,0:T(8,128)(2,1)S(1)}, bf16[3,128,128]{2,1,0:T(8,128)(2,1)S(1)}, u32[]{:S(2)}, u32[]{:S(2)}) collective-permute-start(bf16[3,128,128]{2,1,0:T(8,128)(2,1)S(1)} %get-tuple-element.31), channel_id=1, source_target_pairs={{0,0},{8,1},{1,8},{9,9},{16,16},{24,17},{17,24},{25,25},{32,32},{4... | collective-permute-start | bytes 294920 | tf_op jit(solution)/shard_map/ppermute | solution.py:306
  42.1 13.5 %all-to-all-start.1 = ((bf16[8,64,128]{2,1,0:T(8,128)(2,1)}), bf16[8,64,128]{2,1,0:T(8,128)(2,1)S(1)}, u32[]{:S(2)}, u32[]{:S(2)}) async-start(bf16[8,64,128]{2,1,0:T(8,128)(2,1)} %get-tuple-element.32), calls=%async_computation.1 | async-start | bytes 262144 | tf_op jit(solution)/shard_map/all_to_all | solution.py:374
  47.6 13.1 %collective-permute-start.11 = (bf16[4,3,128,128]{3,2,1,0:T(8,128)(2,1)S(1)}, bf16[4,3,128,128]{3,2,1,0:T(8,128)(2,1)S(1)}, u32[]{:S(2)}, u32[]{:S(2)}) collective-permute-start(bf16[4,3,128,128]{3,2,1,0:T(8,128)(2,1)S(1)} %shard_map.91.mine_ref), channel_id=1, source_target_pairs={{1,0},{0,1},{3,2},{2,3},{5,4},{4,5},{7,6},{6,7},{9,8},{8,9},{11,10... | collective-permute-start | bytes 1179656 | tf_op jit(solution)/shard_map/ppermute | solution.py:301
  57.3 11.0 %all-to-all-start.2 = ((f32[8,24,128]{2,1,0:T(8,128)}), f32[8,24,128]{2,1,0:T(8,128)S(1)}, u32[]{:S(2)}, u32[]{:S(2)}) async-start(f32[8,24,128]{2,1,0:T(8,128)} %get-tuple-element.36), calls=%async_computation.2 | async-start | bytes 196608 | tf_op jit(solution)/shard_map/all_to_all | solution.py:382
  82.3 6.2 %collective-permute-start.12 = (bf16[8,64,128]{2,1,0:T(8,128)(2,1)S(1)}, bf16[8,64,128]{2,1,0:T(8,128)(2,1)S(1)}, u32[]{:S(2)}, u32[]{:S(2)}) collective-permute-start(bf16[8,64,128]{2,1,0:T(8,128)(2,1)S(1)} %all_to_all.25.x_ref), channel_id=1, source_target_pairs={{1,0},{0,1},{3,2},{2,3},{5,4},{4,5},{7,6},{6,7},{9,8},{8,9},{11,10... | collective-permute-start | bytes 393224 | tf_op jit(solution)/shard_map/ppermute | solution.py:301
  89.3 21.7 %copy-start = (bf16[1,16,128,128]{3,2,1,0:T(8,128)(2,1)S(1)}, bf16[1,16,128,128]{3,2,1,0:T(8,128)(2,1)}, u32[]{:S(2)}) copy-start(bf16[1,16,128,128]{3,2,1,0:T(8,128)(2,1)} %param.8) | copy-start | bytes 1572868
  89.3 21.7 %copy-start.1 = (bf16[1,16,128,128]{3,2,1,0:T(8,128)(2,1)S(1)}, bf16[1,16,128,128]{3,2,1,0:T(8,128)(2,1)}, u32[]{:S(2)}) copy-start(bf16[1,16,128,128]{3,2,1,0:T(8,128)(2,1)} %param.9) | copy-start | bytes 1572868
  89.3 21.7 %copy-start.2 = (bf16[16,256,128]{2,1,0:T(8,128)(2,1)S(1)}, bf16[16,256,128]{2,1,0:T(8,128)(2,1)}, u32[]{:S(2)}) copy-start(bf16[16,256,128]{2,1,0:T(8,128)(2,1)} %get-tuple-element.43.fwd_ref) | copy-start | bytes 3145732

commit v5 on v4

--- a/solution.py
+++ b/solution.py
@@ -121,6 +121,26 @@
     top_ref[...] = jnp.full(top_ref.shape, top, F32)
 
 
+def late_kernel(m_ref, late_ref, top_ref):
+    count = m_ref.shape[0]
+    half = count // 2
+    runs = [None] * count
+    for k in reversed(range(count)):
+        if k % half == half - 1:
+            run = m_ref[k, 0].astype(F32) + m_ref[k, 1].astype(F32)
+        else:
+            run = rows_nn(runs[k + 1], m_ref[k, 0], m_ref[k, 1])
+        runs[k] = run * -STEP_SCALE
+    shared = runs[half]
+    first = rows_nn(shared, *split(jnp.concatenate(runs[:half], axis=1)))
+    width = shared.shape[0]
+    pieces = [first[:, width * k : width * (k + 1)] for k in range(half)] + runs[half:]
+    stack = jnp.concatenate([pieces[k] * STEP_SCALE**k for k in range(count)], axis=1)
+    top = jnp.maximum(jnp.max(jnp.abs(stack)), 1e-30)
+    late_ref[0], late_ref[1] = split(stack * (1.0 / top))
+    top_ref[...] = jnp.full(top_ref.shape, top, F32)
+
+
 def order_kernel(z_ref, *refs):
     out_ref = refs[-1]
     count = out_ref.shape[0]
@@ -155,7 +175,7 @@
     dense_ref[...] = acc_ref[...].astype(BF16).reshape(dense_ref.shape)
 
 
-def block_solve_kernel(e_ref, m_ref, unit_ref, top_ref, b_ref, out_ref):
+def block_solve_kernel(e_ref, m_ref, unit_ref, top_ref, s_ref, out_ref):
     count = m_ref.shape[0]
     reduced = e_ref[0].astype(F32)
     for s in range(1, e_ref.shape[0]):
@@ -163,19 +183,22 @@
     solved = []
     for j in range(count):
         b = rows_nt(reduced[COLS * j : COLS * (j + 1)], m_ref[j, 2])
-        b_ref[COLS * j : COLS * (j + 1), :] = b
         if j > 0:
             b = b - rows_nt(solved[-1], m_ref[j, 0], m_ref[j, 1])
         solved.append(b)
     half_grow = STEP_SCALE ** (-count // 2)
-    back = rows_nn(jnp.concatenate(solved, axis=1), unit_ref[0], unit_ref[1])
+    solved_wide = jnp.concatenate(solved, axis=1)
+    s_ref[...] = solved_wide
+    back = rows_nn(solved_wide, unit_ref[0], unit_ref[1])
     back = -((back * half_grow) * top_ref[...] * half_grow)
     ends = jnp.concatenate([solved[-1], back, top_ref[...]], axis=0)
     for z in range(out_ref.shape[0]):
         out_ref[z] = ends
 
 
-def carry_kernel(z_ref, c_ref, ends_ref, mine_ref, other_ref, b_ref, m_ref, x_ref, pack_ref):
+def carry_kernel(
+    z_ref, c_ref, ends_ref, mine_ref, other_ref, s_ref, m_ref, unit_ref, top_ref, late_ref, late_top_ref, x_ref, pack_ref
+):
     planes = ends_ref.shape[0]
     count, _, width = m_ref.shape[0:3]
     core = c_ref[0]
@@ -200,24 +223,32 @@
         state = leaving
         if z < planes - 1:
             inflow = jnp.where(own == z + 1, state, inflow)
+    gain = rows_nt(inflow, unit_ref[0], unit_ref[1])
+    solved = s_ref[...] + (gain * half_grow) * top_ref[:, 0:1] * half_grow
+    solved = [solved[:, width * k : width * (k + 1)] for k in range(count)]
     state = jnp.zeros((COLS, width), F32)
     running = state
-    for z in reversed(range(1, planes)):
-        leaving = backs[z]
-        if z < planes - 1:
-            leaving = leaving + grow * rows_nn(state, pack_ref[z, 0], pack_ref[z, 1])
-        state = leaving
-        running = jnp.where(own == z - 1, state, running)
-    solved = []
+    after = [None] * (count + 1)
+    for i in range(max(planes, count) - 1):
+        z, j = planes - 1 - i, count - 1 - i
+        if z > 0:
+            leaving = backs[z]
+            if z < planes - 1:
+                leaving = leaving + grow * rows_nn(state, pack_ref[z, 0], pack_ref[z, 1])
+            state = leaving
+            running = jnp.where(own == z - 1, state, running)
+        if j > 0:
+            right = solved[j] if after[j + 1] is None else solved[j] - after[j + 1]
+            after[j] = rows_nn(right, m_ref[j, 0], m_ref[j, 1])
+    gain = rows_nn(running, late_ref[0], late_ref[1])
+    gain = (gain * half_grow) * late_top_ref[:, 0:1] * half_grow
+    answers = []
     for j in range(count):
-        inflow = b_ref[COLS * j : COLS * (j + 1), :] - rows_nt(inflow, m_ref[j, 0], m_ref[j, 1])
-        solved.append(inflow)
-    answers = [None] * count
-    for j in reversed(range(count)):
-        right = solved[j] - running
-        if j > 0:
-            running = rows_nn(right, m_ref[j, 0], m_ref[j, 1])
-        answers[j] = rows_nn(right, m_ref[j, 2])
+        if j < count - 1:
+            right = solved[j] - (after[j + 1] + gain[:, width * (j + 1) : width * (j + 2)])
+        else:
+            right = solved[j] - running
+        answers.append(rows_nn(right, m_ref[j, 2]))
     coarse = jnp.concatenate(answers, axis=0).astype(BF16)
     for z in range(x_ref.shape[0]):
         x_ref[z] = coarse
@@ -374,15 +405,21 @@
     sums = lax.all_to_all(dense, "z", 0, 0, tiled=True)
     (own_packs,) = call(order_kernel, (z_index, *packs), [sds((planes // 2, 3, width, width), BF16)])
     other_packs = shift(own_packs, "c", 1)
-    b_rows, ends = call(
+    late, late_top = call(
+        late_kernel,
+        (m_blocks,),
+        [sds((2, width, plane_size * width), BF16), sds((COLS, width), F32)],
+    )
+    s_wide, ends = call(
         block_solve_kernel,
         (sums, m_blocks, unit, top),
-        [sds((plane_size * COLS, width), F32), sds((planes, 3 * COLS, width), F32)],
-    )
+        [sds((COLS, plane_size * width), F32), sds((planes, 3 * COLS, width), F32)],
+    )
+    ends, other_packs, late, late_top = lax.optimization_barrier((ends, other_packs, late, late_top))
     all_ends = lax.all_to_all(ends, "z", 0, 0, tiled=True)
     (x_rows,) = call(
         carry_kernel,
-        (z_index, c_index, all_ends, own_packs, other_packs, b_rows, m_blocks),
+        (z_index, c_index, all_ends, own_packs, other_packs, s_wide, m_blocks, unit, top, late, late_top),
         [sds((planes, plane_size * COLS, width), BF16)],
         scratch=[pltpu.VMEM((planes, 3, width, width), BF16)],
     )

time: 114 us -> 112 us (0.982)
  blocking collectives: 32 us -> 41.9 us
  waiting for transfers between devices: 18.7 us -> 12.5 us
  starting transfers between devices: 44.2 us -> 39.2 us
    all_to_all x0 -> x1, blocking collectives: none -> 9.96 us  [local(): all_ends = lax.all_to_all(ends, 'z', 0, 0, tiled=True)]
    all_to_all x1 -> x0, waiting for transfers between devices: 7.58 us -> none  [local(): all_ends = lax.all_to_all(ends, 'z', 0, 0, tiled=True)]
    all_to_all x1 -> x0, starting transfers between devices: 3.36 us -> none  [local(): all_ends = lax.all_to_all(ends, 'z', 0, 0, tiled=True)]
    ppermute x9, starting transfers between devices: 13.9 us -> 10.7 us  [shift(): lax.ppermute(value, axis, [((i + by) % size, i) for i in range(size)])]
    all_to_all x1, starting transfers between devices: 5.55 us -> 7.1 us  [local(): sums = lax.all_to_all(dense, 'z', 0, 0, tiled=True)]
    all_to_all x1, waiting for transfers between devices: 5.95 us -> 7.26 us  [local(): sums = lax.all_to_all(dense, 'z', 0, 0, tiled=True)]
    pallas_call x7 -> x8, Pallas kernels: 11.7 us -> 10.9 us  [call(): pl.pallas_call(kernel, out_shape=outs, in_specs=[SMEM if a.dtype == jnp.i...]
  transfers between devices with their start and end apart: 16 -> 15, of which waited for: 9 -> 8; matrix products, arithmetic and copies ran while one was open for 0% -> 0% of each run, Pallas kernels for 8% -> 9%
where the time goes in v5:
time: 112 us; the launch traced here: 111 us
  blocking collectives  41.9 us (37%)
  starting transfers between devices  39.2 us (35%)
  Pallas kernels  16.9 us (15%)
  waiting for transfers between devices  12.5 us (11%)
    all_to_all x1, blocking collectives, local(): lax.all_to_all(answer.reshape(peers, -1, width), PLANE_AXES, 0, 0, tiled=...  21.6 us
    ppermute x4, starting transfers between devices, every_other(): lax.ppermute(value, ('z', 'c'), [(2 * (2 * ((z // 2 + by) % half) + c) +...  13.3 us
    pallas_call x8, Pallas kernels, call(): pl.pallas_call(kernel, out_shape=outs, in_specs=[SMEM if a.dtype == jnp.i...  10.9 us
    ppermute x9, starting transfers between devices, shift(): lax.ppermute(value, axis, [((i + by) % size, i) for i in range(size)])  10.7 us
    all_to_all x1, blocking collectives, local(): all_x = lax.all_to_all(x_rows, 'z', 0, 0, tiled=True)  10.3 us
    all_to_all x1, blocking collectives, local(): all_ends = lax.all_to_all(ends, 'z', 0, 0, tiled=True)  9.96 us
    all_to_all x1, starting transfers between devices, local(): lax.all_to_all(send.reshape(both_peers, -1, width), CORE_AXES, 0, 0, tile...  8.07 us
    all_to_all x1, waiting for transfers between devices, local(): sums = lax.all_to_all(dense, 'z', 0, 0, tiled=True)  7.26 us
  transfers between devices with their start and end apart: 15, of which 8 were waited for; matrix products, arithmetic and copies ran while one was open for 0% of the time, Pallas kernels for 9%

profile of v5, /device:TPU:1, one launch (start us, length us, event | category | flops | bytes accessed | tf_op | source)
XLA Modules:
  0.0 111.2 jit_solution(4113873202419767222)
XLA Ops:
  0.6 1.7 %shard_map.87.refs_0_ = bf16[3,128,128]{2,1,0:T(8,128)(2,1)} custom-call(f32[1,128,128]{2,1,0:T(8,128)} %inv_ref.1, f32[1,128,128]{2,1,0:T(8,128)} %cpl_ref.1), custom_call_target="tpu_custom_call" | custom-call | bytes 229376 | tf_op jit(solution)/shard_map/pallas_call | solution.py:316
  2.3 2.0 %collective-permute-start.2 = (bf16[3,128,128]{2,1,0:T(8,128)(2,1)}, bf16[3,128,128]{2,1,0:T(8,128)(2,1)S(1)}, u32[]{:S(2)}, u32[]{:S(2)}) collective-permute-start(bf16[3,128,128]{2,1,0:T(8,128)(2,1)} %shard_map.87.refs_0_), channel_id=1, source_target_pairs={{6,0},{0,2},{2,4},{4,6},{7,1},{1,3},{3,5},{5,7},{14,8},{8,10},{10,... | collective-permute-start | bytes 294920 | tf_op jit(solution)/shard_map/ppermute | solution.py:332
  4.4 2.5 %collective-permute-start.1 = (bf16[3,128,128]{2,1,0:T(8,128)(2,1)}, bf16[3,128,128]{2,1,0:T(8,128)(2,1)S(1)}, u32[]{:S(2)}, u32[]{:S(2)}) collective-permute-start(bf16[3,128,128]{2,1,0:T(8,128)(2,1)} %shard_map.87.refs_0_), channel_id=1, source_target_pairs={{4,0},{6,2},{0,4},{2,6},{5,1},{7,3},{1,5},{3,7},{12,8},{14,10},{8,... | collective-permute-start | bytes 294920 | tf_op jit(solution)/shard_map/ppermute | solution.py:332
  6.8 1.2 %collective-permute-start = (bf16[3,128,128]{2,1,0:T(8,128)(2,1)}, bf16[3,128,128]{2,1,0:T(8,128)(2,1)S(1)}, u32[]{:S(2)}, u32[]{:S(2)}) collective-permute-start(bf16[3,128,128]{2,1,0:T(8,128)(2,1)} %shard_map.87.refs_0_), channel_id=1, source_target_pairs={{2,0},{4,2},{6,4},{0,6},{3,1},{5,3},{7,5},{1,7},{10,8},{12,10},{14... | collective-permute-start | bytes 294920 | tf_op jit(solution)/shard_map/ppermute | solution.py:332
  8.0 3.7 %shard_map.86 = (bf16[16,256,128]{2,1,0:T(8,128)(2,1)}, bf16[32,9,16,128]{3,2,1,0:T(8,128)(2,1)}) custom-call(s32[1]{0:T(128)} %bitcast.2.y_ref, s32[16]{0:T(128)} %bitcast.26, bf16[16,128,256]{2,1,0:T(8,128)(2,1)} %bitcast.24, bf16[16,128,128]{2,1,0:T(8,128)(2,1)} %bitcast.19, bf16[16,128,128]{2,1,0:T(8,128)(2,1)} %bitcast.21, f32[128,256]{1,0:T(8,128)} %bitcast.25), custom_call_target="tpu_custom_call" | custom-call | tf_op jit(solution)/shard_map/pallas_call | solution.py:368
  11.7 8.1 %all-to-all-start = ((bf16[32,144,128]{2,1,0:T(8,128)(2,1)}), bf16[32,144,128]{2,1,0:T(8,128)(2,1)S(1)}, u32[]{:S(2)}, u32[]{:S(2)}) async-start(bf16[32,144,128]{2,1,0:T(8,128)(2,1)} %bitcast.23), calls=%async_computation | async-start | bytes 2359296 | tf_op jit(solution)/shard_map/all_to_all | solution.py:380
  21.9 1.7 %shard_map.89 = (bf16[8,3,128,128]{3,2,1,0:T(8,128)(2,1)S(1)}, bf16[3,128,128]{2,1,0:T(8,128)(2,1)S(1)}, bf16[2,1024,128]{2,1,0:T(8,128)(2,1)S(1)}, f32[8,128]{1,0:T(8,128)S(1)}) custom-call(s32[1]{0:T(128)} %bitcast.10.x_ref, s32[1]{0:T(128)} %bitcast.1.c_ref, bf16[3,128,128]{2,1,0:T(8,128)(2,1)S(1)} %copy-done.3, ...), custom_call_target="tpu_custom_call" | custom-call | bytes 2199560 | tf_op jit(solution)/shard_map/pallas_call | solution.py:316
  23.6 4.6 %collective-permute-start.10 = (bf16[3,128,128]{2,1,0:T(8,128)(2,1)S(1)}, bf16[3,128,128]{2,1,0:T(8,128)(2,1)S(1)}, u32[]{:S(2)}, u32[]{:S(2)}) collective-permute-start(bf16[3,128,128]{2,1,0:T(8,128)(2,1)S(1)} %get-tuple-element.37), channel_id=1, source_target_pairs={{48,0},{56,1},{49,8},{57,9},{0,16},{8,17},{1,24},{9,25},{16,32},{2... | collective-permute-start | bytes 294920 | tf_op jit(solution)/shard_map/ppermute | solution.py:337
  28.2 3.0 %collective-permute-start.9 = (bf16[3,128,128]{2,1,0:T(8,128)(2,1)S(1)}, bf16[3,128,128]{2,1,0:T(8,128)(2,1)S(1)}, u32[]{:S(2)}, u32[]{:S(2)}) collective-permute-start(bf16[3,128,128]{2,1,0:T(8,128)(2,1)S(1)} %get-tuple-element.37), channel_id=1, source_target_pairs={{32,0},{40,1},{33,8},{41,9},{48,16},{56,17},{49,24},{57,25},{0,32}... | collective-permute-start | bytes 294920 | tf_op jit(solution)/shard_map/ppermute | solution.py:337
  31.2 3.0 %collective-permute-start.8 = (bf16[3,128,128]{2,1,0:T(8,128)(2,1)S(1)}, bf16[3,128,128]{2,1,0:T(8,128)(2,1)S(1)}, u32[]{:S(2)}, u32[]{:S(2)}) collective-permute-start(bf16[3,128,128]{2,1,0:T(8,128)(2,1)S(1)} %get-tuple-element.37), channel_id=1, source_target_pairs={{16,0},{24,1},{17,8},{25,9},{32,16},{40,17},{33,24},{41,25},{48,32... | collective-permute-start | bytes 294920 | tf_op jit(solution)/shard_map/ppermute | solution.py:337
  34.2 2.7 %collective-permute-start.7 = (bf16[3,128,128]{2,1,0:T(8,128)(2,1)S(1)}, bf16[3,128,128]{2,1,0:T(8,128)(2,1)S(1)}, u32[]{:S(2)}, u32[]{:S(2)}) collective-permute-start(bf16[3,128,128]{2,1,0:T(8,128)(2,1)S(1)} %get-tuple-element.37), channel_id=1, source_target_pairs={{0,0},{8,1},{1,8},{9,9},{16,16},{24,17},{17,24},{25,25},{32,32},{4... | collective-permute-start | bytes 294920 | tf_op jit(solution)/shard_map/ppermute | solution.py:337
  37.7 1.9 %shard_map.88 = (bf16[8,64,128]{2,1,0:T(8,128)(2,1)}, f32[128,16]{1,0:T(8,128)S(1)}) custom-call(s32[1]{0:T(128)} %bitcast.z_ref, s32[1]{0:T(128)} %bitcast.1.c_ref, bf16[32,9,16,128]{3,2,1,0:T(8,128)(2,1)S(1)} %bitcast.17), custom_call_target="tpu_custom_call" | custom-call | bytes 1318920 | tf_op jit(solution)/shard_map/pallas_call | solution.py:316
  39.7 2.4 %collective-permute-done.7.refs_0_ = bf16[3,128,128]{2,1,0:T(8,128)(2,1)S(1)} collective-permute-done((bf16[3,128,128]{2,1,0:T(8,128)(2,1)S(1)}, bf16[3,128,128]{2,1,0:T(8,128)(2,1)S(1)}, u32[]{:S(2)}, u32[]{:S(2)}) %collective-permute-start.7) | collective-permute-done | bytes 98336 | tf_op jit(solution)/shard_map/ppermute | solution.py:337
  42.2 7.1 %all-to-all-start.1 = ((bf16[8,64,128]{2,1,0:T(8,128)(2,1)}), bf16[8,64,128]{2,1,0:T(8,128)(2,1)S(1)}, u32[]{:S(2)}, u32[]{:S(2)}) async-start(bf16[8,64,128]{2,1,0:T(8,128)(2,1)} %get-tuple-element.38), calls=%async_computation.1 | async-start | bytes 262144 | tf_op jit(solution)/shard_map/all_to_all | solution.py:405
  49.3 1.2 %shard_map.92 = (bf16[2,128,1024]{2,1,0:T(8,128)(2,1)S(1)}, f32[8,128]{1,0:T(8,128)S(1)}) custom-call(bf16[8,3,128,128]{3,2,1,0:T(8,128)(2,1)S(1)} %get-tuple-element.39.m_ref), custom_call_target="tpu_custom_call" | custom-call | bytes 1314816 | tf_op jit(solution)/shard_map/pallas_call | solution.py:316
  50.5 7.3 %all-to-all-done.1.e_ref = bf16[8,64,128]{2,1,0:T(8,128)(2,1)S(1)} async-done(((bf16[8,64,128]{2,1,0:T(8,128)(2,1)}), bf16[8,64,128]{2,1,0:T(8,128)(2,1)S(1)}, u32[]{:S(2)}, u32[]{:S(2)}) %all-to-all-start.1) | async-done | bytes 131104 | tf_op jit(solution)/shard_map/all_to_all | solution.py:405
  57.8 1.1 %shard_map.90 = (f32[8,1024]{1,0:T(8,128)S(1)}, f32[8,24,128]{2,1,0:T(8,128)S(1)}) custom-call(bf16[8,64,128]{2,1,0:T(8,128)(2,1)S(1)} %all-to-all-done.1.e_ref, bf16[8,3,128,128]{3,2,1,0:T(8,128)(2,1)S(1)} %get-tuple-element.39.m_ref, bf16[2,1024,128]{2,1,0:T(8,128)(2,1)S(1)} %get-tuple-element.40.unit_ref, f32[8,128]{1,0:T(8,128)S(1)} %get-tuple-element.41.top_ref), custom_call_target="tpu_custom_call" | custom-call | bytes 1576960 | tf_op jit(solution)/shard_map/pallas_call | solution.py:316
  59.0 10.0 %all_to_all.25.ends_ref = f32[8,24,128]{2,1,0:T(8,128)S(1)} all-to-all(f32[8,24,128]{2,1,0:T(8,128)S(1)} %get-tuple-element.49), channel_id=1, replica_groups=mesh['y'=4,'z'=8,'x'=4,'c'=2] {'z'}, dimensions={0} | all-to-all | bytes 196608 | tf_op jit(solution)/shard_map/all_to_all | solution.py:419
  68.9 2.3 %shard_map.93 = bf16[8,64,128]{2,1,0:T(8,128)(2,1)S(1)} custom-call(s32[1]{0:T(128)} %bitcast.z_ref, s32[1]{0:T(128)} %bitcast.1.c_ref, f32[8,24,128]{2,1,0:T(8,128)S(1)} %all_to_all.25.ends_ref, bf16[4,3,128,128]{3,2,1,0:T(8,128)(2,1)S(1)} %shard_map.91.mine_ref, bf16[4,3,128,128]{3,2,1,0:T(8,128)(2,1)S(1)} %collective-permute-done.11.other_ref, ...), custom_call_target="tpu_custom_call" | custom-call | bytes 2891784 | tf_op jit(solution)/shard_map/pallas_call | solution.py:316
  71.2 10.3 %all_to_all.26.x_ref = bf16[8,64,128]{2,1,0:T(8,128)(2,1)S(1)} all-to-all(bf16[8,64,128]{2,1,0:T(8,128)(2,1)S(1)} %shard_map.93), channel_id=1, replica_groups=mesh['y'=4,'z'=8,'x'=4,'c'=2] {'z'}, dimensions={0} | all-to-all | bytes 262144 | tf_op jit(solution)/shard_map/all_to_all | solution.py:426
  81.6 3.8 %collective-permute-start.12 = (bf16[8,64,128]{2,1,0:T(8,128)(2,1)S(1)}, bf16[8,64,128]{2,1,0:T(8,128)(2,1)S(1)}, u32[]{:S(2)}, u32[]{:S(2)}) collective-permute-start(bf16[8,64,128]{2,1,0:T(8,128)(2,1)S(1)} %all_to_all.26.x_ref), channel_id=1, source_target_pairs={{1,0},{0,1},{3,2},{2,3},{5,4},{4,5},{7,6},{6,7},{9,8},{8,9},{11,10... | collective-permute-start | bytes 393224 | tf_op jit(solution)/shard_map/ppermute | solution.py:332
  85.4 1.0 collective-permute-done.12.other_ref
  87.2 21.6 %all_to_all.27 = bf16[16,272,128]{2,1,0:T(8,128)(2,1)S(1)} all-to-all(bf16[16,272,128]{2,1,0:T(8,128)(2,1)S(1)} %bitcast.18), channel_id=1, replica_groups=mesh['y'=4,'z'=8,'x'=4,'c'=2] {'y','x'}, dimensions={0} | all-to-all | bytes 2228224 | tf_op jit(solution)/shard_map/all_to_all | solution.py:433
  108.8 2.4 %shard_map.95 = (bf16[16,128,256]{2,1,0:T(8,128)(2,1)}, f32[128,256]{1,0:T(8,128)}) custom-call(bf16[16,17,16,128]{3,2,1,0:T(8,128)(2,1)S(1)} %bitcast.15, bf16[16,17,16,128]{3,2,1,0:T(8,128)(2,1)S(1)} %bitcast.16, bf16[16,256,128]{2,1,0:T(8,128)(2,1)S(1)} %copy-done.2, bf16[16,128,128]{2,1,0:T(8,128)(2,1)S(1)} %bitcast.20, bf16[16,128,128]{2,1,0:T(8,128)(2,1)S(1)} %bitcast.22), custom_call_target="tpu_custom_call" | custom-call | tf_op jit(solution)/shard_map/pallas_call | solution.py:437
  (27 shorter events, 3.9 us)
Async XLA Ops:
  2.3 9.3 %collective-permute-start.2 = (bf16[3,128,128]{2,1,0:T(8,128)(2,1)}, bf16[3,128,128]{2,1,0:T(8,128)(2,1)S(1)}, u32[]{:S(2)}, u32[]{:S(2)}) collective-permute-start(bf16[3,128,128]{2,1,0:T(8,128)(2,1)} %shard_map.87.refs_0_), channel_id=1, source_target_pairs={{6,0},{0,2},{2,4},{4,6},{7,1},{1,3},{3,5},{5,7},{14,8},{8,10},{10,... | collective-permute-start | bytes 294920 | tf_op jit(solution)/shard_map/ppermute | solution.py:332
  4.4 7.3 %collective-permute-start.1 = (bf16[3,128,128]{2,1,0:T(8,128)(2,1)}, bf16[3,128,128]{2,1,0:T(8,128)(2,1)S(1)}, u32[]{:S(2)}, u32[]{:S(2)}) collective-permute-start(bf16[3,128,128]{2,1,0:T(8,128)(2,1)} %shard_map.87.refs_0_), channel_id=1, source_target_pairs={{4,0},{6,2},{0,4},{2,6},{5,1},{7,3},{1,5},{3,7},{12,8},{14,10},{8,... | collective-permute-start | bytes 294920 | tf_op jit(solution)/shard_map/ppermute | solution.py:332
  6.8 4.8 %collective-permute-start = (bf16[3,128,128]{2,1,0:T(8,128)(2,1)}, bf16[3,128,128]{2,1,0:T(8,128)(2,1)S(1)}, u32[]{:S(2)}, u32[]{:S(2)}) collective-permute-start(bf16[3,128,128]{2,1,0:T(8,128)(2,1)} %shard_map.87.refs_0_), channel_id=1, source_target_pairs={{2,0},{4,2},{6,4},{0,6},{3,1},{5,3},{7,5},{1,7},{10,8},{12,10},{14... | collective-permute-start | bytes 294920 | tf_op jit(solution)/shard_map/ppermute | solution.py:332
  11.7 8.1 %copy-start.3 = (bf16[3,128,128]{2,1,0:T(8,128)(2,1)S(1)}, bf16[3,128,128]{2,1,0:T(8,128)(2,1)}, u32[]{:S(2)}) copy-start(bf16[3,128,128]{2,1,0:T(8,128)(2,1)} %shard_map.87.refs_0_) | copy-start | bytes 294916
  11.7 26.1 %all-to-all-start = ((bf16[32,144,128]{2,1,0:T(8,128)(2,1)}), bf16[32,144,128]{2,1,0:T(8,128)(2,1)S(1)}, u32[]{:S(2)}, u32[]{:S(2)}) async-start(bf16[32,144,128]{2,1,0:T(8,128)(2,1)} %bitcast.23), calls=%async_computation | async-start | bytes 2359296 | tf_op jit(solution)/shard_map/all_to_all | solution.py:380
  19.8 1.4 %collective-permute-start.3 = (bf16[3,128,128]{2,1,0:T(8,128)(2,1)S(1)}, bf16[3,128,128]{2,1,0:T(8,128)(2,1)S(1)}, u32[]{:S(2)}, u32[]{:S(2)}) collective-permute-start(bf16[3,128,128]{2,1,0:T(8,128)(2,1)S(1)} %copy-done.3), channel_id=1, source_target_pairs={{1,0},{0,1},{3,2},{2,3},{5,4},{4,5},{7,6},{6,7},{9,8},{8,9},{11,10... | collective-permute-start | bytes 294920 | tf_op jit(solution)/shard_map/ppermute | solution.py:332
  20.1 1.3 %collective-permute-start.4 = (bf16[3,128,128]{2,1,0:T(8,128)(2,1)S(1)}, bf16[3,128,128]{2,1,0:T(8,128)(2,1)S(1)}, u32[]{:S(2)}, u32[]{:S(2)}) collective-permute-start(bf16[3,128,128]{2,1,0:T(8,128)(2,1)S(1)} %collective-permute-done.refs_1_), channel_id=1, source_target_pairs={{1,0},{0,1},{3,2},{2,3},{5,4},{4,5},{7,6},{6,7},{9,8},{8,9},{11,10... | collective-permute-start | bytes 294920 | tf_op jit(solution)/shard_map/ppermute | solution.py:332
  20.4 1.3 %collective-permute-start.5 = (bf16[3,128,128]{2,1,0:T(8,128)(2,1)S(1)}, bf16[3,128,128]{2,1,0:T(8,128)(2,1)S(1)}, u32[]{:S(2)}, u32[]{:S(2)}) collective-permute-start(bf16[3,128,128]{2,1,0:T(8,128)(2,1)S(1)} %collective-permute-done.1.refs_2_), channel_id=1, source_target_pairs={{1,0},{0,1},{3,2},{2,3},{5,4},{4,5},{7,6},{6,7},{9,8},{8,9},{11,10... | collective-permute-start | bytes 294920 | tf_op jit(solution)/shard_map/ppermute | solution.py:332
  20.6 1.3 %collective-permute-start.6 = (bf16[3,128,128]{2,1,0:T(8,128)(2,1)S(1)}, bf16[3,128,128]{2,1,0:T(8,128)(2,1)S(1)}, u32[]{:S(2)}, u32[]{:S(2)}) collective-permute-start(bf16[3,128,128]{2,1,0:T(8,128)(2,1)S(1)} %collective-permute-done.2.refs_3_), channel_id=1, source_target_pairs={{1,0},{0,1},{3,2},{2,3},{5,4},{4,5},{7,6},{6,7},{9,8},{8,9},{11,10... | collective-permute-start | bytes 294920 | tf_op jit(solution)/shard_map/ppermute | solution.py:332
  23.6 16.1 %collective-permute-start.10 = (bf16[3,128,128]{2,1,0:T(8,128)(2,1)S(1)}, bf16[3,128,128]{2,1,0:T(8,128)(2,1)S(1)}, u32[]{:S(2)}, u32[]{:S(2)}) collective-permute-start(bf16[3,128,128]{2,1,0:T(8,128)(2,1)S(1)} %get-tuple-element.37), channel_id=1, source_target_pairs={{48,0},{56,1},{49,8},{57,9},{0,16},{8,17},{1,24},{9,25},{16,32},{2... | collective-permute-start | bytes 294920 | tf_op jit(solution)/shard_map/ppermute | solution.py:337
  28.2 11.5 %collective-permute-start.9 = (bf16[3,128,128]{2,1,0:T(8,128)(2,1)S(1)}, bf16[3,128,128]{2,1,0:T(8,128)(2,1)S(1)}, u32[]{:S(2)}, u32[]{:S(2)}) collective-permute-start(bf16[3,128,128]{2,1,0:T(8,128)(2,1)S(1)} %get-tuple-element.37), channel_id=1, source_target_pairs={{32,0},{40,1},{33,8},{41,9},{48,16},{56,17},{49,24},{57,25},{0,32}... | collective-permute-start | bytes 294920 | tf_op jit(solution)/shard_map/ppermute | solution.py:337
  31.2 8.5 %collective-permute-start.8 = (bf16[3,128,128]{2,1,0:T(8,128)(2,1)S(1)}, bf16[3,128,128]{2,1,0:T(8,128)(2,1)S(1)}, u32[]{:S(2)}, u32[]{:S(2)}) collective-permute-start(bf16[3,128,128]{2,1,0:T(8,128)(2,1)S(1)} %get-tuple-element.37), channel_id=1, source_target_pairs={{16,0},{24,1},{17,8},{25,9},{32,16},{40,17},{33,24},{41,25},{48,32... | collective-permute-start | bytes 294920 | tf_op jit(solution)/shard_map/ppermute | solution.py:337
  34.2 7.9 %collective-permute-start.7 = (bf16[3,128,128]{2,1,0:T(8,128)(2,1)S(1)}, bf16[3,128,128]{2,1,0:T(8,128)(2,1)S(1)}, u32[]{:S(2)}, u32[]{:S(2)}) collective-permute-start(bf16[3,128,128]{2,1,0:T(8,128)(2,1)S(1)} %get-tuple-element.37), channel_id=1, source_target_pairs={{0,0},{8,1},{1,8},{9,9},{16,16},{24,17},{17,24},{25,25},{32,32},{4... | collective-permute-start | bytes 294920 | tf_op jit(solution)/shard_map/ppermute | solution.py:337
  42.1 16.9 %collective-permute-start.11 = (bf16[4,3,128,128]{3,2,1,0:T(8,128)(2,1)S(1)}, bf16[4,3,128,128]{3,2,1,0:T(8,128)(2,1)S(1)}, u32[]{:S(2)}, u32[]{:S(2)}) collective-permute-start(bf16[4,3,128,128]{3,2,1,0:T(8,128)(2,1)S(1)} %shard_map.91.mine_ref), channel_id=1, source_target_pairs={{1,0},{0,1},{3,2},{2,3},{5,4},{4,5},{7,6},{6,7},{9,8},{8,9},{11,10... | collective-permute-start | bytes 1179656 | tf_op jit(solution)/shard_map/ppermute | solution.py:332
  42.2 15.6 %all-to-all-start.1 = ((bf16[8,64,128]{2,1,0:T(8,128)(2,1)}), bf16[8,64,128]{2,1,0:T(8,128)(2,1)S(1)}, u32[]{:S(2)}, u32[]{:S(2)}) async-start(bf16[8,64,128]{2,1,0:T(8,128)(2,1)} %get-tuple-element.38), calls=%async_computation.1 | async-start | bytes 262144 | tf_op jit(solution)/shard_map/all_to_all | solution.py:405
  81.6 4.8 %collective-permute-start.12 = (bf16[8,64,128]{2,1,0:T(8,128)(2,1)S(1)}, bf16[8,64,128]{2,1,0:T(8,128)(2,1)S(1)}, u32[]{:S(2)}, u32[]{:S(2)}) collective-permute-start(bf16[8,64,128]{2,1,0:T(8,128)(2,1)S(1)} %all_to_all.26.x_ref), channel_id=1, source_target_pairs={{1,0},{0,1},{3,2},{2,3},{5,4},{4,5},{7,6},{6,7},{9,8},{8,9},{11,10... | collective-permute-start | bytes 393224 | tf_op jit(solution)/shard_map/ppermute | solution.py:332
  87.2 21.7 %copy-start = (bf16[1,16,128,128]{3,2,1,0:T(8,128)(2,1)S(1)}, bf16[1,16,128,128]{3,2,1,0:T(8,128)(2,1)}, u32[]{:S(2)}) copy-start(bf16[1,16,128,128]{3,2,1,0:T(8,128)(2,1)} %param.8) | copy-start | bytes 1572868
  87.2 21.7 %copy-start.1 = (bf16[1,16,128,128]{3,2,1,0:T(8,128)(2,1)S(1)}, bf16[1,16,128,128]{3,2,1,0:T(8,128)(2,1)}, u32[]{:S(2)}) copy-start(bf16[1,16,128,128]{3,2,1,0:T(8,128)(2,1)} %param.9) | copy-start | bytes 1572868
  87.2 21.7 %copy-start.2 = (bf16[16,256,128]{2,1,0:T(8,128)(2,1)S(1)}, bf16[16,256,128]{2,1,0:T(8,128)(2,1)}, u32[]{:S(2)}) copy-start(bf16[16,256,128]{2,1,0:T(8,128)(2,1)} %get-tuple-element.55.fwd_ref) | copy-start | bytes 3145732

commit v6 on v5

--- a/solution.py
+++ b/solution.py
@@ -14,7 +14,7 @@
 CORE_AXES = ("y", "x", "c")
 STEP_SCALE = 2.0**-8
 COLS = 8
-LEAF_STEP = 8
+LEAF_STEP = 16
 
 
 def dot_nn(a, b):
@@ -141,11 +141,11 @@
     top_ref[...] = jnp.full(top_ref.shape, top, F32)
 
 
-def order_kernel(z_ref, *refs):
+def order_kernel(steps, z_ref, *refs):
     out_ref = refs[-1]
     count = out_ref.shape[0]
-    for d in range(count):
-        out_ref[lax.rem(z_ref[0] // 2 + d, count)] = refs[d][...]
+    for i, d in enumerate(steps):
+        out_ref[lax.rem(z_ref[0] // 2 + d, count)] = refs[i][...]
 
 
 def densify_kernel(plane_size, z_ref, c_ref, v_ref, dense_ref, code_ref, acc_ref):
@@ -390,7 +390,8 @@
             sds((COLS, width), F32),
         ],
     )
-    packs = [every_other(pack, d) for d in range(planes // 2)]
+    steps = sorted(range(planes // 2), key=lambda d: -abs(d - planes // 4))
+    packs = [every_other(pack, d) for d in steps]
 
     dense, codes = call(
         functools.partial(densify_kernel, plane_size),
@@ -403,7 +404,7 @@
     )
     dense, *packs = lax.optimization_barrier((dense, *packs))
     sums = lax.all_to_all(dense, "z", 0, 0, tiled=True)
-    (own_packs,) = call(order_kernel, (z_index, *packs), [sds((planes // 2, 3, width, width), BF16)])
+    (own_packs,) = call(functools.partial(order_kernel, steps), (z_index, *packs), [sds((planes // 2, 3, width, width), BF16)])
     other_packs = shift(own_packs, "c", 1)
     late, late_top = call(
         late_kernel,

time: 112 us -> 110 us (0.982)
  waiting for transfers between devices: 12.5 us -> 10.7 us
  starting transfers between devices: 39.2 us -> 41 us
  blocking collectives: 41.9 us -> 40.2 us
    all_to_all x1, blocking collectives: 21.6 us -> 20 us  [local(): lax.all_to_all(answer.reshape(peers, -1, width), PLANE_AXES, 0, 0, tiled=...]
where the time goes in v6:
time: 110 us; the launch traced here: 109 us
  starting transfers between devices  41 us (37%)
  blocking collectives  40.2 us (37%)
  Pallas kernels  16.4 us (15%)
  waiting for transfers between devices  10.7 us (10%)
    all_to_all x1, blocking collectives, local(): lax.all_to_all(answer.reshape(peers, -1, width), PLANE_AXES, 0, 0, tiled=...  20 us
    ppermute x4, starting transfers between devices, every_other(): lax.ppermute(value, ('z', 'c'), [(2 * (2 * ((z // 2 + by) % half) + c) +...  14.2 us
    pallas_call x8, Pallas kernels, call(): pl.pallas_call(kernel, out_shape=outs, in_specs=[SMEM if a.dtype == jnp.i...  10.9 us
    ppermute x9, starting transfers between devices, shift(): lax.ppermute(value, axis, [((i + by) % size, i) for i in range(size)])  10.7 us
    all_to_all x1, blocking collectives, local(): all_x = lax.all_to_all(x_rows, 'z', 0, 0, tiled=True)  10.3 us
    all_to_all x1, blocking collectives, local(): all_ends = lax.all_to_all(ends, 'z', 0, 0, tiled=True)  9.96 us
    all_to_all x1, starting transfers between devices, local(): lax.all_to_all(send.reshape(both_peers, -1, width), CORE_AXES, 0, 0, tile...  8.07 us
    all_to_all x1, starting transfers between devices, local(): sums = lax.all_to_all(dense, 'z', 0, 0, tiled=True)  8 us
  transfers between devices with their start and end apart: 15, of which 8 were waited for; matrix products, arithmetic and copies ran while one was open for 0% of the time, Pallas kernels for 9%

profile of v6, /device:TPU:1, one launch (start us, length us, event | category | flops | bytes accessed | tf_op | source)
XLA Modules:
  0.0 109.0 jit_solution(15578274566290858263)
XLA Ops:
  0.6 1.7 %shard_map.87.refs_0_ = bf16[3,128,128]{2,1,0:T(8,128)(2,1)} custom-call(f32[1,128,128]{2,1,0:T(8,128)} %inv_ref.1, f32[1,128,128]{2,1,0:T(8,128)} %cpl_ref.1), custom_call_target="tpu_custom_call" | custom-call | bytes 229376 | tf_op jit(solution)/shard_map/pallas_call | solution.py:316
  2.3 2.0 %collective-permute-start.2 = (bf16[3,128,128]{2,1,0:T(8,128)(2,1)}, bf16[3,128,128]{2,1,0:T(8,128)(2,1)S(1)}, u32[]{:S(2)}, u32[]{:S(2)}) collective-permute-start(bf16[3,128,128]{2,1,0:T(8,128)(2,1)} %shard_map.87.refs_0_), channel_id=1, source_target_pairs={{6,0},{0,2},{2,4},{4,6},{7,1},{1,3},{3,5},{5,7},{14,8},{8,10},{10,... | collective-permute-start | bytes 294920 | tf_op jit(solution)/shard_map/ppermute | solution.py:332
  4.4 2.5 %collective-permute-start.1 = (bf16[3,128,128]{2,1,0:T(8,128)(2,1)}, bf16[3,128,128]{2,1,0:T(8,128)(2,1)S(1)}, u32[]{:S(2)}, u32[]{:S(2)}) collective-permute-start(bf16[3,128,128]{2,1,0:T(8,128)(2,1)} %shard_map.87.refs_0_), channel_id=1, source_target_pairs={{4,0},{6,2},{0,4},{2,6},{5,1},{7,3},{1,5},{3,7},{12,8},{14,10},{8,... | collective-permute-start | bytes 294920 | tf_op jit(solution)/shard_map/ppermute | solution.py:332
  6.8 1.2 %collective-permute-start = (bf16[3,128,128]{2,1,0:T(8,128)(2,1)}, bf16[3,128,128]{2,1,0:T(8,128)(2,1)S(1)}, u32[]{:S(2)}, u32[]{:S(2)}) collective-permute-start(bf16[3,128,128]{2,1,0:T(8,128)(2,1)} %shard_map.87.refs_0_), channel_id=1, source_target_pairs={{2,0},{4,2},{6,4},{0,6},{3,1},{5,3},{7,5},{1,7},{10,8},{12,10},{14... | collective-permute-start | bytes 294920 | tf_op jit(solution)/shard_map/ppermute | solution.py:332
  8.0 3.7 %shard_map.86 = (bf16[16,256,128]{2,1,0:T(8,128)(2,1)}, bf16[32,9,16,128]{3,2,1,0:T(8,128)(2,1)}) custom-call(s32[1]{0:T(128)} %bitcast.2.y_ref, s32[16]{0:T(128)} %bitcast.26, bf16[16,128,256]{2,1,0:T(8,128)(2,1)} %bitcast.24, bf16[16,128,128]{2,1,0:T(8,128)(2,1)} %bitcast.19, bf16[16,128,128]{2,1,0:T(8,128)(2,1)} %bitcast.21, f32[128,256]{1,0:T(8,128)} %bitcast.25), custom_call_target="tpu_custom_call" | custom-call | tf_op jit(solution)/shard_map/pallas_call | solution.py:368
  11.7 8.1 %all-to-all-start = ((bf16[32,144,128]{2,1,0:T(8,128)(2,1)}), bf16[32,144,128]{2,1,0:T(8,128)(2,1)S(1)}, u32[]{:S(2)}, u32[]{:S(2)}) async-start(bf16[32,144,128]{2,1,0:T(8,128)(2,1)} %bitcast.23), calls=%async_computation | async-start | bytes 2359296 | tf_op jit(solution)/shard_map/all_to_all | solution.py:380
  21.9 1.7 %shard_map.89 = (bf16[8,3,128,128]{3,2,1,0:T(8,128)(2,1)S(1)}, bf16[3,128,128]{2,1,0:T(8,128)(2,1)S(1)}, bf16[2,1024,128]{2,1,0:T(8,128)(2,1)S(1)}, f32[8,128]{1,0:T(8,128)S(1)}) custom-call(s32[1]{0:T(128)} %bitcast.10.x_ref, s32[1]{0:T(128)} %bitcast.1.c_ref, bf16[3,128,128]{2,1,0:T(8,128)(2,1)S(1)} %copy-done.3, ...), custom_call_target="tpu_custom_call" | custom-call | bytes 2199560 | tf_op jit(solution)/shard_map/pallas_call | solution.py:316
  23.6 6.7 %collective-permute-start.10 = (bf16[3,128,128]{2,1,0:T(8,128)(2,1)S(1)}, bf16[3,128,128]{2,1,0:T(8,128)(2,1)S(1)}, u32[]{:S(2)}, u32[]{:S(2)}) collective-permute-start(bf16[3,128,128]{2,1,0:T(8,128)(2,1)S(1)} %get-tuple-element.37), channel_id=1, source_target_pairs={{32,0},{40,1},{33,8},{41,9},{48,16},{56,17},{49,24},{57,25},{0,32}... | collective-permute-start | bytes 294920 | tf_op jit(solution)/shard_map/ppermute | solution.py:337
  30.3 1.8 %collective-permute-start.9 = (bf16[3,128,128]{2,1,0:T(8,128)(2,1)S(1)}, bf16[3,128,128]{2,1,0:T(8,128)(2,1)S(1)}, u32[]{:S(2)}, u32[]{:S(2)}) collective-permute-start(bf16[3,128,128]{2,1,0:T(8,128)(2,1)S(1)} %get-tuple-element.37), channel_id=1, source_target_pairs={{48,0},{56,1},{49,8},{57,9},{0,16},{8,17},{1,24},{9,25},{16,32},{2... | collective-permute-start | bytes 294920 | tf_op jit(solution)/shard_map/ppermute | solution.py:337
  32.1 1.2 %collective-permute-start.8 = (bf16[3,128,128]{2,1,0:T(8,128)(2,1)S(1)}, bf16[3,128,128]{2,1,0:T(8,128)(2,1)S(1)}, u32[]{:S(2)}, u32[]{:S(2)}) collective-permute-start(bf16[3,128,128]{2,1,0:T(8,128)(2,1)S(1)} %get-tuple-element.37), channel_id=1, source_target_pairs={{16,0},{24,1},{17,8},{25,9},{32,16},{40,17},{33,24},{41,25},{48,32... | collective-permute-start | bytes 294920 | tf_op jit(solution)/shard_map/ppermute | solution.py:337
  33.3 4.5 %collective-permute-start.7 = (bf16[3,128,128]{2,1,0:T(8,128)(2,1)S(1)}, bf16[3,128,128]{2,1,0:T(8,128)(2,1)S(1)}, u32[]{:S(2)}, u32[]{:S(2)}) collective-permute-start(bf16[3,128,128]{2,1,0:T(8,128)(2,1)S(1)} %get-tuple-element.37), channel_id=1, source_target_pairs={{0,0},{8,1},{1,8},{9,9},{16,16},{24,17},{17,24},{25,25},{32,32},{4... | collective-permute-start | bytes 294920 | tf_op jit(solution)/shard_map/ppermute | solution.py:337
  37.9 1.9 %shard_map.88 = (bf16[8,64,128]{2,1,0:T(8,128)(2,1)}, f32[128,16]{1,0:T(8,128)S(1)}) custom-call(s32[1]{0:T(128)} %bitcast.z_ref, s32[1]{0:T(128)} %bitcast.1.c_ref, bf16[32,9,16,128]{3,2,1,0:T(8,128)(2,1)S(1)} %bitcast.17), custom_call_target="tpu_custom_call" | custom-call | bytes 1318920 | tf_op jit(solution)/shard_map/pallas_call | solution.py:316
  40.1 1.1 %collective-permute-done.7.refs_0_ = bf16[3,128,128]{2,1,0:T(8,128)(2,1)S(1)} collective-permute-done((bf16[3,128,128]{2,1,0:T(8,128)(2,1)S(1)}, bf16[3,128,128]{2,1,0:T(8,128)(2,1)S(1)}, u32[]{:S(2)}, u32[]{:S(2)}) %collective-permute-start.7) | collective-permute-done | bytes 98336 | tf_op jit(solution)/shard_map/ppermute | solution.py:337
  41.3 8.0 %all-to-all-start.1 = ((bf16[8,64,128]{2,1,0:T(8,128)(2,1)}), bf16[8,64,128]{2,1,0:T(8,128)(2,1)S(1)}, u32[]{:S(2)}, u32[]{:S(2)}) async-start(bf16[8,64,128]{2,1,0:T(8,128)(2,1)} %get-tuple-element.38), calls=%async_computation.1 | async-start | bytes 262144 | tf_op jit(solution)/shard_map/all_to_all | solution.py:406
  49.3 1.2 %shard_map.92 = (bf16[2,128,1024]{2,1,0:T(8,128)(2,1)S(1)}, f32[8,128]{1,0:T(8,128)S(1)}) custom-call(bf16[8,3,128,128]{3,2,1,0:T(8,128)(2,1)S(1)} %get-tuple-element.39.m_ref), custom_call_target="tpu_custom_call" | custom-call | bytes 1314816 | tf_op jit(solution)/shard_map/pallas_call | solution.py:316
  50.5 7.3 %all-to-all-done.1.e_ref = bf16[8,64,128]{2,1,0:T(8,128)(2,1)S(1)} async-done(((bf16[8,64,128]{2,1,0:T(8,128)(2,1)}), bf16[8,64,128]{2,1,0:T(8,128)(2,1)S(1)}, u32[]{:S(2)}, u32[]{:S(2)}) %all-to-all-start.1) | async-done | bytes 131104 | tf_op jit(solution)/shard_map/all_to_all | solution.py:406
  57.8 1.1 %shard_map.90 = (f32[8,1024]{1,0:T(8,128)S(1)}, f32[8,24,128]{2,1,0:T(8,128)S(1)}) custom-call(bf16[8,64,128]{2,1,0:T(8,128)(2,1)S(1)} %all-to-all-done.1.e_ref, bf16[8,3,128,128]{3,2,1,0:T(8,128)(2,1)S(1)} %get-tuple-element.39.m_ref, bf16[2,1024,128]{2,1,0:T(8,128)(2,1)S(1)} %get-tuple-element.40.unit_ref, f32[8,128]{1,0:T(8,128)S(1)} %get-tuple-element.41.top_ref), custom_call_target="tpu_custom_call" | custom-call | bytes 1576960 | tf_op jit(solution)/shard_map/pallas_call | solution.py:316
  59.0 10.0 %all_to_all.25.ends_ref = f32[8,24,128]{2,1,0:T(8,128)S(1)} all-to-all(f32[8,24,128]{2,1,0:T(8,128)S(1)} %get-tuple-element.49), channel_id=1, replica_groups=mesh['y'=4,'z'=8,'x'=4,'c'=2] {'z'}, dimensions={0} | all-to-all | bytes 196608 | tf_op jit(solution)/shard_map/all_to_all | solution.py:420
  68.9 2.3 %shard_map.93 = bf16[8,64,128]{2,1,0:T(8,128)(2,1)S(1)} custom-call(s32[1]{0:T(128)} %bitcast.z_ref, s32[1]{0:T(128)} %bitcast.1.c_ref, f32[8,24,128]{2,1,0:T(8,128)S(1)} %all_to_all.25.ends_ref, bf16[4,3,128,128]{3,2,1,0:T(8,128)(2,1)S(1)} %shard_map.91.mine_ref, bf16[4,3,128,128]{3,2,1,0:T(8,128)(2,1)S(1)} %collective-permute-done.11.other_ref, ...), custom_call_target="tpu_custom_call" | custom-call | bytes 2891784 | tf_op jit(solution)/shard_map/pallas_call | solution.py:316
  71.2 10.3 %all_to_all.26.x_ref = bf16[8,64,128]{2,1,0:T(8,128)(2,1)S(1)} all-to-all(bf16[8,64,128]{2,1,0:T(8,128)(2,1)S(1)} %shard_map.93), channel_id=1, replica_groups=mesh['y'=4,'z'=8,'x'=4,'c'=2] {'z'}, dimensions={0} | all-to-all | bytes 262144 | tf_op jit(solution)/shard_map/all_to_all | solution.py:427
  81.6 3.8 %collective-permute-start.12 = (bf16[8,64,128]{2,1,0:T(8,128)(2,1)S(1)}, bf16[8,64,128]{2,1,0:T(8,128)(2,1)S(1)}, u32[]{:S(2)}, u32[]{:S(2)}) collective-permute-start(bf16[8,64,128]{2,1,0:T(8,128)(2,1)S(1)} %all_to_all.26.x_ref), channel_id=1, source_target_pairs={{1,0},{0,1},{3,2},{2,3},{5,4},{4,5},{7,6},{6,7},{9,8},{8,9},{11,10... | collective-permute-start | bytes 393224 | tf_op jit(solution)/shard_map/ppermute | solution.py:332
  85.4 1.0 collective-permute-done.12.other_ref
  87.2 20.0 %all_to_all.27 = bf16[16,272,128]{2,1,0:T(8,128)(2,1)S(1)} all-to-all(bf16[16,272,128]{2,1,0:T(8,128)(2,1)S(1)} %bitcast.18), channel_id=1, replica_groups=mesh['y'=4,'z'=8,'x'=4,'c'=2] {'y','x'}, dimensions={0} | all-to-all | bytes 2228224 | tf_op jit(solution)/shard_map/all_to_all | solution.py:434
  107.2 1.8 %shard_map.95 = (bf16[16,128,256]{2,1,0:T(8,128)(2,1)}, f32[128,256]{1,0:T(8,128)}) custom-call(bf16[16,17,16,128]{3,2,1,0:T(8,128)(2,1)S(1)} %bitcast.15, bf16[16,17,16,128]{3,2,1,0:T(8,128)(2,1)S(1)} %bitcast.16, bf16[16,256,128]{2,1,0:T(8,128)(2,1)S(1)} %copy-done.2, bf16[16,128,128]{2,1,0:T(8,128)(2,1)S(1)} %bitcast.20, bf16[16,128,128]{2,1,0:T(8,128)(2,1)S(1)} %bitcast.22), custom_call_target="tpu_custom_call" | custom-call | tf_op jit(solution)/shard_map/pallas_call | solution.py:438
  (27 shorter events, 3.3 us)
Async XLA Ops:
  2.3 9.3 %collective-permute-start.2 = (bf16[3,128,128]{2,1,0:T(8,128)(2,1)}, bf16[3,128,128]{2,1,0:T(8,128)(2,1)S(1)}, u32[]{:S(2)}, u32[]{:S(2)}) collective-permute-start(bf16[3,128,128]{2,1,0:T(8,128)(2,1)} %shard_map.87.refs_0_), channel_id=1, source_target_pairs={{6,0},{0,2},{2,4},{4,6},{7,1},{1,3},{3,5},{5,7},{14,8},{8,10},{10,... | collective-permute-start | bytes 294920 | tf_op jit(solution)/shard_map/ppermute | solution.py:332
  4.4 7.3 %collective-permute-start.1 = (bf16[3,128,128]{2,1,0:T(8,128)(2,1)}, bf16[3,128,128]{2,1,0:T(8,128)(2,1)S(1)}, u32[]{:S(2)}, u32[]{:S(2)}) collective-permute-start(bf16[3,128,128]{2,1,0:T(8,128)(2,1)} %shard_map.87.refs_0_), channel_id=1, source_target_pairs={{4,0},{6,2},{0,4},{2,6},{5,1},{7,3},{1,5},{3,7},{12,8},{14,10},{8,... | collective-permute-start | bytes 294920 | tf_op jit(solution)/shard_map/ppermute | solution.py:332
  6.8 4.8 %collective-permute-start = (bf16[3,128,128]{2,1,0:T(8,128)(2,1)}, bf16[3,128,128]{2,1,0:T(8,128)(2,1)S(1)}, u32[]{:S(2)}, u32[]{:S(2)}) collective-permute-start(bf16[3,128,128]{2,1,0:T(8,128)(2,1)} %shard_map.87.refs_0_), channel_id=1, source_target_pairs={{2,0},{4,2},{6,4},{0,6},{3,1},{5,3},{7,5},{1,7},{10,8},{12,10},{14... | collective-permute-start | bytes 294920 | tf_op jit(solution)/shard_map/ppermute | solution.py:332
  11.7 8.1 %copy-start.3 = (bf16[3,128,128]{2,1,0:T(8,128)(2,1)S(1)}, bf16[3,128,128]{2,1,0:T(8,128)(2,1)}, u32[]{:S(2)}) copy-start(bf16[3,128,128]{2,1,0:T(8,128)(2,1)} %shard_map.87.refs_0_) | copy-start | bytes 294916
  11.7 26.2 %all-to-all-start = ((bf16[32,144,128]{2,1,0:T(8,128)(2,1)}), bf16[32,144,128]{2,1,0:T(8,128)(2,1)S(1)}, u32[]{:S(2)}, u32[]{:S(2)}) async-start(bf16[32,144,128]{2,1,0:T(8,128)(2,1)} %bitcast.23), calls=%async_computation | async-start | bytes 2359296 | tf_op jit(solution)/shard_map/all_to_all | solution.py:380
  19.8 1.4 %collective-permute-start.3 = (bf16[3,128,128]{2,1,0:T(8,128)(2,1)S(1)}, bf16[3,128,128]{2,1,0:T(8,128)(2,1)S(1)}, u32[]{:S(2)}, u32[]{:S(2)}) collective-permute-start(bf16[3,128,128]{2,1,0:T(8,128)(2,1)S(1)} %copy-done.3), channel_id=1, source_target_pairs={{1,0},{0,1},{3,2},{2,3},{5,4},{4,5},{7,6},{6,7},{9,8},{8,9},{11,10... | collective-permute-start | bytes 294920 | tf_op jit(solution)/shard_map/ppermute | solution.py:332
  20.1 1.3 %collective-permute-start.4 = (bf16[3,128,128]{2,1,0:T(8,128)(2,1)S(1)}, bf16[3,128,128]{2,1,0:T(8,128)(2,1)S(1)}, u32[]{:S(2)}, u32[]{:S(2)}) collective-permute-start(bf16[3,128,128]{2,1,0:T(8,128)(2,1)S(1)} %collective-permute-done.refs_1_), channel_id=1, source_target_pairs={{1,0},{0,1},{3,2},{2,3},{5,4},{4,5},{7,6},{6,7},{9,8},{8,9},{11,10... | collective-permute-start | bytes 294920 | tf_op jit(solution)/shard_map/ppermute | solution.py:332
  20.4 1.3 %collective-permute-start.5 = (bf16[3,128,128]{2,1,0:T(8,128)(2,1)S(1)}, bf16[3,128,128]{2,1,0:T(8,128)(2,1)S(1)}, u32[]{:S(2)}, u32[]{:S(2)}) collective-permute-start(bf16[3,128,128]{2,1,0:T(8,128)(2,1)S(1)} %collective-permute-done.1.refs_2_), channel_id=1, source_target_pairs={{1,0},{0,1},{3,2},{2,3},{5,4},{4,5},{7,6},{6,7},{9,8},{8,9},{11,10... | collective-permute-start | bytes 294920 | tf_op jit(solution)/shard_map/ppermute | solution.py:332
  20.6 1.3 %collective-permute-start.6 = (bf16[3,128,128]{2,1,0:T(8,128)(2,1)S(1)}, bf16[3,128,128]{2,1,0:T(8,128)(2,1)S(1)}, u32[]{:S(2)}, u32[]{:S(2)}) collective-permute-start(bf16[3,128,128]{2,1,0:T(8,128)(2,1)S(1)} %collective-permute-done.2.refs_3_), channel_id=1, source_target_pairs={{1,0},{0,1},{3,2},{2,3},{5,4},{4,5},{7,6},{6,7},{9,8},{8,9},{11,10... | collective-permute-start | bytes 294920 | tf_op jit(solution)/shard_map/ppermute | solution.py:332
  23.6 16.2 %collective-permute-start.10 = (bf16[3,128,128]{2,1,0:T(8,128)(2,1)S(1)}, bf16[3,128,128]{2,1,0:T(8,128)(2,1)S(1)}, u32[]{:S(2)}, u32[]{:S(2)}) collective-permute-start(bf16[3,128,128]{2,1,0:T(8,128)(2,1)S(1)} %get-tuple-element.37), channel_id=1, source_target_pairs={{32,0},{40,1},{33,8},{41,9},{48,16},{56,17},{49,24},{57,25},{0,32}... | collective-permute-start | bytes 294920 | tf_op jit(solution)/shard_map/ppermute | solution.py:337
  30.3 9.5 %collective-permute-start.9 = (bf16[3,128,128]{2,1,0:T(8,128)(2,1)S(1)}, bf16[3,128,128]{2,1,0:T(8,128)(2,1)S(1)}, u32[]{:S(2)}, u32[]{:S(2)}) collective-permute-start(bf16[3,128,128]{2,1,0:T(8,128)(2,1)S(1)} %get-tuple-element.37), channel_id=1, source_target_pairs={{48,0},{56,1},{49,8},{57,9},{0,16},{8,17},{1,24},{9,25},{16,32},{2... | collective-permute-start | bytes 294920 | tf_op jit(solution)/shard_map/ppermute | solution.py:337
  32.1 8.0 %collective-permute-start.8 = (bf16[3,128,128]{2,1,0:T(8,128)(2,1)S(1)}, bf16[3,128,128]{2,1,0:T(8,128)(2,1)S(1)}, u32[]{:S(2)}, u32[]{:S(2)}) collective-permute-start(bf16[3,128,128]{2,1,0:T(8,128)(2,1)S(1)} %get-tuple-element.37), channel_id=1, source_target_pairs={{16,0},{24,1},{17,8},{25,9},{32,16},{40,17},{33,24},{41,25},{48,32... | collective-permute-start | bytes 294920 | tf_op jit(solution)/shard_map/ppermute | solution.py:337
  33.3 7.9 %collective-permute-start.7 = (bf16[3,128,128]{2,1,0:T(8,128)(2,1)S(1)}, bf16[3,128,128]{2,1,0:T(8,128)(2,1)S(1)}, u32[]{:S(2)}, u32[]{:S(2)}) collective-permute-start(bf16[3,128,128]{2,1,0:T(8,128)(2,1)S(1)} %get-tuple-element.37), channel_id=1, source_target_pairs={{0,0},{8,1},{1,8},{9,9},{16,16},{24,17},{17,24},{25,25},{32,32},{4... | collective-permute-start | bytes 294920 | tf_op jit(solution)/shard_map/ppermute | solution.py:337
  41.2 17.7 %collective-permute-start.11 = (bf16[4,3,128,128]{3,2,1,0:T(8,128)(2,1)S(1)}, bf16[4,3,128,128]{3,2,1,0:T(8,128)(2,1)S(1)}, u32[]{:S(2)}, u32[]{:S(2)}) collective-permute-start(bf16[4,3,128,128]{3,2,1,0:T(8,128)(2,1)S(1)} %shard_map.91.mine_ref), channel_id=1, source_target_pairs={{1,0},{0,1},{3,2},{2,3},{5,4},{4,5},{7,6},{6,7},{9,8},{8,9},{11,10... | collective-permute-start | bytes 1179656 | tf_op jit(solution)/shard_map/ppermute | solution.py:332
  41.3 16.5 %all-to-all-start.1 = ((bf16[8,64,128]{2,1,0:T(8,128)(2,1)}), bf16[8,64,128]{2,1,0:T(8,128)(2,1)S(1)}, u32[]{:S(2)}, u32[]{:S(2)}) async-start(bf16[8,64,128]{2,1,0:T(8,128)(2,1)} %get-tuple-element.38), calls=%async_computation.1 | async-start | bytes 262144 | tf_op jit(solution)/shard_map/all_to_all | solution.py:406
  81.6 4.8 %collective-permute-start.12 = (bf16[8,64,128]{2,1,0:T(8,128)(2,1)S(1)}, bf16[8,64,128]{2,1,0:T(8,128)(2,1)S(1)}, u32[]{:S(2)}, u32[]{:S(2)}) collective-permute-start(bf16[8,64,128]{2,1,0:T(8,128)(2,1)S(1)} %all_to_all.26.x_ref), channel_id=1, source_target_pairs={{1,0},{0,1},{3,2},{2,3},{5,4},{4,5},{7,6},{6,7},{9,8},{8,9},{11,10... | collective-permute-start | bytes 393224 | tf_op jit(solution)/shard_map/ppermute | solution.py:332
  87.2 20.0 %copy-start = (bf16[1,16,128,128]{3,2,1,0:T(8,128)(2,1)S(1)}, bf16[1,16,128,128]{3,2,1,0:T(8,128)(2,1)}, u32[]{:S(2)}) copy-start(bf16[1,16,128,128]{3,2,1,0:T(8,128)(2,1)} %param.8) | copy-start | bytes 1572868
  87.2 20.0 %copy-start.1 = (bf16[1,16,128,128]{3,2,1,0:T(8,128)(2,1)S(1)}, bf16[1,16,128,128]{3,2,1,0:T(8,128)(2,1)}, u32[]{:S(2)}) copy-start(bf16[1,16,128,128]{3,2,1,0:T(8,128)(2,1)} %param.9) | copy-start | bytes 1572868
  87.2 20.0 %copy-start.2 = (bf16[16,256,128]{2,1,0:T(8,128)(2,1)S(1)}, bf16[16,256,128]{2,1,0:T(8,128)(2,1)}, u32[]{:S(2)}) copy-start(bf16[16,256,128]{2,1,0:T(8,128)(2,1)} %get-tuple-element.55.fwd_ref) | copy-start | bytes 3145732

commit v7 on v6

--- a/solution.py
+++ b/solution.py
@@ -78,7 +78,7 @@
 
 def own_pair_kernel(inv_ref, cpl_ref, out_ref):
     inverse = inv_ref[0]
-    out_ref[0], out_ref[1] = split(dot_nn(inverse, cpl_ref[0]))
+    out_ref[0], out_ref[1] = split(rows_nn(inverse, *split(cpl_ref[0])))
     out_ref[2] = inverse.astype(BF16)
 
 

time: 110 us -> 109 us (level)
  no operation moved by 1% of the time
where the time goes in v7:
time: 109 us
  starting transfers between devices  40.9 us (38%)
  blocking collectives  40.2 us (37%)
  Pallas kernels  16.3 us (15%)
  waiting for transfers between devices  10.7 us (10%)
    all_to_all x1, blocking collectives, local(): lax.all_to_all(answer.reshape(peers, -1, width), PLANE_AXES, 0, 0, tiled=...  20 us
    ppermute x4, starting transfers between devices, every_other(): lax.ppermute(value, ('z', 'c'), [(2 * (2 * ((z // 2 + by) % half) + c) +...  14.2 us
    pallas_call x8, Pallas kernels, call(): pl.pallas_call(kernel, out_shape=outs, in_specs=[SMEM if a.dtype == jnp.i...  10.8 us
    ppermute x9, starting transfers between devices, shift(): lax.ppermute(value, axis, [((i + by) % size, i) for i in range(size)])  10.7 us
    all_to_all x1, blocking collectives, local(): all_x = lax.all_to_all(x_rows, 'z', 0, 0, tiled=True)  10.3 us
    all_to_all x1, blocking collectives, local(): all_ends = lax.all_to_all(ends, 'z', 0, 0, tiled=True)  9.96 us
    all_to_all x1, starting transfers between devices, local(): lax.all_to_all(send.reshape(both_peers, -1, width), CORE_AXES, 0, 0, tile...  8.07 us
    all_to_all x1, starting transfers between devices, local(): sums = lax.all_to_all(dense, 'z', 0, 0, tiled=True)  7.99 us
  transfers between devices with their start and end apart: 15, of which 8 were waited for; matrix products, arithmetic and copies ran while one was open for 0% of the time, Pallas kernels for 9%

profile of v7, /device:TPU:1, one launch (start us, length us, event | category | flops | bytes accessed | tf_op | source)
XLA Modules:
  0.0 109.0 jit_solution(9257951643614155381)
XLA Ops:
  0.6 1.7 %shard_map.87.refs_0_ = bf16[3,128,128]{2,1,0:T(8,128)(2,1)} custom-call(f32[1,128,128]{2,1,0:T(8,128)} %inv_ref.1, f32[1,128,128]{2,1,0:T(8,128)} %cpl_ref.1), custom_call_target="tpu_custom_call" | custom-call | bytes 229376 | tf_op jit(solution)/shard_map/pallas_call | solution.py:316
  2.3 2.0 %collective-permute-start.2 = (bf16[3,128,128]{2,1,0:T(8,128)(2,1)}, bf16[3,128,128]{2,1,0:T(8,128)(2,1)S(1)}, u32[]{:S(2)}, u32[]{:S(2)}) collective-permute-start(bf16[3,128,128]{2,1,0:T(8,128)(2,1)} %shard_map.87.refs_0_), channel_id=1, source_target_pairs={{6,0},{0,2},{2,4},{4,6},{7,1},{1,3},{3,5},{5,7},{14,8},{8,10},{10,... | collective-permute-start | bytes 294920 | tf_op jit(solution)/shard_map/ppermute | solution.py:332
  4.4 2.4 %collective-permute-start.1 = (bf16[3,128,128]{2,1,0:T(8,128)(2,1)}, bf16[3,128,128]{2,1,0:T(8,128)(2,1)S(1)}, u32[]{:S(2)}, u32[]{:S(2)}) collective-permute-start(bf16[3,128,128]{2,1,0:T(8,128)(2,1)} %shard_map.87.refs_0_), channel_id=1, source_target_pairs={{4,0},{6,2},{0,4},{2,6},{5,1},{7,3},{1,5},{3,7},{12,8},{14,10},{8,... | collective-permute-start | bytes 294920 | tf_op jit(solution)/shard_map/ppermute | solution.py:332
  6.8 1.2 %collective-permute-start = (bf16[3,128,128]{2,1,0:T(8,128)(2,1)}, bf16[3,128,128]{2,1,0:T(8,128)(2,1)S(1)}, u32[]{:S(2)}, u32[]{:S(2)}) collective-permute-start(bf16[3,128,128]{2,1,0:T(8,128)(2,1)} %shard_map.87.refs_0_), channel_id=1, source_target_pairs={{2,0},{4,2},{6,4},{0,6},{3,1},{5,3},{7,5},{1,7},{10,8},{12,10},{14... | collective-permute-start | bytes 294920 | tf_op jit(solution)/shard_map/ppermute | solution.py:332
  8.0 3.7 %shard_map.86 = (bf16[16,256,128]{2,1,0:T(8,128)(2,1)}, bf16[32,9,16,128]{3,2,1,0:T(8,128)(2,1)}) custom-call(s32[1]{0:T(128)} %bitcast.2.y_ref, s32[16]{0:T(128)} %bitcast.26, bf16[16,128,256]{2,1,0:T(8,128)(2,1)} %bitcast.24, bf16[16,128,128]{2,1,0:T(8,128)(2,1)} %bitcast.19, bf16[16,128,128]{2,1,0:T(8,128)(2,1)} %bitcast.21, f32[128,256]{1,0:T(8,128)} %bitcast.25), custom_call_target="tpu_custom_call" | custom-call | tf_op jit(solution)/shard_map/pallas_call | solution.py:368
  11.7 8.1 %all-to-all-start = ((bf16[32,144,128]{2,1,0:T(8,128)(2,1)}), bf16[32,144,128]{2,1,0:T(8,128)(2,1)S(1)}, u32[]{:S(2)}, u32[]{:S(2)}) async-start(bf16[32,144,128]{2,1,0:T(8,128)(2,1)} %bitcast.23), calls=%async_computation | async-start | bytes 2359296 | tf_op jit(solution)/shard_map/all_to_all | solution.py:380
  21.9 1.7 %shard_map.89 = (bf16[8,3,128,128]{3,2,1,0:T(8,128)(2,1)S(1)}, bf16[3,128,128]{2,1,0:T(8,128)(2,1)S(1)}, bf16[2,1024,128]{2,1,0:T(8,128)(2,1)S(1)}, f32[8,128]{1,0:T(8,128)S(1)}) custom-call(s32[1]{0:T(128)} %bitcast.10.x_ref, s32[1]{0:T(128)} %bitcast.1.c_ref, bf16[3,128,128]{2,1,0:T(8,128)(2,1)S(1)} %copy-done.3, ...), custom_call_target="tpu_custom_call" | custom-call | bytes 2199560 | tf_op jit(solution)/shard_map/pallas_call | solution.py:316
  23.6 6.7 %collective-permute-start.10 = (bf16[3,128,128]{2,1,0:T(8,128)(2,1)S(1)}, bf16[3,128,128]{2,1,0:T(8,128)(2,1)S(1)}, u32[]{:S(2)}, u32[]{:S(2)}) collective-permute-start(bf16[3,128,128]{2,1,0:T(8,128)(2,1)S(1)} %get-tuple-element.37), channel_id=1, source_target_pairs={{32,0},{40,1},{33,8},{41,9},{48,16},{56,17},{49,24},{57,25},{0,32}... | collective-permute-start | bytes 294920 | tf_op jit(solution)/shard_map/ppermute | solution.py:337
  30.3 1.8 %collective-permute-start.9 = (bf16[3,128,128]{2,1,0:T(8,128)(2,1)S(1)}, bf16[3,128,128]{2,1,0:T(8,128)(2,1)S(1)}, u32[]{:S(2)}, u32[]{:S(2)}) collective-permute-start(bf16[3,128,128]{2,1,0:T(8,128)(2,1)S(1)} %get-tuple-element.37), channel_id=1, source_target_pairs={{48,0},{56,1},{49,8},{57,9},{0,16},{8,17},{1,24},{9,25},{16,32},{2... | collective-permute-start | bytes 294920 | tf_op jit(solution)/shard_map/ppermute | solution.py:337
  32.1 1.2 %collective-permute-start.8 = (bf16[3,128,128]{2,1,0:T(8,128)(2,1)S(1)}, bf16[3,128,128]{2,1,0:T(8,128)(2,1)S(1)}, u32[]{:S(2)}, u32[]{:S(2)}) collective-permute-start(bf16[3,128,128]{2,1,0:T(8,128)(2,1)S(1)} %get-tuple-element.37), channel_id=1, source_target_pairs={{16,0},{24,1},{17,8},{25,9},{32,16},{40,17},{33,24},{41,25},{48,32... | collective-permute-start | bytes 294920 | tf_op jit(solution)/shard_map/ppermute | solution.py:337
  33.3 4.5 %collective-permute-start.7 = (bf16[3,128,128]{2,1,0:T(8,128)(2,1)S(1)}, bf16[3,128,128]{2,1,0:T(8,128)(2,1)S(1)}, u32[]{:S(2)}, u32[]{:S(2)}) collective-permute-start(bf16[3,128,128]{2,1,0:T(8,128)(2,1)S(1)} %get-tuple-element.37), channel_id=1, source_target_pairs={{0,0},{8,1},{1,8},{9,9},{16,16},{24,17},{17,24},{25,25},{32,32},{4... | collective-permute-start | bytes 294920 | tf_op jit(solution)/shard_map/ppermute | solution.py:337
  37.8 1.9 %shard_map.88 = (bf16[8,64,128]{2,1,0:T(8,128)(2,1)}, f32[128,16]{1,0:T(8,128)S(1)}) custom-call(s32[1]{0:T(128)} %bitcast.z_ref, s32[1]{0:T(128)} %bitcast.1.c_ref, bf16[32,9,16,128]{3,2,1,0:T(8,128)(2,1)S(1)} %bitcast.17), custom_call_target="tpu_custom_call" | custom-call | bytes 1318920 | tf_op jit(solution)/shard_map/pallas_call | solution.py:316
  40.0 1.1 %collective-permute-done.7.refs_0_ = bf16[3,128,128]{2,1,0:T(8,128)(2,1)S(1)} collective-permute-done((bf16[3,128,128]{2,1,0:T(8,128)(2,1)S(1)}, bf16[3,128,128]{2,1,0:T(8,128)(2,1)S(1)}, u32[]{:S(2)}, u32[]{:S(2)}) %collective-permute-start.7) | collective-permute-done | bytes 98336 | tf_op jit(solution)/shard_map/ppermute | solution.py:337
  41.3 8.0 %all-to-all-start.1 = ((bf16[8,64,128]{2,1,0:T(8,128)(2,1)}), bf16[8,64,128]{2,1,0:T(8,128)(2,1)S(1)}, u32[]{:S(2)}, u32[]{:S(2)}) async-start(bf16[8,64,128]{2,1,0:T(8,128)(2,1)} %get-tuple-element.38), calls=%async_computation.1 | async-start | bytes 262144 | tf_op jit(solution)/shard_map/all_to_all | solution.py:406
  49.3 1.2 %shard_map.92 = (bf16[2,128,1024]{2,1,0:T(8,128)(2,1)S(1)}, f32[8,128]{1,0:T(8,128)S(1)}) custom-call(bf16[8,3,128,128]{3,2,1,0:T(8,128)(2,1)S(1)} %get-tuple-element.39.m_ref), custom_call_target="tpu_custom_call" | custom-call | bytes 1314816 | tf_op jit(solution)/shard_map/pallas_call | solution.py:316
  50.5 7.3 %all-to-all-done.1.e_ref = bf16[8,64,128]{2,1,0:T(8,128)(2,1)S(1)} async-done(((bf16[8,64,128]{2,1,0:T(8,128)(2,1)}), bf16[8,64,128]{2,1,0:T(8,128)(2,1)S(1)}, u32[]{:S(2)}, u32[]{:S(2)}) %all-to-all-start.1) | async-done | bytes 131104 | tf_op jit(solution)/shard_map/all_to_all | solution.py:406
  57.8 1.1 %shard_map.90 = (f32[8,1024]{1,0:T(8,128)S(1)}, f32[8,24,128]{2,1,0:T(8,128)S(1)}) custom-call(bf16[8,64,128]{2,1,0:T(8,128)(2,1)S(1)} %all-to-all-done.1.e_ref, bf16[8,3,128,128]{3,2,1,0:T(8,128)(2,1)S(1)} %get-tuple-element.39.m_ref, bf16[2,1024,128]{2,1,0:T(8,128)(2,1)S(1)} %get-tuple-element.40.unit_ref, f32[8,128]{1,0:T(8,128)S(1)} %get-tuple-element.41.top_ref), custom_call_target="tpu_custom_call" | custom-call | bytes 1576960 | tf_op jit(solution)/shard_map/pallas_call | solution.py:316
  58.9 10.0 %all_to_all.25.ends_ref = f32[8,24,128]{2,1,0:T(8,128)S(1)} all-to-all(f32[8,24,128]{2,1,0:T(8,128)S(1)} %get-tuple-element.49), channel_id=1, replica_groups=mesh['y'=4,'z'=8,'x'=4,'c'=2] {'z'}, dimensions={0} | all-to-all | bytes 196608 | tf_op jit(solution)/shard_map/all_to_all | solution.py:420
  68.9 2.3 %shard_map.93 = bf16[8,64,128]{2,1,0:T(8,128)(2,1)S(1)} custom-call(s32[1]{0:T(128)} %bitcast.z_ref, s32[1]{0:T(128)} %bitcast.1.c_ref, f32[8,24,128]{2,1,0:T(8,128)S(1)} %all_to_all.25.ends_ref, bf16[4,3,128,128]{3,2,1,0:T(8,128)(2,1)S(1)} %shard_map.91.mine_ref, bf16[4,3,128,128]{3,2,1,0:T(8,128)(2,1)S(1)} %collective-permute-done.11.other_ref, ...), custom_call_target="tpu_custom_call" | custom-call | bytes 2891784 | tf_op jit(solution)/shard_map/pallas_call | solution.py:316
  71.2 10.3 %all_to_all.26.x_ref = bf16[8,64,128]{2,1,0:T(8,128)(2,1)S(1)} all-to-all(bf16[8,64,128]{2,1,0:T(8,128)(2,1)S(1)} %shard_map.93), channel_id=1, replica_groups=mesh['y'=4,'z'=8,'x'=4,'c'=2] {'z'}, dimensions={0} | all-to-all | bytes 262144 | tf_op jit(solution)/shard_map/all_to_all | solution.py:427
  81.5 3.8 %collective-permute-start.12 = (bf16[8,64,128]{2,1,0:T(8,128)(2,1)S(1)}, bf16[8,64,128]{2,1,0:T(8,128)(2,1)S(1)}, u32[]{:S(2)}, u32[]{:S(2)}) collective-permute-start(bf16[8,64,128]{2,1,0:T(8,128)(2,1)S(1)} %all_to_all.26.x_ref), channel_id=1, source_target_pairs={{1,0},{0,1},{3,2},{2,3},{5,4},{4,5},{7,6},{6,7},{9,8},{8,9},{11,10... | collective-permute-start | bytes 393224 | tf_op jit(solution)/shard_map/ppermute | solution.py:332
  85.4 1.0 collective-permute-done.12.other_ref
  87.2 20.0 %all_to_all.27 = bf16[16,272,128]{2,1,0:T(8,128)(2,1)S(1)} all-to-all(bf16[16,272,128]{2,1,0:T(8,128)(2,1)S(1)} %bitcast.18), channel_id=1, replica_groups=mesh['y'=4,'z'=8,'x'=4,'c'=2] {'y','x'}, dimensions={0} | all-to-all | bytes 2228224 | tf_op jit(solution)/shard_map/all_to_all | solution.py:434
  107.2 1.8 %shard_map.95 = (bf16[16,128,256]{2,1,0:T(8,128)(2,1)}, f32[128,256]{1,0:T(8,128)}) custom-call(bf16[16,17,16,128]{3,2,1,0:T(8,128)(2,1)S(1)} %bitcast.15, bf16[16,17,16,128]{3,2,1,0:T(8,128)(2,1)S(1)} %bitcast.16, bf16[16,256,128]{2,1,0:T(8,128)(2,1)S(1)} %copy-done.2, bf16[16,128,128]{2,1,0:T(8,128)(2,1)S(1)} %bitcast.20, bf16[16,128,128]{2,1,0:T(8,128)(2,1)S(1)} %bitcast.22), custom_call_target="tpu_custom_call" | custom-call | tf_op jit(solution)/shard_map/pallas_call | solution.py:438
  (27 shorter events, 3.3 us)
Async XLA Ops:
  2.3 9.3 %collective-permute-start.2 = (bf16[3,128,128]{2,1,0:T(8,128)(2,1)}, bf16[3,128,128]{2,1,0:T(8,128)(2,1)S(1)}, u32[]{:S(2)}, u32[]{:S(2)}) collective-permute-start(bf16[3,128,128]{2,1,0:T(8,128)(2,1)} %shard_map.87.refs_0_), channel_id=1, source_target_pairs={{6,0},{0,2},{2,4},{4,6},{7,1},{1,3},{3,5},{5,7},{14,8},{8,10},{10,... | collective-permute-start | bytes 294920 | tf_op jit(solution)/shard_map/ppermute | solution.py:332
  4.4 7.3 %collective-permute-start.1 = (bf16[3,128,128]{2,1,0:T(8,128)(2,1)}, bf16[3,128,128]{2,1,0:T(8,128)(2,1)S(1)}, u32[]{:S(2)}, u32[]{:S(2)}) collective-permute-start(bf16[3,128,128]{2,1,0:T(8,128)(2,1)} %shard_map.87.refs_0_), channel_id=1, source_target_pairs={{4,0},{6,2},{0,4},{2,6},{5,1},{7,3},{1,5},{3,7},{12,8},{14,10},{8,... | collective-permute-start | bytes 294920 | tf_op jit(solution)/shard_map/ppermute | solution.py:332
  6.8 4.8 %collective-permute-start = (bf16[3,128,128]{2,1,0:T(8,128)(2,1)}, bf16[3,128,128]{2,1,0:T(8,128)(2,1)S(1)}, u32[]{:S(2)}, u32[]{:S(2)}) collective-permute-start(bf16[3,128,128]{2,1,0:T(8,128)(2,1)} %shard_map.87.refs_0_), channel_id=1, source_target_pairs={{2,0},{4,2},{6,4},{0,6},{3,1},{5,3},{7,5},{1,7},{10,8},{12,10},{14... | collective-permute-start | bytes 294920 | tf_op jit(solution)/shard_map/ppermute | solution.py:332
  11.7 8.1 %copy-start.3 = (bf16[3,128,128]{2,1,0:T(8,128)(2,1)S(1)}, bf16[3,128,128]{2,1,0:T(8,128)(2,1)}, u32[]{:S(2)}) copy-start(bf16[3,128,128]{2,1,0:T(8,128)(2,1)} %shard_map.87.refs_0_) | copy-start | bytes 294916
  11.7 26.2 %all-to-all-start = ((bf16[32,144,128]{2,1,0:T(8,128)(2,1)}), bf16[32,144,128]{2,1,0:T(8,128)(2,1)S(1)}, u32[]{:S(2)}, u32[]{:S(2)}) async-start(bf16[32,144,128]{2,1,0:T(8,128)(2,1)} %bitcast.23), calls=%async_computation | async-start | bytes 2359296 | tf_op jit(solution)/shard_map/all_to_all | solution.py:380
  19.7 1.4 %collective-permute-start.3 = (bf16[3,128,128]{2,1,0:T(8,128)(2,1)S(1)}, bf16[3,128,128]{2,1,0:T(8,128)(2,1)S(1)}, u32[]{:S(2)}, u32[]{:S(2)}) collective-permute-start(bf16[3,128,128]{2,1,0:T(8,128)(2,1)S(1)} %copy-done.3), channel_id=1, source_target_pairs={{1,0},{0,1},{3,2},{2,3},{5,4},{4,5},{7,6},{6,7},{9,8},{8,9},{11,10... | collective-permute-start | bytes 294920 | tf_op jit(solution)/shard_map/ppermute | solution.py:332
  20.1 1.3 %collective-permute-start.4 = (bf16[3,128,128]{2,1,0:T(8,128)(2,1)S(1)}, bf16[3,128,128]{2,1,0:T(8,128)(2,1)S(1)}, u32[]{:S(2)}, u32[]{:S(2)}) collective-permute-start(bf16[3,128,128]{2,1,0:T(8,128)(2,1)S(1)} %collective-permute-done.refs_1_), channel_id=1, source_target_pairs={{1,0},{0,1},{3,2},{2,3},{5,4},{4,5},{7,6},{6,7},{9,8},{8,9},{11,10... | collective-permute-start | bytes 294920 | tf_op jit(solution)/shard_map/ppermute | solution.py:332
  20.3 1.3 %collective-permute-start.5 = (bf16[3,128,128]{2,1,0:T(8,128)(2,1)S(1)}, bf16[3,128,128]{2,1,0:T(8,128)(2,1)S(1)}, u32[]{:S(2)}, u32[]{:S(2)}) collective-permute-start(bf16[3,128,128]{2,1,0:T(8,128)(2,1)S(1)} %collective-permute-done.1.refs_2_), channel_id=1, source_target_pairs={{1,0},{0,1},{3,2},{2,3},{5,4},{4,5},{7,6},{6,7},{9,8},{8,9},{11,10... | collective-permute-start | bytes 294920 | tf_op jit(solution)/shard_map/ppermute | solution.py:332
  20.6 1.3 %collective-permute-start.6 = (bf16[3,128,128]{2,1,0:T(8,128)(2,1)S(1)}, bf16[3,128,128]{2,1,0:T(8,128)(2,1)S(1)}, u32[]{:S(2)}, u32[]{:S(2)}) collective-permute-start(bf16[3,128,128]{2,1,0:T(8,128)(2,1)S(1)} %collective-permute-done.2.refs_3_), channel_id=1, source_target_pairs={{1,0},{0,1},{3,2},{2,3},{5,4},{4,5},{7,6},{6,7},{9,8},{8,9},{11,10... | collective-permute-start | bytes 294920 | tf_op jit(solution)/shard_map/ppermute | solution.py:332
  23.6 16.2 %collective-permute-start.10 = (bf16[3,128,128]{2,1,0:T(8,128)(2,1)S(1)}, bf16[3,128,128]{2,1,0:T(8,128)(2,1)S(1)}, u32[]{:S(2)}, u32[]{:S(2)}) collective-permute-start(bf16[3,128,128]{2,1,0:T(8,128)(2,1)S(1)} %get-tuple-element.37), channel_id=1, source_target_pairs={{32,0},{40,1},{33,8},{41,9},{48,16},{56,17},{49,24},{57,25},{0,32}... | collective-permute-start | bytes 294920 | tf_op jit(solution)/shard_map/ppermute | solution.py:337
  30.3 9.5 %collective-permute-start.9 = (bf16[3,128,128]{2,1,0:T(8,128)(2,1)S(1)}, bf16[3,128,128]{2,1,0:T(8,128)(2,1)S(1)}, u32[]{:S(2)}, u32[]{:S(2)}) collective-permute-start(bf16[3,128,128]{2,1,0:T(8,128)(2,1)S(1)} %get-tuple-element.37), channel_id=1, source_target_pairs={{48,0},{56,1},{49,8},{57,9},{0,16},{8,17},{1,24},{9,25},{16,32},{2... | collective-permute-start | bytes 294920 | tf_op jit(solution)/shard_map/ppermute | solution.py:337
  32.1 8.0 %collective-permute-start.8 = (bf16[3,128,128]{2,1,0:T(8,128)(2,1)S(1)}, bf16[3,128,128]{2,1,0:T(8,128)(2,1)S(1)}, u32[]{:S(2)}, u32[]{:S(2)}) collective-permute-start(bf16[3,128,128]{2,1,0:T(8,128)(2,1)S(1)} %get-tuple-element.37), channel_id=1, source_target_pairs={{16,0},{24,1},{17,8},{25,9},{32,16},{40,17},{33,24},{41,25},{48,32... | collective-permute-start | bytes 294920 | tf_op jit(solution)/shard_map/ppermute | solution.py:337
  33.3 7.9 %collective-permute-start.7 = (bf16[3,128,128]{2,1,0:T(8,128)(2,1)S(1)}, bf16[3,128,128]{2,1,0:T(8,128)(2,1)S(1)}, u32[]{:S(2)}, u32[]{:S(2)}) collective-permute-start(bf16[3,128,128]{2,1,0:T(8,128)(2,1)S(1)} %get-tuple-element.37), channel_id=1, source_target_pairs={{0,0},{8,1},{1,8},{9,9},{16,16},{24,17},{17,24},{25,25},{32,32},{4... | collective-permute-start | bytes 294920 | tf_op jit(solution)/shard_map/ppermute | solution.py:337
  41.2 17.7 %collective-permute-start.11 = (bf16[4,3,128,128]{3,2,1,0:T(8,128)(2,1)S(1)}, bf16[4,3,128,128]{3,2,1,0:T(8,128)(2,1)S(1)}, u32[]{:S(2)}, u32[]{:S(2)}) collective-permute-start(bf16[4,3,128,128]{3,2,1,0:T(8,128)(2,1)S(1)} %shard_map.91.mine_ref), channel_id=1, source_target_pairs={{1,0},{0,1},{3,2},{2,3},{5,4},{4,5},{7,6},{6,7},{9,8},{8,9},{11,10... | collective-permute-start | bytes 1179656 | tf_op jit(solution)/shard_map/ppermute | solution.py:332
  41.3 16.5 %all-to-all-start.1 = ((bf16[8,64,128]{2,1,0:T(8,128)(2,1)}), bf16[8,64,128]{2,1,0:T(8,128)(2,1)S(1)}, u32[]{:S(2)}, u32[]{:S(2)}) async-start(bf16[8,64,128]{2,1,0:T(8,128)(2,1)} %get-tuple-element.38), calls=%async_computation.1 | async-start | bytes 262144 | tf_op jit(solution)/shard_map/all_to_all | solution.py:406
  81.5 4.8 %collective-permute-start.12 = (bf16[8,64,128]{2,1,0:T(8,128)(2,1)S(1)}, bf16[8,64,128]{2,1,0:T(8,128)(2,1)S(1)}, u32[]{:S(2)}, u32[]{:S(2)}) collective-permute-start(bf16[8,64,128]{2,1,0:T(8,128)(2,1)S(1)} %all_to_all.26.x_ref), channel_id=1, source_target_pairs={{1,0},{0,1},{3,2},{2,3},{5,4},{4,5},{7,6},{6,7},{9,8},{8,9},{11,10... | collective-permute-start | bytes 393224 | tf_op jit(solution)/shard_map/ppermute | solution.py:332
  87.1 20.0 %copy-start = (bf16[1,16,128,128]{3,2,1,0:T(8,128)(2,1)S(1)}, bf16[1,16,128,128]{3,2,1,0:T(8,128)(2,1)}, u32[]{:S(2)}) copy-start(bf16[1,16,128,128]{3,2,1,0:T(8,128)(2,1)} %param.8) | copy-start | bytes 1572868
  87.1 20.0 %copy-start.1 = (bf16[1,16,128,128]{3,2,1,0:T(8,128)(2,1)S(1)}, bf16[1,16,128,128]{3,2,1,0:T(8,128)(2,1)}, u32[]{:S(2)}) copy-start(bf16[1,16,128,128]{3,2,1,0:T(8,128)(2,1)} %param.9) | copy-start | bytes 1572868
  87.2 20.0 %copy-start.2 = (bf16[16,256,128]{2,1,0:T(8,128)(2,1)S(1)}, bf16[16,256,128]{2,1,0:T(8,128)(2,1)}, u32[]{:S(2)}) copy-start(bf16[16,256,128]{2,1,0:T(8,128)(2,1)} %get-tuple-element.55.fwd_ref) | copy-start | bytes 3145732
